TPU v7x, 1024 devices: a whole 8x8x8 slice. The times are simulated.
1024 devices in a mesh: dp: 8 (over z), lat: 64 (over y, x), inner: 2 (over core).
Axes of the slice: x: 8, y: 8, z: 8, core: 2. Of those that a mesh axis runs over, the one named last changes fastest.
Arguments:
- err_main: bfloat16 [1024, 4096], P(('dp', 'lat', 'inner')), may hold values from -6 to 6
- err_aux: bfloat16 [1024, 4096], P(('dp', 'lat', 'inner')), may hold values from -6 to 6
- resid: bfloat16 [1024, 4096], P(('dp', 'lat', 'inner')), may hold values from -6 to 6
- top_idx: int32 [1024, 64], P('dp'), may hold values from 0 to 4194303, as said below
- top_val: bfloat16 [1024, 64], P('dp'), may hold values from 0.099609375 to 3
- aux_idx: int32 [1024, 512], P('dp'), may hold values from 0 to 32767, as said below
- aux_val: bfloat16 [1024, 512], P('dp'), may hold values from 0.099609375 to 3
- blocks: int32 [256], P(('lat', 'inner')), may hold values from -1 to 255, as said below
- dead: int32 [32768], P(('lat', 'inner')), may hold values 0 or 1
- dec_rows: bfloat16 [32768, 4096], P(('lat', 'inner')), may hold values from -0.09375 to 0.09375
Outputs:
- dec_grad: bfloat16 [32768, 4096], P(('lat', 'inner'), 'dp')
- enc_grad: bfloat16 [32768, 4096], P(('lat', 'inner'), 'dp')
Inputs may be any that keep to these rules, and one draw needn't show every extreme that they name: `top_idx`: each row holds 64 different latents, all in active blocks. `aux_idx`: each row holds 512 different slots, none in an empty block slot. A shard's first slot is always filled, its filled blocks differ, and some shard fills all 2 slots.
All inputs are finite; a program needn't handle non-finite values. No bound on the sum of `dead` on one device may be relied on, other than what follows from the above.
Results may differ from a plain program's by a relative error of at most 0.018.
Values may be sent and summed in bfloat16 or wider, within the bound.
No kernel may reach another device: no remote copies, remote signals or barrier semaphores. Data moves between devices by JAX's collectives and lax.ppermute only.
A program may use at most 32 MiB of HBM per device.

v0:
```python
import jax
import jax.numpy as jnp
from jax import lax
from jax.sharding import PartitionSpec as P

LAT_DEV = 32768


def contract_rows(left, right):
    return lax.dot_general(
        left, right, (((0,), (0,)), ((), ())), preferred_element_type=jnp.float32
    )


def slot_dpre(main_rows, aux_rows, sel_main, sel_aux, dec):
    dval_main = lax.dot_general(
        main_rows, dec, (((1,), (1,)), ((), ())), preferred_element_type=jnp.float32
    )
    dval_aux = lax.dot_general(
        aux_rows, dec, (((1,), (1,)), ((), ())), preferred_element_type=jnp.float32
    )
    return (jnp.where(sel_main > 0, dval_main, 0.0) + jnp.where(sel_aux > 0, dval_aux, 0.0)).astype(
        jnp.bfloat16
    )


def make_dpre(main_rows, aux_rows, sel_main, sel_aux, dec_rows):
    return slot_dpre(main_rows, aux_rows, sel_main, sel_aux, dec_rows)


def slot_terms(main_cols, aux_cols, resid_cols, sel_main, sel_aux, dpre):
    dec_term = contract_rows(main_cols, sel_main) + contract_rows(aux_cols, sel_aux)
    enc_term = contract_rows(resid_cols, dpre)
    return (dec_term, enc_term)


def make_terms(main_cols, aux_cols, resid_cols, sel_main, sel_aux, dpre):
    dec_term, enc_term = slot_terms(main_cols, aux_cols, resid_cols, sel_main, sel_aux, dpre)
    return jnp.concatenate([dec_term, enc_term], axis=1)


def local(err_main, err_aux, resid, top_idx, top_val, aux_idx, aux_val, blocks, dead, dec_rows):
    width = dec_rows.shape[0]
    span = width // blocks.shape[0]
    shard = lax.axis_index(("lat", "inner"))
    group = top_idx.shape[0]
    slot_ids = jnp.arange(blocks.shape[0], dtype=jnp.int32)
    tok_ids = jnp.arange(group, dtype=jnp.int32)[:, None]

    def select(owner, local_col, vals):
        cols = jnp.where(owner == shard, local_col, width)
        table_out = (
            jnp.zeros((group, width + 1), jnp.float32)
            .at[tok_ids, cols]
            .add(vals.astype(jnp.float32))
        )
        return table_out[:, :width]

    main_local = top_idx % LAT_DEV
    main_slot = jnp.sum(jnp.where(blocks == (main_local // span)[..., None], slot_ids, 0), axis=-1)
    dead_f = dead.astype(jnp.float32)
    sel_main = select(top_idx // LAT_DEV, main_slot * span + main_local % span, top_val).astype(
        jnp.bfloat16
    )
    sel_aux = (select(aux_idx // width, aux_idx % width, aux_val) * dead_f[None, :]).astype(
        jnp.bfloat16
    )
    main_rows, aux_rows, resid_rows = (
        lax.all_gather(err_main, ("lat", "inner"), axis=0, tiled=True),
        lax.all_gather(err_aux, ("lat", "inner"), axis=0, tiled=True),
        lax.all_gather(resid, ("lat", "inner"), axis=0, tiled=True),
    )
    dpre = make_dpre(main_rows, aux_rows, sel_main, sel_aux, dec_rows)
    terms = make_terms(main_rows, aux_rows, resid_rows, sel_main, sel_aux, dpre)
    summed = lax.psum_scatter(
        terms.astype(jnp.bfloat16), "dp", scatter_dimension=0, tiled=True
    ).astype(jnp.float32)
    dec_grad = summed[:, :width].T.astype(jnp.bfloat16)
    enc_grad = summed[:, width:].T.astype(jnp.bfloat16)
    return (dec_grad, enc_grad)


def solution(mesh):
    in_specs = (
        P(("dp", "lat", "inner"), None),
        P(("dp", "lat", "inner"), None),
        P(("dp", "lat", "inner"), None),
        P("dp", None),
        P("dp", None),
        P("dp", None),
        P("dp", None),
        P(("lat", "inner")),
        P(("lat", "inner")),
        P(("lat", "inner"), None),
    )
    out_specs = (P(("lat", "inner"), "dp"), P(("lat", "inner"), "dp"))
    return jax.shard_map(local, mesh=mesh, in_specs=in_specs, out_specs=out_specs, check_vma=False)
```

profile of v0, /device:TPU:1, one launch (start us, length us, event | category | flops | bytes accessed | tf_op | source)
XLA Modules:
  0.0 630.0 jit_solution(6956890381755017439)
XLA Ops:
  7.2 0.0 copy-start
  7.2 0.0 copy-start.3
  7.2 0.0 copy-start.4
  7.2 0.0 all-gather.7.cloned.1.call-start
  7.2 0.7 all-gather.7.cloned.1.call-update
  7.9 0.0 all-gather.9.cloned.1.call-start
  8.0 0.7 all-gather.9.cloned.1.call-update
  8.7 0.0 all-gather.11.cloned.1.call-start
  8.7 0.7 all-gather.11.cloned.1.call-update
  9.4 0.0 reduce-scatter.2.cloned.1.call-start
  9.5 0.8 add_select_fusion.3
  10.3 0.7 select_reduce_fusion
  11.0 0.8 fusion.34
  11.8 0.7 and_reduce_fusion.1
  12.6 0.7 multiply_reduce_fusion.1
  13.3 0.0 copy-start.2
  13.3 0.1 copy.16
  13.4 0.1 reshape.18
  13.5 0.8 copy.17
  14.3 0.1 reshape.20
  14.4 56.6 %scatter_custom_fusion = f32[32896]{0:T(1024)S(1)} fusion(s32[8192]{0:T(1024)S(1)} %reshape.18, f32[8192]{0:T(1024)S(1)} %reshape.20, f32[]{:T(128)} %constant.80.clone.1), kind=kCustom, calls=%fused_computation.49 | custom fusion | flops 8192 | bytes 131588
  71.0 0.7 convert_element_type.28
  71.7 0.1 copy.18
  71.8 1.2 fusion.20
  73.1 0.0 copy-done.4
  73.1 0.1 multiply_reduce_fusion
  73.2 0.0 copy-done.3
  73.2 0.2 and_reduce_fusion
  73.4 0.1 copy.23
  73.5 0.0 copy-done.2
  73.5 0.1 copy.24
  73.6 447.7 %scatter_custom_fusion.1 = f32[32896]{0:T(1024)S(1)} fusion(s32[65536]{0:T(1024)S(1)} %bitcast.47, f32[65536]{0:T(1024)S(1)} %bitcast.48, f32[]{:T(128)} %constant.80.clone.1), kind=kCustom, calls=%fused_computation.47 | custom fusion | flops 65536 | bytes 131588
  521.4 0.1 copy.19
  521.5 0.0 all-gather.7.cloned.1.call-done
  521.5 0.0 copy-start.1
  521.5 0.0 copy-done
  521.5 3.2 convolution_select_fusion.1
  524.7 0.0 copy-done.1
  524.7 3.6 fusion.11
  528.4 0.0 all-gather.9.cloned.1.call-done
  528.4 5.8 fusion.1
  534.2 0.0 all-gather.11.cloned.1.call-done
  534.2 6.6 %fusion.2 = bf16[4096,256]{0,1:T(8,128)(2,1)} fusion(f32[128,256]{1,0:T(8,128)S(1)} %convolution_select_fusion.1, bf16[256,4096]{1,0:T(8,128)(2,1)S(1)} %copy-done, bf16[128,1,4096]{2,1,0:T(2,128)(2,1)} %all-gather.11.cloned.1.call-done, bf16[128,1,4096]{2,1,0:T(2,128)(2,1)} %all-gather.9.cloned.1.call-done, f32[128,257]{1,0:T(8,128)S(1)} %bitcast.43, ...), kind=kOutput, calls=%fused_computation.6 | convolution fusion | flops 538116096 | bytes 6554624 | tf_op jit(solution)/shard_map/dot_general | solution.py:10
  540.7 4.6 pad_maximum_fusion
  545.4 0.0 reduce-scatter.2.cloned.1.call-update
  545.4 76.2 %reduce-scatter.2.cloned.1.call-done = bf16[512,512]{0,1:T(8,128)(2,1)} async-done(((bf16[4096,512]{0,1:T(8,128)(2,1)}), bf16[512,512]{0,1:T(8,128)(2,1)}) %reduce-scatter.2.cloned.1.call-update) | async-done | bytes 524304 | tf_op jit(solution)/shard_map/reduce_scatter | solution.py:75
  621.6 1.9 slice_bitcast_fusion
  (6 shorter events, 0.1 us)
Async XLA Ops:
  7.2 514.4 %copy-start = (bf16[256,4096]{1,0:T(8,128)(2,1)S(1)}, bf16[256,4096]{1,0:T(8,128)(2,1)}, u32[]{:S(2)}) copy-start(bf16[256,4096]{1,0:T(8,128)(2,1)} %param.19) | copy-start | bytes 6291460
  7.2 66.0 %copy-start.3 = (s32[2]{0:T(128)S(1)}, s32[2]{0:T(128)}, u32[]{:S(2)}) copy-start(s32[2]{0:T(128)} %constant.105) | copy-start | bytes 28
  7.2 65.9 %copy-start.4 = (s32[2]{0:T(128)S(1)}, s32[2]{0:T(128)}, u32[]{:S(2)}) copy-start(s32[2]{0:T(128)} %constant.102) | copy-start | bytes 28
  7.2 514.3 %all-gather.7.cloned.1.call-start = ((), (), s32[]{:S(2)}) async-start(), calls=%async_computation.2 | async-start | bytes 2113536 | tf_op jit(solution)/shard_map/all_gather | solution.py:69
  7.9 520.4 %all-gather.9.cloned.1.call-start = ((), (), s32[]{:S(2)}) async-start(), calls=%async_computation.3 | async-start | bytes 2113536 | tf_op jit(solution)/shard_map/all_gather | solution.py:70
  8.7 525.5 %all-gather.11.cloned.1.call-start = ((), (), s32[]{:S(2)}) async-start(), calls=%async_computation.4 | async-start | bytes 2113536 | tf_op jit(solution)/shard_map/all_gather | solution.py:71
  9.4 612.2 %reduce-scatter.2.cloned.1.call-start = ((), (), s32[]{:S(2)}) async-start(), calls=%async_computation.1 | async-start | bytes 4718592 | tf_op jit(solution)/shard_map/reduce_scatter | solution.py:75
  13.3 60.2 %copy-start.2 = (bf16[128,512]{1,0:T(8,128)(2,1)S(1)}, bf16[128,512]{1,0:T(8,128)(2,1)}, u32[]{:S(2)}) copy-start(bf16[128,512]{1,0:T(8,128)(2,1)} %param.16) | copy-start | bytes 393220
  521.5 3.2 copy-start.1
Sparse Core Ops, SparseCore 0:
  12.3 100.1 all-gather.6
  116.8 86.1 all-gather.8
  207.3 86.1 all-gather.10
  545.5 76.0 reduce-scatter.1
where the time goes:
time: 631 us; the launch traced here: 630 us
  other arithmetic  515 us (82%)
  waiting for transfers between devices  78.3 us (12%)
  matrix products  19.2 us (3%)
  between operations  14 us (2%)
    unnamed x9, other arithmetic  506 us
    reduce_scatter x1, waiting for transfers between devices, local(): lax.psum_scatter(terms.astype(jnp.bfloat16), 'dp', scatter_dimension=0, t...  76.2 us
    dot_general x3, matrix products, contract_rows(): lax.dot_general(left, right, (((0,), (0,)), ((), ())), preferred_element_...  16 us
  transfers between devices with their start and end apart: 4, of which 1 were waited for; matrix products, arithmetic and copies ran while one was open for 83% of the time, Pallas kernels for 0%

commit v1 on v0

v1 whole, which is shorter than its diff:
```python
import jax
import jax.numpy as jnp
from jax import lax
from jax.experimental import pallas as pl
from jax.experimental.pallas import tpu as pltpu
from jax.sharding import PartitionSpec as P

LAT_DEV = 32768
BLOCK = 128


def sel_kernel(n_main, n_aux, main_col, main_val, aux_col, aux_val, dead, out):
    slots = dead.shape[1]
    lanes = [lax.broadcasted_iota(jnp.int32, (8, 128), 1) + 128 * k for k in range(slots // 128)]

    def place(acc, col, val, width):
        for j in range(width):
            c = jnp.broadcast_to(col[:, j : j + 1], (8, 128))
            v = jnp.broadcast_to(val[:, j : j + 1], (8, 128))
            acc = [jnp.where(c == lane, v, a) for lane, a in zip(lanes, acc)]
        return acc

    zero = [jnp.zeros((8, 128), jnp.float32) for _ in lanes]
    main = place(zero, main_col[...], main_val[...], n_main)

    def step(i, acc):
        part = pl.ds(pl.multiple_of(i * 128, 128), 128)
        return tuple(place(list(acc), aux_col[:, part], aux_val[:, part], 128))

    aux = lax.fori_loop(0, n_aux // 128, step, tuple(zero))
    for k in range(len(lanes)):
        out[:, 128 * k : 128 * k + 128] = main[k]
        out[:, slots + 128 * k : slots + 128 * k + 128] = (
            aux[k] * dead[:, 128 * k : 128 * k + 128]
        )


def make_sel(main_col, main_val, aux_col, aux_val, dead):
    rows, n_main = main_col.shape
    n_aux = aux_col.shape[1]
    slots = dead.shape[1]

    def spec(width):
        return pl.BlockSpec((8, width), lambda i: (i, 0))

    def kernel(*refs):
        sel_kernel(n_main, n_aux, *refs)

    return pl.pallas_call(
        kernel,
        grid=(rows // 8,),
        in_specs=[spec(n_main), spec(n_main), spec(n_aux), spec(n_aux)]
        + [pl.BlockSpec((1, slots), lambda i: (0, 0))],
        out_specs=spec(2 * slots),
        out_shape=jax.ShapeDtypeStruct((rows, 2 * slots), jnp.float32),
        cost_estimate=pl.CostEstimate(
            flops=rows * n_aux * slots * 8, bytes_accessed=1 << 20, transcendentals=0
        ),
        name="sel",
    )(main_col, main_val, aux_col, aux_val, dead)


def rows_dot(left, right):
    return lax.dot_general(
        left, right, (((1,), (1,)), ((), ())), preferred_element_type=jnp.float32
    )


def cols_dot(left, right):
    return lax.dot_general(
        left, right, (((0,), (0,)), ((), ())), preferred_element_type=jnp.float32
    )


def local(
    n_dp, n_lat, n_in, err_main, err_aux, resid, top_idx, top_val, aux_idx, aux_val, blocks, dead, dec_rows
):
    width, d = dec_rows.shape
    cols = d // n_dp
    group = top_idx.shape[0]
    mine = group // n_in
    slots = width * n_in
    dp = lax.axis_index("dp")
    lat = lax.axis_index("lat")
    core = lax.axis_index("inner")

    rows = jnp.concatenate([err_main, err_aux, resid, resid], axis=0)
    rows = rows.reshape(4, n_dp, cols).transpose(1, 0, 2)
    rows = lax.all_to_all(rows, "dp", 0, 0, tiled=True)
    rows = rows[:, :3].transpose(1, 0, 2).reshape(3 * n_dp, cols)
    rows = lax.all_to_all(
        jnp.broadcast_to(rows[None], (n_lat,) + rows.shape), "lat", 0, 0, tiled=True
    )
    rows = rows.reshape(n_lat, 3, n_dp, cols).transpose(1, 2, 0, 3).reshape(3, n_dp * n_lat, cols)
    main, aux, res = rows[0], rows[1], rows[2]

    dec = lax.all_gather(
        lax.dynamic_slice_in_dim(dec_rows, dp * cols, cols, 1), "inner", axis=0, tiled=True
    )
    table = lax.all_gather(blocks, "inner", axis=0, tiled=True)
    dead_all = lax.all_gather(dead, "inner", axis=0, tiled=True)

    def own(v):
        return lax.dynamic_index_in_dim(v.reshape(mine, n_in, -1), core, 1, keepdims=False)

    top_own, aux_own = own(top_idx), own(aux_idx)
    per = table.shape[0] // n_in
    keys = jnp.where(
        table >= 0,
        (lat * n_in + jnp.arange(table.shape[0], dtype=jnp.int32) // per) * (LAT_DEV // BLOCK) + table,
        -1,
    )
    main_col = jnp.full(top_own.shape, -1, jnp.int32)
    for k in range(table.shape[0]):
        main_col = jnp.where(top_own // BLOCK == keys[k], k * BLOCK + top_own % BLOCK, main_col)
    sel = make_sel(
        main_col,
        own(top_val).astype(jnp.float32),
        aux_own - lat * slots,
        own(aux_val).astype(jnp.float32),
        dead_all.astype(jnp.float32)[None],
    ).astype(jnp.bfloat16)
    sel = lax.all_gather(sel, "dp", axis=0, tiled=True)
    sel_main, sel_aux = sel[:, :slots], sel[:, slots:]

    part = (
        jnp.where(sel_main > 0, rows_dot(main, dec), 0.0)
        + jnp.where(sel_aux > 0, rows_dot(aux, dec), 0.0)
    ).astype(jnp.bfloat16)
    part = lax.all_to_all(part.reshape(n_dp, n_lat, slots), "dp", 0, 0, tiled=True)
    dpre = jnp.sum(part.astype(jnp.float32), axis=0).astype(jnp.bfloat16)
    dpre = lax.all_to_all(
        jnp.broadcast_to(dpre[None], (n_dp,) + dpre.shape), "dp", 0, 0, tiled=True
    ).reshape(n_dp * n_lat, slots)

    swap = [(i, (i + 1) % n_in) for i in range(n_in)]

    def over_cores(term):
        theirs = lax.dynamic_slice_in_dim(term, (1 - core) * width, width, 0).astype(jnp.bfloat16)
        ours = lax.dynamic_slice_in_dim(term, core * width, width, 0)
        got = lax.ppermute(theirs, "inner", swap)
        return (ours + got.astype(jnp.float32)).astype(jnp.bfloat16)

    dec_grad = over_cores(cols_dot(sel_main, main) + cols_dot(sel_aux, aux))
    enc_grad = over_cores(cols_dot(dpre, res))
    return (dec_grad, enc_grad)


def solution(mesh):
    tokens = P(("dp", "lat", "inner"), None)
    shard = ("lat", "inner")
    in_specs = (tokens,) * 3 + (P("dp", None),) * 4 + (P(shard), P(shard), P(shard, None))
    out_specs = (P(shard, "dp"), P(shard, "dp"))
    n_dp, n_lat, n_in = (mesh.shape[a] for a in ("dp", "lat", "inner"))

    def step(*args):
        return local(n_dp, n_lat, n_in, *args)

    return jax.shard_map(step, mesh=mesh, in_specs=in_specs, out_specs=out_specs, check_vma=False)
```

time: 631 us -> 180 us (0.29)
  other arithmetic: 515 us -> 13.8 us
  starting transfers between devices: 0.15 us -> 53.4 us
  waiting for transfers between devices: 78.3 us -> 35.2 us
  blocking collectives: 0 us -> 24.4 us
  Pallas kernels: 0 us -> 20.5 us
  matrix products: 19.2 us -> 5.83 us
  local copies, waits for them, and re-layouts: 3.35 us -> 11.4 us
    unnamed x9 -> x0, other arithmetic: 506 us -> none
    reduce_scatter x1 -> x0, waiting for transfers between devices: 76.2 us -> none  [local(): lax.psum_scatter(terms.astype(jnp.bfloat16), 'dp', scatter_dimension=0, t...]
    all_to_all x0 -> x3, starting transfers between devices: none -> 35 us  [the longest x1 17.2 us: local(): rows = lax.all_to_all(rows, 'dp', 0, 0, tiled=True)]
    all_gather x3 -> x1, waiting for transfers between devices: 0.02 us -> 32.2 us  [local(): sel = lax.all_gather(sel, 'dp', axis=0, tiled=True)]
    pallas_call x0 -> x1, Pallas kernels: none -> 20.5 us  [make_sel(): pl.pallas_call(kernel, grid=(rows // 8,), in_specs=[spec(n_main), spec(n_...]
    ppermute x0 -> x2, starting transfers between devices: none -> 18.4 us  [over_cores(): got = lax.ppermute(theirs, 'inner', swap)]
    all_to_all x0 -> x1, blocking collectives: none -> 16 us  [local(): lax.all_to_all(part.reshape(n_dp, n_lat, slots), 'dp', 0, 0, tiled=True)]
    dot_general x4 -> x5, matrix products: 19.2 us -> 5.83 us  [the longest x3 3.72 us: cols_dot(): lax.dot_general(left, right, (((0,), (0,)), ((), ())), preferred_element_...]
  transfers between devices with their start and end apart: 4 -> 6, of which waited for: 1 -> 4; matrix products, arithmetic and copies ran while one was open for 83% -> 11% of each run, Pallas kernels for 0% -> 11%
where the time goes in v1:
time: 180 us
  starting transfers between devices  53.4 us (30%)
  waiting for transfers between devices  35.2 us (20%)
  blocking collectives  24.4 us (14%)
  Pallas kernels  20.5 us (11%)
  between operations  15 us (8%)
  other arithmetic  13.8 us (8%)
  local copies, waits for them, and re-layouts  11.4 us (6%)
  matrix products  5.83 us (3%)
    all_gather x1, waiting for transfers between devices, local(): sel = lax.all_gather(sel, 'dp', axis=0, tiled=True)  32.2 us
    pallas_call x1, Pallas kernels, make_sel(): pl.pallas_call(kernel, grid=(rows // 8,), in_specs=[spec(n_main), spec(n_...  20.5 us
    ppermute x2, starting transfers between devices, over_cores(): got = lax.ppermute(theirs, 'inner', swap)  18.4 us
    all_to_all x1, starting transfers between devices, local(): rows = lax.all_to_all(rows, 'dp', 0, 0, tiled=True)  17.2 us
    all_to_all x1, blocking collectives, local(): lax.all_to_all(part.reshape(n_dp, n_lat, slots), 'dp', 0, 0, tiled=True)  16 us
    all_to_all x1, starting transfers between devices, local(): lax.all_to_all(jnp.broadcast_to(rows[None], (n_lat,) + rows.shape), 'lat'...  13.6 us
    unnamed x32, local copies, waits for them, and re-layouts  4.35 us
    all_to_all x1, starting transfers between devices, local(): lax.all_to_all(jnp.broadcast_to(dpre[None], (n_dp,) + dpre.shape), 'dp',...  4.15 us
  transfers between devices with their start and end apart: 6, of which 4 were waited for; matrix products, arithmetic and copies ran while one was open for 11% of the time, Pallas kernels for 11%

profile of v1, /device:TPU:1, one launch (start us, length us, event | category | flops | bytes accessed | tf_op | source)
XLA Modules:
  0.0 179.5 jit_solution(13828599406549932444)
XLA Ops:
  7.2 0.0 copy-start
  7.2 1.6 pad_maximum_fusion
  8.8 17.2 %all-to-all-start = ((bf16[8,4,512]{2,1,0:T(4,128)(2,1)}), bf16[8,4,512]{2,1,0:T(4,128)(2,1)S(1)}, u32[]{:S(2)}, u32[]{:S(2)}) async-start(bf16[8,4,512]{2,1,0:T(4,128)(2,1)} %bitcast.14), calls=%async_computation | async-start | bytes 65536 | tf_op jit(solution)/shard_map/all_to_all | solution.py:89
  26.0 1.3 dynamic-slice
  28.0 0.9 dynamic-update-slice
  28.8 2.4 %all-reduce = s32[4]{0:T(128)S(1)} all-reduce(s32[4]{0:T(128)S(1)} %dynamic-update-slice), channel_id=1, replica_groups=mesh['dp'=8,'lat'=64,'inner'=2] {'inner'}, use_global_device_ids=true, to_apply=%add | all-reduce | flops 4 | bytes 32
  31.2 1.7 all-to-all-done
  32.9 1.2 broadcast_in_dim.26
  34.2 0.0 copy-start.12
  34.2 13.6 %all-to-all-start.1 = ((bf16[64,24,512]{2,1,0:T(8,128)(2,1)}), bf16[64,24,512]{2,1,0:T(8,128)(2,1)}, u32[]{:S(2)}, u32[]{:S(2)}) async-start(bf16[64,24,512]{2,1,0:T(8,128)(2,1)} %broadcast_in_dim.26), calls=%async_computation.1 | async-start | bytes 3145728 | tf_op jit(solution)/shard_map/all_to_all | solution.py:91
  47.8 0.0 all-gather.3.cloned.1.call-start
  47.8 0.0 copy-done.10
  47.9 0.1 copy.24
  47.9 0.0 copy-done.11
  48.0 0.1 copy.25
  48.1 0.0 copy-done.8
  48.1 0.1 reshape.45
  48.2 0.0 copy-done.9
  48.2 0.1 reshape.46
  48.3 0.0 copy-done.12
  48.3 3.9 %all-gather = s32[2,1,256]{2,1,0:T(1,128)S(1)} all-gather(s32[1,1,256]{2,1,0:T(1,128)S(1)} %bitcast.60), channel_id=1, replica_groups=mesh['dp'=8,'lat'=64,'inner'=2] {'inner'}, dimensions={0}, use_global_device_ids=true | all-gather | bytes 3072 | tf_op jit(solution)/shard_map/all_gather | solution.py:101
  52.2 0.6 convert_element_type.54
  52.8 0.7 fusion.13
  53.5 0.1 constant_dynamic-slice_fusion.2
  53.6 0.1 constant_dynamic-slice_fusion.1
  53.8 0.6 fusion.8.refs_1_
  54.4 3.3 %select_select_fusion.refs_0_ = s32[64,64]{1,0:T(8,128)} fusion(s32[64,64]{1,0:T(8,128)S(1)} %bitcast.57, s32[]{:T(128)} %bitcast.6, s32[]{:T(128)} %bitcast.5, s32[]{:T(128)} %bitcast.4, s32[]{:T(128)} %bitcast.3), kind=kLoop, calls=%fused_computation.22 | loop fusion | flops 122880 | bytes 32784 | tf_op jit(solution)/shard_map/jit(_where)/select_n | solution.py:115
  57.7 0.7 fusion.6.refs_3_
  58.3 0.7 fusion.5.refs_2_
  59.0 20.5 %sel.1 = f32[64,1024]{1,0:T(8,128)} custom-call(s32[64,64]{1,0:T(8,128)} %select_select_fusion.refs_0_, f32[64,64]{1,0:T(8,128)} %fusion.8.refs_1_, s32[64,512]{1,0:T(8,128)} %fusion.5.refs_2_, f32[64,512]{1,0:T(8,128)} %fusion.6.refs_3_, f32[1,512]{1,0:T(1,128)} %bitcast.59), custom_call_target="tpu_custom_call" | custom-call | flops 134217728 | bytes 1048576 | tf_op jit(solution)/shard_map/sel/pallas_call | solution.py:49
  79.5 1.6 convert_element_type.44
  81.1 0.0 all-gather.3.cloned.1.call-update
  81.1 0.0 copy-done
  81.2 2.2 %all_gather.15 = bf16[512,512]{1,0:T(8,128)(2,1)S(1)} all-gather(bf16[256,512]{1,0:T(8,128)(2,1)S(1)} %constant_dynamic-slice_fusion), channel_id=1, replica_groups=mesh['dp'=8,'lat'=64,'inner'=2] {'inner'}, dimensions={0}, use_global_device_ids=true | all-gather | bytes 786432 | tf_op jit(solution)/shard_map/all_gather | solution.py:97
  83.3 1.0 all-to-all-done.1
  84.3 1.9 %copy.30 = bf16[64,24,512]{2,0,1:T(8,128)(2,1)S(1)} copy(bf16[64,24,512]{2,1,0:T(8,128)(2,1)} %all-to-all-done.1) | data formatting | bytes 3145728 | tf_op jit(solution)/shard_map/all_to_all | solution.py:91
  86.2 1.1 fusion.12
  87.3 32.2 %all-gather.3.cloned.1.call-done = bf16[512,1024]{1,0:T(8,128)(2,1)} async-done(((bf16[64,1024]{1,0:T(8,128)(2,1)}), bf16[512,1024]{1,0:T(8,128)(2,1)}) %all-gather.3.cloned.1.call-update) | async-done | bytes 1048592 | tf_op jit(solution)/shard_map/all_gather | solution.py:123
  119.5 1.6 convolution_select_fusion
  121.2 0.0 copy-done.1
  121.2 0.0 copy-done.3
  121.2 0.5 fusion.1
  121.7 0.0 copy-start.2
  121.7 16.0 %all_to_all.20 = bf16[8,64,512]{2,1,0:T(8,128)(2,1)} all-to-all(bf16[8,64,512]{2,1,0:T(8,128)(2,1)S(1)} %bitcast.52), channel_id=1, replica_groups=mesh['dp'=8,'lat'=64,'inner'=2] {'dp'}, dimensions={0} | all-to-all | bytes 1048576 | tf_op jit(solution)/shard_map/all_to_all | solution.py:130
  137.6 1.1 reduce_sum.12
  138.8 0.8 broadcast_in_dim.28
  139.6 4.2 %all-to-all-start.3 = ((bf16[8,64,512]{2,1,0:T(8,128)(2,1)}), bf16[8,64,512]{2,1,0:T(8,128)(2,1)}, u32[]{:S(2)}, u32[]{:S(2)}) async-start(bf16[8,64,512]{2,1,0:T(8,128)(2,1)} %broadcast_in_dim.28), calls=%async_computation.3 | async-start | bytes 1048576 | tf_op jit(solution)/shard_map/all_to_all | solution.py:132
  143.8 0.0 copy-done.2
  143.8 0.0 copy-start.4
  143.8 1.6 fusion.3
  145.4 0.0 copy-done.4
  145.4 0.5 convolution_add_fusion
  145.9 0.0 copy-start.5
  145.9 1.0 copy-done.5
  146.9 8.7 %collective-permute-start = (bf16[256,512]{1,0:T(8,128)(2,1)S(1)}, bf16[256,512]{1,0:T(8,128)(2,1)}, u32[]{:S(2)}, u32[]{:S(2)}) collective-permute-start(bf16[256,512]{1,0:T(8,128)(2,1)S(1)} %dynamic-slice_convert_fusion.1), channel_id=1, source_target_pairs={{0,1},{1,0},{2,3},{3,2},{4,5},{5,4},{6,7},{7,6},{8,9},{9,8},{10,11... | collective-permute-start | bytes 786440 | tf_op jit(solution)/shard_map/ppermute | solution.py:141
  155.6 0.3 all-to-all-done.3
  156.0 1.7 fusion.14
  157.7 1.0 copy-done.7
  158.6 0.7 dynamic-slice_convert_fusion
  159.4 9.6 %collective-permute-start.1 = (bf16[256,512]{1,0:T(8,128)(2,1)}, bf16[256,512]{1,0:T(8,128)(2,1)}, u32[]{:S(2)}, u32[]{:S(2)}) collective-permute-start(bf16[256,512]{1,0:T(8,128)(2,1)} %dynamic-slice_convert_fusion), channel_id=1, source_target_pairs={{0,1},{1,0},{2,3},{3,2},{4,5},{5,4},{6,7},{7,6},{8,9},{9,8},{10,11... | collective-permute-start | bytes 786440 | tf_op jit(solution)/shard_map/ppermute | solution.py:141
  169.0 0.0 collective-permute-done
  169.0 1.7 add_convert_fusion.1
  170.8 0.0 collective-permute-done.1
  170.8 1.9 %add_convert_fusion = bf16[256,512]{1,0:T(8,128)(2,1)} fusion(bf16[256,512]{1,0:T(8,128)(2,1)} %collective-permute-done.1, f32[512,512]{1,0:T(8,128)} %copy-done.7, s32[]{:T(128)S(6)} %select_n.79), kind=kLoop, calls=%fused_computation.5 | loop fusion | flops 393216 | bytes 1048580 | tf_op jit(solution)/shard_map/convert_element_type | solution.py:142
  (16 shorter events, 0.2 us)
Async XLA Ops:
  7.2 73.9 %copy-start = (bf16[256,4096]{1,0:T(8,128)(2,1)S(1)}, bf16[256,4096]{1,0:T(8,128)(2,1)}, u32[]{:S(2)}) copy-start(bf16[256,4096]{1,0:T(8,128)(2,1)} %param.19) | copy-start | bytes 6291460
  8.8 24.1 %all-to-all-start = ((bf16[8,4,512]{2,1,0:T(4,128)(2,1)}), bf16[8,4,512]{2,1,0:T(4,128)(2,1)S(1)}, u32[]{:S(2)}, u32[]{:S(2)}) async-start(bf16[8,4,512]{2,1,0:T(4,128)(2,1)} %bitcast.14), calls=%async_computation | async-start | bytes 65536 | tf_op jit(solution)/shard_map/all_to_all | solution.py:89
  34.2 13.7 %copy-start.10 = (s32[128,64]{0,1:T(8,128)S(1)}, s32[128,64]{0,1:T(8,128)}, u32[]{:S(2)}) copy-start(s32[128,64]{0,1:T(8,128)} %param.13) | copy-start | bytes 98308
  34.2 13.8 %copy-start.11 = (bf16[128,64]{0,1:T(8,128)(2,1)S(1)}, bf16[128,64]{0,1:T(8,128)(2,1)}, u32[]{:S(2)}) copy-start(bf16[128,64]{0,1:T(8,128)(2,1)} %param.14) | copy-start | bytes 49156
  34.2 13.9 %copy-start.8 = (s32[128,512]{1,0:T(8,128)S(1)}, s32[128,512]{1,0:T(8,128)}, u32[]{:S(2)}) copy-start(s32[128,512]{1,0:T(8,128)} %param.15) | copy-start | bytes 786436
  34.2 14.1 %copy-start.9 = (bf16[128,512]{1,0:T(8,128)(2,1)S(1)}, bf16[128,512]{1,0:T(8,128)(2,1)}, u32[]{:S(2)}) copy-start(bf16[128,512]{1,0:T(8,128)(2,1)} %param.16) | copy-start | bytes 393220
  34.2 14.1 %copy-start.12 = (s32[256]{0:T(256)S(1)}, s32[256]{0:T(256)}, u32[]{:S(2)}) copy-start(s32[256]{0:T(256)} %param.18) | copy-start | bytes 3076
  34.2 50.1 %all-to-all-start.1 = ((bf16[64,24,512]{2,1,0:T(8,128)(2,1)}), bf16[64,24,512]{2,1,0:T(8,128)(2,1)}, u32[]{:S(2)}, u32[]{:S(2)}) async-start(bf16[64,24,512]{2,1,0:T(8,128)(2,1)} %broadcast_in_dim.26), calls=%async_computation.1 | async-start | bytes 3145728 | tf_op jit(solution)/shard_map/all_to_all | solution.py:91
  47.8 71.7 %all-gather.3.cloned.1.call-start = ((), (), s32[]{:S(2)}) async-start(), calls=%async_computation.4 | async-start | bytes 1179648 | tf_op jit(solution)/shard_map/all_gather | solution.py:123
  119.5 1.6 copy-start.1
  119.5 1.6 copy-start.3
  121.7 22.1 %copy-start.2 = (bf16[1,8,64,512]{3,2,1,0:T(8,128)(2,1)S(1)}, bf16[1,8,64,512]{3,2,1,0:T(8,128)(2,1)}, u32[]{:S(2)}) copy-start(bf16[1,8,64,512]{3,2,1,0:T(8,128)(2,1)} %get-tuple-element.4) | copy-start | bytes 1572868
  139.6 16.4 %all-to-all-start.3 = ((bf16[8,64,512]{2,1,0:T(8,128)(2,1)}), bf16[8,64,512]{2,1,0:T(8,128)(2,1)}, u32[]{:S(2)}, u32[]{:S(2)}) async-start(bf16[8,64,512]{2,1,0:T(8,128)(2,1)} %broadcast_in_dim.28), calls=%async_computation.3 | async-start | bytes 1048576 | tf_op jit(solution)/shard_map/all_to_all | solution.py:132
  143.8 1.6 copy-start.4
  145.9 1.0 copy-start.5
  146.9 22.1 %copy-start.6 = (f32[512,512]{1,0:T(8,128)S(1)}, f32[512,512]{1,0:T(8,128)}, u32[]{:S(2)}) copy-start(f32[512,512]{1,0:T(8,128)} %copy-done.5) | copy-start | bytes 3145732
  146.9 22.1 %collective-permute-start = (bf16[256,512]{1,0:T(8,128)(2,1)S(1)}, bf16[256,512]{1,0:T(8,128)(2,1)}, u32[]{:S(2)}, u32[]{:S(2)}) collective-permute-start(bf16[256,512]{1,0:T(8,128)(2,1)S(1)} %dynamic-slice_convert_fusion.1), channel_id=1, source_target_pairs={{0,1},{1,0},{2,3},{3,2},{4,5},{5,4},{6,7},{7,6},{8,9},{9,8},{10,11... | collective-permute-start | bytes 786440 | tf_op jit(solution)/shard_map/ppermute | solution.py:141
  157.7 1.0 copy-start.7
  159.4 11.4 %collective-permute-start.1 = (bf16[256,512]{1,0:T(8,128)(2,1)}, bf16[256,512]{1,0:T(8,128)(2,1)}, u32[]{:S(2)}, u32[]{:S(2)}) collective-permute-start(bf16[256,512]{1,0:T(8,128)(2,1)} %dynamic-slice_convert_fusion), channel_id=1, source_target_pairs={{0,1},{1,0},{2,3},{3,2},{4,5},{5,4},{6,7},{7,6},{8,9},{9,8},{10,11... | collective-permute-start | bytes 786440 | tf_op jit(solution)/shard_map/ppermute | solution.py:141
Sparse Core Ops, SparseCore 0:
  81.2 38.2 all-gather.2

commit v2 on v1

v2 whole, which is shorter than its diff:
```python
import math

import jax
import jax.numpy as jnp
from jax import lax
from jax.experimental import pallas as pl
from jax.experimental.pallas import tpu as pltpu
from jax.sharding import PartitionSpec as P

LAT_DEV = 32768
BLOCK = 128
STEPS = 2048
BITS = 13


def sel_kernel(place_ref, top_idx, top_val, aux_idx, aux_val, dead, out, packed, found):
    slots = dead.shape[1]
    n_aux = aux_idx.shape[1]
    n_top = top_idx.shape[1]
    rows = top_idx.shape[0]
    side = math.isqrt(rows // 2)
    core, lat = place_ref[0], place_ref[1]
    n_blocks = slots // BLOCK

    def pack(col, val):
        return col * (1 << BITS) + (val[...].astype(jnp.float32) * STEPS).astype(jnp.int32)

    col = aux_idx[...] - lat * slots
    col = jnp.where((col >= 0) & (col < slots), (col + core * (slots // 2)) & (slots - 1), -1)
    col = pack(col, aux_val)
    for i in range(n_aux // 128):
        packed[rows * i : rows * (i + 1), :] = col[:, 128 * i : 128 * (i + 1)]
    block, inside = top_idx[...] >> 7, top_idx[...] & (BLOCK - 1)
    col = jnp.full(top_idx.shape, -1, jnp.int32)
    for m in range(n_blocks):
        col = jnp.where(block == place_ref[2 + m], m * BLOCK + inside, col)
    packed[rows * (n_aux // 128) :, :n_top] = pack(col, top_val)

    lanes = [lax.broadcasted_iota(jnp.int32, (side, 128), 1) + 128 * k for k in range(slots // 128)]
    zero = tuple(jnp.zeros((side, 128), jnp.int32) for _ in lanes)

    def step(a, carry):
        def put(acc, i, width):
            along_x = packed[pl.ds(rows * i + 2 * side * a, side, stride=2), :]
            along_y = packed[pl.ds(rows * i + 2 * a + 1, side, stride=2 * side), :]
            part = jnp.where(core == 0, along_x, along_y)
            for j in range(width):
                v = jnp.broadcast_to(part[:, j : j + 1], (side, 128))
                c = v >> BITS
                acc = [jnp.where(c == lane, v, a) for lane, a in zip(lanes, acc)]
            return tuple(acc)

        main = put(zero, n_aux // 128, n_top)
        aux = lax.fori_loop(0, n_aux // 128, lambda i, acc: put(acc, i, 128), zero)
        to = pl.ds(pl.multiple_of(a * side, side), side)
        for k in range(len(lanes)):
            found[to, 128 * k : 128 * k + 128] = main[k]
            found[to, slots + 128 * k : slots + 128 * k + 128] = aux[k]
        return carry

    lax.fori_loop(0, side, step, 0)
    value = (found[...] & ((1 << BITS) - 1)).astype(jnp.float32) * (1.0 / STEPS)
    out[:, :slots] = value[:, :slots].astype(jnp.bfloat16)
    out[:, slots:] = (value[:, slots:] * dead[...].astype(jnp.float32)).astype(jnp.bfloat16)


def make_sel(place, top_idx, top_val, aux_idx, aux_val, dead):
    rows = top_idx.shape[0]
    parts = aux_idx.shape[1] // 128 + 1
    slots = dead.shape[1]
    whole = pl.BlockSpec(memory_space=pltpu.VMEM)
    return pl.pallas_call(
        sel_kernel,
        in_specs=[pl.BlockSpec(memory_space=pltpu.SMEM)] + [whole] * 5,
        out_specs=whole,
        out_shape=jax.ShapeDtypeStruct((rows // 2, 2 * slots), jnp.bfloat16),
        scratch_shapes=[
            pltpu.VMEM((rows * parts, 128), jnp.int32),
            pltpu.VMEM((rows // 2, 2 * slots), jnp.int32),
        ],
        cost_estimate=pl.CostEstimate(
            flops=rows * parts * 128 * slots * 32, bytes_accessed=1 << 20, transcendentals=0
        ),
        name="sel",
    )(place, top_idx, top_val, aux_idx, aux_val, dead)


def rows_dot(left, right):
    return lax.dot_general(
        left, right, (((1,), (1,)), ((), ())), preferred_element_type=jnp.float32
    )


def cols_dot(left, right):
    return lax.dot_general(
        left, right, (((0,), (0,)), ((), ())), preferred_element_type=jnp.float32
    )


def plane_groups(n_dp, side, n_in):
    def device(z, y, x, c):
        return ((z * side + y) * side + x) * n_in + c

    ranks = range(side)
    along_x = [[[device(z, y, x, c) for x in ranks] for z in range(n_dp) for y in ranks] for c in range(2)]
    along_y = [[[device(z, y, x, c) for y in ranks] for z in range(n_dp) for x in ranks] for c in range(2)]
    return along_x[0] + along_y[1], along_y[0] + along_x[1]


def local(
    n_dp, n_lat, n_in, err_main, err_aux, resid, top_idx, top_val, aux_idx, aux_val, blocks, dead, dec_rows
):
    width, d = dec_rows.shape
    cols = d // n_dp
    slots = width * n_in
    side = math.isqrt(n_lat)
    dp = lax.axis_index("dp")
    lat = lax.axis_index("lat")
    core = lax.axis_index("inner")
    swap = [(i, (i + 1) % n_in) for i in range(n_in)]
    first, second = plane_groups(n_dp, side, n_in)

    def grow(v, step):
        got = lax.ppermute(v, "dp", [(i, i ^ step) for i in range(n_dp)])
        return jnp.concatenate([v, got], axis=0)

    def spread(v, groups):
        return lax.all_to_all(
            jnp.broadcast_to(v[None], (side,) + v.shape),
            ("dp", "lat", "inner"), 0, 0, axis_index_groups=groups, tiled=True,
        )

    full = jnp.concatenate([err_main, err_aux], axis=0)
    cut = jnp.concatenate([full, resid, resid], axis=0).reshape(4, n_dp, cols).transpose(1, 0, 2)
    cut = lax.all_to_all(cut, "dp", 0, 0, tiled=True)
    cut = cut[:, :3].reshape(2, 2, 2, 3, cols)
    for bit in range(3):
        cut = jnp.where((dp >> bit) & 1 == 1, jnp.flip(cut, 2 - bit), cut)
    cut = cut.transpose(3, 2, 1, 0, 4).reshape(2, 3 * n_dp * cols // 2)

    near = spread(jnp.concatenate([full, cut], axis=1), first)
    full = spread(near[:, :, :d], second)
    part = spread(near[:, :, d:].reshape(side, 3 * n_dp, cols), second)
    part = part.reshape(n_lat, 3, n_dp, cols)
    main, aux, res = (part[:, i].reshape(n_lat * n_dp, cols) for i in range(3))

    dec_other = lax.ppermute(dec_rows, "inner", swap)
    small = jnp.concatenate([dead, blocks, jnp.zeros((128 - blocks.shape[0],), jnp.int32)])
    small_other = lax.ppermute(small, "inner", swap)
    dead_all = jnp.concatenate([dead, small_other[:width]])[None]
    table = jnp.concatenate([blocks, small_other[width : width + blocks.shape[0]]])
    owner = lat * n_in + (core + jnp.arange(table.shape[0], dtype=jnp.int32) // blocks.shape[0]) % n_in
    keys = jnp.where(table >= 0, owner * (LAT_DEV // BLOCK) + table, -1)
    place = jnp.concatenate([jnp.stack([core, lat]), keys])
    sel = make_sel(place, top_idx, top_val, aux_idx, aux_val, dead_all)
    sel_all = grow(sel[None], 4)
    sel_all, full = lax.optimization_barrier((sel_all, full))
    sel_all = grow(grow(sel_all, 2), 1).transpose(1, 0, 2).reshape(n_lat * n_dp, 2 * slots)

    both = full.reshape(n_lat, 2, d).transpose(1, 0, 2).reshape(2 * n_lat, d)
    dval = jnp.concatenate([rows_dot(both, dec_rows), rows_dot(both, dec_other)], axis=1)
    dpre = jnp.where(sel[:, :slots] > 0, dval[:n_lat], 0.0) + jnp.where(
        sel[:, slots:] > 0, dval[n_lat:], 0.0
    )
    dpre_all = grow(grow(grow(dpre.astype(jnp.bfloat16)[None], 4), 2), 1)
    dpre_all = dpre_all.transpose(1, 0, 2).reshape(n_lat * n_dp, slots)

    def half(other):
        def pick(table, i):
            return table[:, i * slots + other * width : i * slots + (other + 1) * width]

        dec_term = cols_dot(pick(sel_all, 0), main) + cols_dot(pick(sel_all, 1), aux)
        return dec_term, cols_dot(pick(dpre_all, 0), res)

    sent = jnp.stack(half(1)).astype(jnp.bfloat16)
    got = lax.ppermute(sent, "inner", swap).astype(jnp.float32)
    dec_term, enc_term = half(0)
    return ((dec_term + got[0]).astype(jnp.bfloat16), (enc_term + got[1]).astype(jnp.bfloat16))


def solution(mesh):
    tokens = P(("dp", "lat", "inner"), None)
    shard = ("lat", "inner")
    in_specs = (tokens,) * 3 + (P("dp", None),) * 4 + (P(shard), P(shard), P(shard, None))
    out_specs = (P(shard, "dp"), P(shard, "dp"))
    n_dp, n_lat, n_in = (mesh.shape[a] for a in ("dp", "lat", "inner"))

    def step(*args):
        return local(n_dp, n_lat, n_in, *args)

    return jax.shard_map(step, mesh=mesh, in_specs=in_specs, out_specs=out_specs, check_vma=False)
```

time: 180 us -> 165 us (0.917)
  waiting for transfers between devices: 35.2 us -> 50.2 us
  between operations: 15 us -> 1.02 us
  starting transfers between devices: 53.4 us -> 65.4 us
  other arithmetic: 13.8 us -> 5.16 us
  Pallas kernels: 20.5 us -> 12.9 us
  blocking collectives: 24.4 us -> 17.1 us
  local copies, waits for them, and re-layouts: 11.4 us -> 5.7 us
    all_gather x1 -> x0, waiting for transfers between devices: 32.2 us -> none  [local(): sel = lax.all_gather(sel, 'dp', axis=0, tiled=True)]
    ppermute x2 -> x9, waiting for transfers between devices: 0.01 us -> 31.6 us  [the longest x6 30.4 us: grow(): got = lax.ppermute(v, 'dp', [(i, i ^ step) for i in range(n_dp)])]
    ppermute x2 -> x9, starting transfers between devices: 18.4 us -> 38 us  [the longest x6 22 us: grow(): got = lax.ppermute(v, 'dp', [(i, i ^ step) for i in range(n_dp)])]
    all_to_all x3, waiting for transfers between devices: 2.99 us -> 18.7 us  [the longest x2 11.8 us: spread(): lax.all_to_all(jnp.broadcast_to(v[None], (side,) + v.shape), ('dp', 'lat'...]
    pallas_call x1, Pallas kernels: 20.5 us -> 12.9 us  [make_sel(): pl.pallas_call(sel_kernel, in_specs=[pl.BlockSpec(memory_space=pltpu.SMEM...]
    all_to_all x3, starting transfers between devices: 35 us -> 27.4 us  [the longest x1 17.2 us: local(): cut = lax.all_to_all(cut, 'dp', 0, 0, tiled=True)]
    convert_element_type x6 -> x1, other arithmetic: 7.1 us -> 0.11 us  [local(): got = lax.ppermute(sent, 'inner', swap).astype(jnp.float32)]
    all_gather x2 -> x0, blocking collectives: 6.03 us -> none  [the longest x1 3.85 us: local(): dead_all = lax.all_gather(dead, 'inner', axis=0, tiled=True)]
  transfers between devices with their start and end apart: 6 -> 12, of which waited for: 4 -> 7; matrix products, arithmetic and copies ran while one was open for 11% -> 6% of each run, Pallas kernels for 11% -> 8%
where the time goes in v2:
time: 165 us; the launch traced here: 164 us
  starting transfers between devices  65.4 us (40%)
  waiting for transfers between devices  50.2 us (30%)
  blocking collectives  17.1 us (10%)
  Pallas kernels  12.9 us (8%)
  matrix products  6.66 us (4%)
  local copies, waits for them, and re-layouts  5.7 us (3%)
  other arithmetic  5.16 us (3%)
    ppermute x6, waiting for transfers between devices, grow(): got = lax.ppermute(v, 'dp', [(i, i ^ step) for i in range(n_dp)])  30.4 us
    ppermute x6, starting transfers between devices, grow(): got = lax.ppermute(v, 'dp', [(i, i ^ step) for i in range(n_dp)])  22 us
    all_to_all x1, starting transfers between devices, local(): cut = lax.all_to_all(cut, 'dp', 0, 0, tiled=True)  17.2 us
    all_to_all x1, blocking collectives, spread(): lax.all_to_all(jnp.broadcast_to(v[None], (side,) + v.shape), ('dp', 'lat'...  17.1 us
    pallas_call x1, Pallas kernels, make_sel(): pl.pallas_call(sel_kernel, in_specs=[pl.BlockSpec(memory_space=pltpu.SMEM...  12.9 us
    all_to_all x2, waiting for transfers between devices, spread(): lax.all_to_all(jnp.broadcast_to(v[None], (side,) + v.shape), ('dp', 'lat'...  11.8 us
    all_to_all x2, starting transfers between devices, spread(): lax.all_to_all(jnp.broadcast_to(v[None], (side,) + v.shape), ('dp', 'lat'...  10.2 us
    all_to_all x1, waiting for transfers between devices, local(): cut = lax.all_to_all(cut, 'dp', 0, 0, tiled=True)  6.88 us
  transfers between devices with their start and end apart: 12, of which 7 were waited for; matrix products, arithmetic and copies ran while one was open for 6% of the time, Pallas kernels for 8%

profile of v2, /device:TPU:1, one launch (start us, length us, event | category | flops | bytes accessed | tf_op | source)
XLA Modules:
  0.0 164.2 jit_solution(819631479246993340)
XLA Ops:
  0.6 1.5 pad_maximum_fusion.7
  2.1 17.2 %all-to-all-start = ((bf16[8,4,512]{2,1,0:T(4,128)(2,1)}), bf16[8,4,512]{2,1,0:T(4,128)(2,1)S(1)}, u32[]{:S(2)}, u32[]{:S(2)}) async-start(bf16[8,4,512]{2,1,0:T(4,128)(2,1)} %bitcast.5), calls=%async_computation | async-start | bytes 65536 | tf_op jit(solution)/shard_map/all_to_all | solution.py:135
  19.4 6.9 %all-to-all-done = bf16[8,4,512]{2,1,0:T(4,128)(2,1)S(1)} async-done(((bf16[8,4,512]{2,1,0:T(4,128)(2,1)}), bf16[8,4,512]{2,1,0:T(4,128)(2,1)S(1)}, u32[]{:S(2)}, u32[]{:S(2)}) %all-to-all-start) | async-done | bytes 32800 | tf_op jit(solution)/shard_map/all_to_all | solution.py:135
  26.3 0.2 rev.12
  26.7 0.8 pad_maximum_fusion.6
  27.5 0.2 broadcast_in_dim.41
  27.7 17.1 %all_to_all.20 = bf16[8,2,10240]{2,1,0:T(2,128)(2,1)S(1)} all-to-all(bf16[8,2,10240]{2,1,0:T(2,128)(2,1)S(1)} %broadcast_in_dim.41), channel_id=1, replica_groups={{0,2,4,6,8,10,12,14},{16,18,20,22,24,26,28,30},{32,34,36,38,40,42,44,46..., dimensions={0} | all-to-all | bytes 655360 | tf_op jit(solution)/shard_map/all_to_all | solution.py:128
  44.8 0.1 slice.81
  44.9 0.1 copy.28
  44.9 1.1 broadcast_in_dim.42
  46.0 6.5 %all-to-all-start.2 = ((bf16[8,8,2,4096]{3,1,2,0:T(8,128)(2,1)}), bf16[8,8,2,4096]{3,1,2,0:T(8,128)(2,1)S(1)}, u32[]{:S(2)}, u32[]{:S(2)}) async-start(bf16[8,8,2,4096]{3,1,2,0:T(8,128)(2,1)} %broadcast_in_dim.42), calls=%async_computation.2 | async-start | bytes 2097152 | tf_op jit(solution)/shard_map/all_to_all | solution.py:128
  52.5 5.7 %collective-permute-start.4 = (bf16[256,4096]{1,0:T(8,128)(2,1)}, bf16[256,4096]{1,0:T(8,128)(2,1)}, u32[]{:S(2)}, u32[]{:S(2)}) collective-permute-start(bf16[256,4096]{1,0:T(8,128)(2,1)} %param.19), channel_id=1, source_target_pairs={{0,1},{1,0},{2,3},{3,2},{4,5},{5,4},{6,7},{7,6},{8,9},{9,8},{10,11... | collective-permute-start | bytes 6291464 | tf_op jit(solution)/shard_map/ppermute | solution.py:147
  58.2 0.1 slice.83
  58.4 0.1 broadcast_in_dim.43
  58.5 11.8 %all-to-all-done.2 = bf16[8,8,2,4096]{3,1,2,0:T(8,128)(2,1)S(1)} async-done(((bf16[8,8,2,4096]{3,1,2,0:T(8,128)(2,1)}), bf16[8,8,2,4096]{3,1,2,0:T(8,128)(2,1)S(1)}, u32[]{:S(2)}, u32[]{:S(2)}) %all-to-all-start.2) | async-done | bytes 1048608 | tf_op jit(solution)/shard_map/all_to_all | solution.py:128
  70.3 1.3 broadcast_in_dim.44
  71.6 3.7 %all-to-all-start.3 = ((bf16[8,8,24,512]{3,2,1,0:T(8,128)(2,1)}), bf16[8,8,24,512]{3,2,1,0:T(8,128)(2,1)S(1)}, u32[]{:S(2)}, u32[]{:S(2)}) async-start(bf16[8,8,24,512]{3,2,1,0:T(8,128)(2,1)} %broadcast_in_dim.44), calls=%async_computation.3 | async-start | bytes 3145728 | tf_op jit(solution)/shard_map/all_to_all | solution.py:128
  75.3 0.0 copy-done.4
  75.4 0.0 copy-done.5
  75.4 0.1 pad_add_fusion
  75.4 6.9 %collective-permute-start = (s32[384]{0:T(512)S(1)}, s32[384]{0:T(512)S(1)}, u32[]{:S(2)}, u32[]{:S(2)}) collective-permute-start(s32[384]{0:T(512)S(1)} %pad_add_fusion), channel_id=1, source_target_pairs={{0,1},{1,0},{2,3},{3,2},{4,5},{5,4},{6,7},{7,6},{8,9},{9,8},{10,11... | collective-permute-start | bytes 4616 | tf_op jit(solution)/shard_map/ppermute | solution.py:149
  82.3 0.0 copy-done.2
  82.3 0.7 copy.24.top_idx
  83.1 0.0 copy-done.3
  83.1 0.7 copy.25.top_val
  83.8 0.0 collective-permute-done
  83.8 0.1 compare_select_fusion.2
  83.9 0.7 pad_add_fusion.2.place_ref
  84.5 0.6 pad_add_fusion.1
  85.1 12.9 %sel.1 = bf16[64,1024]{1,0:T(8,128)(2,1)} custom-call(s32[6]{0:T(128)} %pad_add_fusion.2.place_ref, s32[128,64]{1,0:T(8,128)} %copy.24.top_idx, bf16[128,64]{1,0:T(8,128)(2,1)} %copy.25.top_val, s32[128,512]{1,0:T(8,128)} %aux_idx.1, bf16[128,512]{1,0:T(8,128)(2,1)} %aux_val.1, s32[1,512]{1,0:T(1,128)} %bitcast.83), custom_call_target="tpu_custom_call" | custom-call | flops 1342177280 | bytes 1048576 | tf_op jit(solution)/shard_map/sel/pallas_call | solution.py:72
  98.0 2.3 %collective-permute-start.1 = (bf16[1,64,1024]{2,1,0:T(8,128)(2,1)}, bf16[1,64,1024]{2,1,0:T(8,128)(2,1)S(1)}, u32[]{:S(2)}, u32[]{:S(2)}) collective-permute-start(bf16[1,64,1024]{2,1,0:T(8,128)(2,1)} %bitcast.79), channel_id=1, source_target_pairs={{0,512},{128,640},{256,768},{384,896},{512,0},{640,128},{768,256},... | collective-permute-start | bytes 393224 | tf_op jit(solution)/shard_map/ppermute | solution.py:124
  100.3 9.1 %collective-permute-done.1 = bf16[1,64,1024]{2,1,0:T(8,128)(2,1)S(1)} collective-permute-done((bf16[1,64,1024]{2,1,0:T(8,128)(2,1)}, bf16[1,64,1024]{2,1,0:T(8,128)(2,1)S(1)}, u32[]{:S(2)}, u32[]{:S(2)}) %collective-permute-start.1) | collective-permute-done | bytes 131104 | tf_op jit(solution)/shard_map/ppermute | solution.py:124
  109.4 0.9 pad_maximum_fusion.2
  110.4 0.1 copy.30
  110.4 4.7 %collective-permute-start.2 = (bf16[2,64,1024]{2,1,0:T(8,128)(2,1)S(1)}, bf16[2,64,1024]{2,1,0:T(8,128)(2,1)S(1)}, u32[]{:S(2)}, u32[]{:S(2)}) collective-permute-start(bf16[2,64,1024]{2,1,0:T(8,128)(2,1)S(1)} %pad_maximum_fusion.2), channel_id=1, source_target_pairs={{0,256},{128,384},{256,0},{384,128},{512,768},{640,896},{768,512},... | collective-permute-start | bytes 786440 | tf_op jit(solution)/shard_map/ppermute | solution.py:124
  115.2 0.0 copy-done
  115.2 0.8 fusion.28
  116.0 0.0 copy-start.1
  116.0 0.0 collective-permute-done.4
  116.0 2.5 %fusion.29 = f32[128,256]{1,0:T(8,128)S(1)} fusion(bf16[128,4096]{1,0:T(8,128)(2,1)S(1)} %bitcast.66, bf16[256,4096]{1,0:T(8,128)(2,1)} %collective-permute-done.4), kind=kOutput, calls=%fused_computation.65 | convolution fusion | flops 268435456 | bytes 3276800 | tf_op jit(solution)/shard_map/dot_general | solution.py:89
  118.6 4.4 %collective-permute-start.5 = (bf16[1,64,512]{2,1,0:T(8,128)(2,1)S(1)}, bf16[1,64,512]{2,1,0:T(8,128)(2,1)S(1)}, u32[]{:S(2)}, u32[]{:S(2)}) collective-permute-start(bf16[1,64,512]{2,1,0:T(8,128)(2,1)S(1)} %fusion.21), channel_id=1, source_target_pairs={{0,512},{128,640},{256,768},{384,896},{512,0},{640,128},{768,256},... | collective-permute-start | bytes 196616 | tf_op jit(solution)/shard_map/ppermute | solution.py:124
  123.0 4.6 %collective-permute-done.5 = bf16[1,64,512]{2,1,0:T(8,128)(2,1)S(1)} collective-permute-done((bf16[1,64,512]{2,1,0:T(8,128)(2,1)S(1)}, bf16[1,64,512]{2,1,0:T(8,128)(2,1)S(1)}, u32[]{:S(2)}, u32[]{:S(2)}) %collective-permute-start.5) | collective-permute-done | bytes 65568 | tf_op jit(solution)/shard_map/ppermute | solution.py:124
  127.7 6.7 %collective-permute-start.6 = (bf16[2,64,512]{2,1,0:T(8,128)(2,1)S(1)}, bf16[2,64,512]{2,1,0:T(8,128)(2,1)S(1)}, u32[]{:S(2)}, u32[]{:S(2)}) collective-permute-start(bf16[2,64,512]{2,1,0:T(8,128)(2,1)S(1)} %pad_maximum_fusion.5), channel_id=1, source_target_pairs={{0,256},{128,384},{256,0},{384,128},{512,768},{640,896},{768,512},... | collective-permute-start | bytes 393224 | tf_op jit(solution)/shard_map/ppermute | solution.py:124
  134.4 0.0 collective-permute-done.2
  134.5 1.9 %collective-permute-start.3 = (bf16[4,64,1024]{2,1,0:T(8,128)(2,1)S(1)}, bf16[4,64,1024]{2,1,0:T(8,128)(2,1)S(1)}, u32[]{:S(2)}, u32[]{:S(2)}) collective-permute-start(bf16[4,64,1024]{2,1,0:T(8,128)(2,1)S(1)} %pad_maximum_fusion), channel_id=1, source_target_pairs={{0,128},{128,0},{256,384},{384,256},{512,640},{640,512},{768,896},... | collective-permute-start | bytes 1572872 | tf_op jit(solution)/shard_map/ppermute | solution.py:124
  136.4 2.8 %collective-permute-done.6 = bf16[2,64,512]{2,1,0:T(8,128)(2,1)S(1)} collective-permute-done((bf16[2,64,512]{2,1,0:T(8,128)(2,1)S(1)}, bf16[2,64,512]{2,1,0:T(8,128)(2,1)S(1)}, u32[]{:S(2)}, u32[]{:S(2)}) %collective-permute-start.6) | collective-permute-done | bytes 131104 | tf_op jit(solution)/shard_map/ppermute | solution.py:124
  139.3 1.9 %collective-permute-start.7 = (bf16[4,64,512]{2,1,0:T(8,128)(2,1)S(1)}, bf16[4,64,512]{2,1,0:T(8,128)(2,1)S(1)}, u32[]{:S(2)}, u32[]{:S(2)}) collective-permute-start(bf16[4,64,512]{2,1,0:T(8,128)(2,1)S(1)} %pad_maximum_fusion.3), channel_id=1, source_target_pairs={{0,128},{128,0},{256,384},{384,256},{512,640},{640,512},{768,896},... | collective-permute-start | bytes 786440 | tf_op jit(solution)/shard_map/ppermute | solution.py:124
  141.2 13.8 %collective-permute-done.7 = bf16[4,64,512]{2,1,0:T(8,128)(2,1)S(1)} collective-permute-done((bf16[4,64,512]{2,1,0:T(8,128)(2,1)S(1)}, bf16[4,64,512]{2,1,0:T(8,128)(2,1)S(1)}, u32[]{:S(2)}, u32[]{:S(2)}) %collective-permute-start.7) | collective-permute-done | bytes 262176 | tf_op jit(solution)/shard_map/ppermute | solution.py:124
  155.0 0.1 maximum_bitcast_fusion.1
  155.0 0.3 copy.37
  155.3 0.0 collective-permute-done.3
  155.3 0.1 maximum_bitcast_fusion
  155.5 0.6 copy.36
  156.0 0.0 all-to-all-done.3
  156.1 0.3 fusion.1
  156.4 0.3 fusion.7
  156.7 0.3 fusion.2
  157.0 0.1 pad_maximum_fusion.1
  157.1 3.4 %collective-permute-start.8 = (bf16[2,256,512]{2,1,0:T(8,128)(2,1)S(1)}, bf16[2,256,512]{2,1,0:T(8,128)(2,1)S(1)}, u32[]{:S(2)}, u32[]{:S(2)}) collective-permute-start(bf16[2,256,512]{2,1,0:T(8,128)(2,1)S(1)} %pad_maximum_fusion.1), channel_id=1, source_target_pairs={{0,1},{1,0},{2,3},{3,2},{4,5},{5,4},{6,7},{7,6},{8,9},{9,8},{10,11... | collective-permute-start | bytes 1572872 | tf_op jit(solution)/shard_map/ppermute | solution.py:176
  160.5 0.3 fusion.8
  160.9 1.2 collective-permute-done.8
  162.0 0.1 convert_element_type.14
  162.2 1.0 fusion.4
  163.2 1.0 fusion.6
  (19 shorter events, 0.3 us)
Async XLA Ops:
  2.1 24.1 %all-to-all-start = ((bf16[8,4,512]{2,1,0:T(4,128)(2,1)}), bf16[8,4,512]{2,1,0:T(4,128)(2,1)S(1)}, u32[]{:S(2)}, u32[]{:S(2)}) async-start(bf16[8,4,512]{2,1,0:T(4,128)(2,1)} %bitcast.5), calls=%async_computation | async-start | bytes 65536 | tf_op jit(solution)/shard_map/all_to_all | solution.py:135
  46.0 24.3 %all-to-all-start.2 = ((bf16[8,8,2,4096]{3,1,2,0:T(8,128)(2,1)}), bf16[8,8,2,4096]{3,1,2,0:T(8,128)(2,1)S(1)}, u32[]{:S(2)}, u32[]{:S(2)}) async-start(bf16[8,8,2,4096]{3,1,2,0:T(8,128)(2,1)} %broadcast_in_dim.42), calls=%async_computation.2 | async-start | bytes 2097152 | tf_op jit(solution)/shard_map/all_to_all | solution.py:128
  52.5 63.5 %collective-permute-start.4 = (bf16[256,4096]{1,0:T(8,128)(2,1)}, bf16[256,4096]{1,0:T(8,128)(2,1)}, u32[]{:S(2)}, u32[]{:S(2)}) collective-permute-start(bf16[256,4096]{1,0:T(8,128)(2,1)} %param.19), channel_id=1, source_target_pairs={{0,1},{1,0},{2,3},{3,2},{4,5},{5,4},{6,7},{7,6},{8,9},{9,8},{10,11... | collective-permute-start | bytes 6291464 | tf_op jit(solution)/shard_map/ppermute | solution.py:147
  71.6 3.8 %copy-start.4 = (s32[256]{0:T(256)S(1)}, s32[256]{0:T(256)}, u32[]{:S(2)}) copy-start(s32[256]{0:T(256)} %param.18) | copy-start | bytes 3076
  71.6 3.8 %copy-start.5 = (s32[2]{0:T(128)S(1)}, s32[2]{0:T(128)}, u32[]{:S(2)}) copy-start(s32[2]{0:T(128)} %param.17) | copy-start | bytes 28
  71.6 10.7 %copy-start.2 = (s32[128,64]{0,1:T(8,128)S(1)}, s32[128,64]{0,1:T(8,128)}, u32[]{:S(2)}) copy-start(s32[128,64]{0,1:T(8,128)} %param.13) | copy-start | bytes 98308
  71.6 11.5 %copy-start.3 = (bf16[128,64]{0,1:T(8,128)(2,1)S(1)}, bf16[128,64]{0,1:T(8,128)(2,1)}, u32[]{:S(2)}) copy-start(bf16[128,64]{0,1:T(8,128)(2,1)} %param.14) | copy-start | bytes 49156
  71.6 84.4 %all-to-all-start.3 = ((bf16[8,8,24,512]{3,2,1,0:T(8,128)(2,1)}), bf16[8,8,24,512]{3,2,1,0:T(8,128)(2,1)S(1)}, u32[]{:S(2)}, u32[]{:S(2)}) async-start(bf16[8,8,24,512]{3,2,1,0:T(8,128)(2,1)} %broadcast_in_dim.44), calls=%async_computation.3 | async-start | bytes 3145728 | tf_op jit(solution)/shard_map/all_to_all | solution.py:128
  75.4 8.3 %collective-permute-start = (s32[384]{0:T(512)S(1)}, s32[384]{0:T(512)S(1)}, u32[]{:S(2)}, u32[]{:S(2)}) collective-permute-start(s32[384]{0:T(512)S(1)} %pad_add_fusion), channel_id=1, source_target_pairs={{0,1},{1,0},{2,3},{3,2},{4,5},{5,4},{6,7},{7,6},{8,9},{9,8},{10,11... | collective-permute-start | bytes 4616 | tf_op jit(solution)/shard_map/ppermute | solution.py:149
  98.0 17.1 %copy-start = (bf16[256,4096]{1,0:T(8,128)(2,1)S(1)}, bf16[256,4096]{1,0:T(8,128)(2,1)}, u32[]{:S(2)}) copy-start(bf16[256,4096]{1,0:T(8,128)(2,1)} %param.19) | copy-start | bytes 6291460
  98.0 11.4 %collective-permute-start.1 = (bf16[1,64,1024]{2,1,0:T(8,128)(2,1)}, bf16[1,64,1024]{2,1,0:T(8,128)(2,1)S(1)}, u32[]{:S(2)}, u32[]{:S(2)}) collective-permute-start(bf16[1,64,1024]{2,1,0:T(8,128)(2,1)} %bitcast.79), channel_id=1, source_target_pairs={{0,512},{128,640},{256,768},{384,896},{512,0},{640,128},{768,256},... | collective-permute-start | bytes 393224 | tf_op jit(solution)/shard_map/ppermute | solution.py:124
  110.4 24.0 %collective-permute-start.2 = (bf16[2,64,1024]{2,1,0:T(8,128)(2,1)S(1)}, bf16[2,64,1024]{2,1,0:T(8,128)(2,1)S(1)}, u32[]{:S(2)}, u32[]{:S(2)}) collective-permute-start(bf16[2,64,1024]{2,1,0:T(8,128)(2,1)S(1)} %pad_maximum_fusion.2), channel_id=1, source_target_pairs={{0,256},{128,384},{256,0},{384,128},{512,768},{640,896},{768,512},... | collective-permute-start | bytes 786440 | tf_op jit(solution)/shard_map/ppermute | solution.py:124
  116.0 2.5 %copy-start.1 = (bf16[64,1024]{1,0:T(8,128)(2,1)S(1)}, bf16[64,1024]{1,0:T(8,128)(2,1)}, u32[]{:S(2)}) copy-start(bf16[64,1024]{1,0:T(8,128)(2,1)} %sel.1) | copy-start | bytes 393220
  118.6 9.1 %collective-permute-start.5 = (bf16[1,64,512]{2,1,0:T(8,128)(2,1)S(1)}, bf16[1,64,512]{2,1,0:T(8,128)(2,1)S(1)}, u32[]{:S(2)}, u32[]{:S(2)}) collective-permute-start(bf16[1,64,512]{2,1,0:T(8,128)(2,1)S(1)} %fusion.21), channel_id=1, source_target_pairs={{0,512},{128,640},{256,768},{384,896},{512,0},{640,128},{768,256},... | collective-permute-start | bytes 196616 | tf_op jit(solution)/shard_map/ppermute | solution.py:124
  127.7 11.6 %collective-permute-start.6 = (bf16[2,64,512]{2,1,0:T(8,128)(2,1)S(1)}, bf16[2,64,512]{2,1,0:T(8,128)(2,1)S(1)}, u32[]{:S(2)}, u32[]{:S(2)}) collective-permute-start(bf16[2,64,512]{2,1,0:T(8,128)(2,1)S(1)} %pad_maximum_fusion.5), channel_id=1, source_target_pairs={{0,256},{128,384},{256,0},{384,128},{512,768},{640,896},{768,512},... | collective-permute-start | bytes 393224 | tf_op jit(solution)/shard_map/ppermute | solution.py:124
  134.5 20.8 %collective-permute-start.3 = (bf16[4,64,1024]{2,1,0:T(8,128)(2,1)S(1)}, bf16[4,64,1024]{2,1,0:T(8,128)(2,1)S(1)}, u32[]{:S(2)}, u32[]{:S(2)}) collective-permute-start(bf16[4,64,1024]{2,1,0:T(8,128)(2,1)S(1)} %pad_maximum_fusion), channel_id=1, source_target_pairs={{0,128},{128,0},{256,384},{384,256},{512,640},{640,512},{768,896},... | collective-permute-start | bytes 1572872 | tf_op jit(solution)/shard_map/ppermute | solution.py:124
  139.3 15.7 %collective-permute-start.7 = (bf16[4,64,512]{2,1,0:T(8,128)(2,1)S(1)}, bf16[4,64,512]{2,1,0:T(8,128)(2,1)S(1)}, u32[]{:S(2)}, u32[]{:S(2)}) collective-permute-start(bf16[4,64,512]{2,1,0:T(8,128)(2,1)S(1)} %pad_maximum_fusion.3), channel_id=1, source_target_pairs={{0,128},{128,0},{256,384},{384,256},{512,640},{640,512},{768,896},... | collective-permute-start | bytes 786440 | tf_op jit(solution)/shard_map/ppermute | solution.py:124
  157.1 4.9 %collective-permute-start.8 = (bf16[2,256,512]{2,1,0:T(8,128)(2,1)S(1)}, bf16[2,256,512]{2,1,0:T(8,128)(2,1)S(1)}, u32[]{:S(2)}, u32[]{:S(2)}) collective-permute-start(bf16[2,256,512]{2,1,0:T(8,128)(2,1)S(1)} %pad_maximum_fusion.1), channel_id=1, source_target_pairs={{0,1},{1,0},{2,3},{3,2},{4,5},{5,4},{6,7},{7,6},{8,9},{9,8},{10,11... | collective-permute-start | bytes 1572872 | tf_op jit(solution)/shard_map/ppermute | solution.py:176

commit v3 on v2

v3 whole, which is shorter than its diff:
```python
import math

import jax
import jax.numpy as jnp
from jax import lax
from jax.experimental import pallas as pl
from jax.experimental.pallas import tpu as pltpu
from jax.sharding import PartitionSpec as P

LAT_DEV = 32768
BLOCK = 128


def sel_kernel(place, top_idx, top_val, aux_idx, aux_val, dead, out, high, low, val, found):
    rows, n_top = top_idx.shape
    n_aux = aux_idx.shape[1]
    slots = dead.shape[1]
    side = math.isqrt(rows // 2)
    tables = 2 * slots // 128
    core = place[0]

    def put(at, col, v):
        to = pl.ds(at, col.shape[1])
        high[:, to] = col >> 7
        low[:, to] = col & 127
        val[:, to] = v[...].astype(jnp.float32)

    col = aux_idx[...] - place[1] * slots
    inside = (col >= 0) & (col < slots)
    put(0, jnp.where(inside, slots + ((col + core * (slots // 2)) & (slots - 1)), -1), aux_val)
    block, inside = top_idx[...] >> 7, top_idx[...] & (BLOCK - 1)
    col = jnp.full(top_idx.shape, -1, jnp.int32)
    for m in range(slots // BLOCK):
        col = jnp.where(block == place[2 + m], m * BLOCK + inside, col)
    put(n_aux, col, top_val)

    n = n_aux + n_top
    row_high = lax.broadcasted_iota(jnp.int32, (tables, n), 0)
    row_low = lax.broadcasted_iota(jnp.int32, (128, n), 0)

    def step(a, carry):
        for b in range(side):
            row = jnp.where(core == 0, 2 * (side * a + b), 2 * (side * b + a) + 1)
            one = pl.ds(row, 1)
            spread = jnp.where(row_high == high[one, :n], val[one, :n], 0.0).astype(jnp.bfloat16)
            hot = jnp.where(row_low == low[one, :n], 1.0, 0.0).astype(jnp.bfloat16)
            table = lax.dot_general(
                spread, hot, (((1,), (1,)), ((), ())), preferred_element_type=jnp.float32
            )
            found[pl.ds(side * a + b, tables, stride=side * side), :] = table
        return carry

    lax.fori_loop(0, side, step, 0)
    for k in range(tables):
        table = found[side * side * k : side * side * (k + 1), :]
        if 128 * k >= slots:
            table = table * dead[:, 128 * k - slots : 128 * (k + 1) - slots].astype(jnp.float32)
        out[:, 128 * k : 128 * (k + 1)] = table.astype(out.dtype)


def make_sel(place, top_idx, top_val, aux_idx, aux_val, dead):
    rows, n_top = top_idx.shape
    entries = aux_idx.shape[1] + 128
    slots = dead.shape[1]
    whole = pl.BlockSpec(memory_space=pltpu.VMEM)
    return pl.pallas_call(
        sel_kernel,
        in_specs=[pl.BlockSpec(memory_space=pltpu.SMEM)] + [whole] * 5,
        out_specs=whole,
        out_shape=jax.ShapeDtypeStruct((rows // 2, 2 * slots), jnp.bfloat16),
        scratch_shapes=[
            pltpu.VMEM((rows, entries), jnp.int32),
            pltpu.VMEM((rows, entries), jnp.int32),
            pltpu.VMEM((rows, entries), jnp.float32),
            pltpu.VMEM((rows * slots // 128, 128), jnp.float32),
        ],
        cost_estimate=pl.CostEstimate(
            flops=rows * entries * slots * 32, bytes_accessed=1 << 20, transcendentals=0
        ),
        name="sel",
    )(place, top_idx, top_val, aux_idx, aux_val, dead)


def rows_dot(left, right):
    return lax.dot_general(
        left, right, (((1,), (1,)), ((), ())), preferred_element_type=jnp.float32
    )


def cols_dot(left, right):
    return lax.dot_general(
        left, right, (((0,), (0,)), ((), ())), preferred_element_type=jnp.float32
    )


def plane_groups(n_dp, side, n_in):
    def device(z, a, b, c):
        y, x = (a, b) if c == 0 else (b, a)
        return ((z * side + y) * side + x) * n_in + c

    ranks, dps, cores = range(side), range(n_dp), range(n_in)
    first = [[device(z, a, b, c) for b in ranks] for z in dps for a in ranks for c in cores]
    wide = [[device(z, a, b, c) for z in dps for b in ranks] for a in ranks for c in cores]
    second = [[device(z, a, b, c) for a in ranks] for z in dps for b in ranks for c in cores]
    return first, wide, second


def local(
    n_dp, n_lat, n_in, err_main, err_aux, resid, top_idx, top_val, aux_idx, aux_val, blocks, dead, dec_rows
):
    width, d = dec_rows.shape
    cols = d // n_dp
    slots = width * n_in
    side = math.isqrt(n_lat)
    dp = lax.axis_index("dp")
    lat = lax.axis_index("lat")
    core = lax.axis_index("inner")
    swap = [(i, (i + 1) % n_in) for i in range(n_in)]
    first, wide, second = plane_groups(n_dp, side, n_in)

    def send(v, step):
        return lax.ppermute(v, "dp", [(i, i ^ step) for i in range(n_dp)])

    def grow(v, step):
        return jnp.concatenate([v, send(v, step)], axis=0)

    def exchange(v, groups):
        return lax.all_to_all(v, ("dp", "lat", "inner"), 0, 0, axis_index_groups=groups, tiled=True)

    def spread(v, groups):
        return exchange(jnp.broadcast_to(v[None], (side,) + v.shape), groups)

    dec_other = lax.ppermute(dec_rows, "inner", swap)
    small = jnp.concatenate([dead, blocks, jnp.zeros((128 - blocks.shape[0],), jnp.int32)])
    small_other = lax.ppermute(small, "inner", swap)
    dead_all = jnp.concatenate([dead, small_other[:width]])[None]
    table = jnp.concatenate([blocks, small_other[width : width + blocks.shape[0]]])
    owner = lat * n_in + (core + jnp.arange(table.shape[0], dtype=jnp.int32) // blocks.shape[0]) % n_in
    keys = jnp.where(table >= 0, owner * (LAT_DEV // BLOCK) + table, -1)
    place = jnp.concatenate([jnp.stack([core, lat]), keys])
    sel = make_sel(place, top_idx, top_val, aux_idx, aux_val, dead_all)

    near = spread(jnp.concatenate([err_main, err_aux], axis=0), first)
    near, sel = lax.optimization_barrier((near, sel))
    full = spread(near, second)
    sel_all = grow(sel[None], 4)

    both = full.reshape(n_lat, 2, d).transpose(1, 0, 2).reshape(2 * n_lat, d)
    dval = jnp.concatenate([rows_dot(both, dec_rows), rows_dot(both, dec_other)], axis=1)
    dpre = jnp.where(sel[:, :slots] > 0, dval[:n_lat], 0.0) + jnp.where(
        sel[:, slots:] > 0, dval[n_lat:], 0.0
    )

    cut = jnp.concatenate([err_main, err_aux, resid, resid], axis=0)
    cut = cut.reshape(4, n_dp, cols).transpose(1, 0, 2)
    cut, sel_all = lax.optimization_barrier((cut, sel_all))
    cut = jnp.broadcast_to(cut[:, None], (n_dp, side, 4, cols)).reshape(n_dp * side, 4, cols)
    cut = exchange(cut, wide).reshape(2, 2, 2, side, 4, cols)
    sel_all = grow(sel_all, 2)
    dpre_all = grow(dpre.astype(jnp.bfloat16)[None], 4)
    cut, sel_all, dpre_all = lax.optimization_barrier((cut, sel_all, dpre_all))
    for bit in range(3):
        cut = jnp.where((dp >> bit) & 1 == 1, jnp.flip(cut, 2 - bit), cut)
    cut = cut[..., :3, :].transpose(3, 4, 2, 1, 0, 5).reshape(side, 3 * n_dp, cols)
    part = spread(cut, second).reshape(n_lat, 3, n_dp, cols)
    main, aux, res = (part[:, i].reshape(n_lat * n_dp, cols) for i in range(3))
    sel_all = grow(sel_all, 1).transpose(1, 0, 2).reshape(n_lat * n_dp, 2 * slots)
    dpre_all = jnp.concatenate([dpre_all] + [send(dpre_all, step) for step in (2, 1, 3)], axis=0)
    dpre_all = dpre_all.transpose(1, 0, 2).reshape(n_lat * n_dp, slots)

    def half(other):
        def pick(table, i):
            return table[:, i * slots + other * width : i * slots + (other + 1) * width]

        dec_term = cols_dot(pick(sel_all, 0), main) + cols_dot(pick(sel_all, 1), aux)
        return dec_term, cols_dot(pick(dpre_all, 0), res)

    sent = jnp.stack(half(1)).astype(jnp.bfloat16)
    got = lax.ppermute(sent, "inner", swap).astype(jnp.float32)
    dec_term, enc_term = half(0)
    return ((dec_term + got[0]).astype(jnp.bfloat16), (enc_term + got[1]).astype(jnp.bfloat16))


def solution(mesh):
    tokens = P(("dp", "lat", "inner"), None)
    shard = ("lat", "inner")
    in_specs = (tokens,) * 3 + (P("dp", None),) * 4 + (P(shard), P(shard), P(shard, None))
    out_specs = (P(shard, "dp"), P(shard, "dp"))
    n_dp, n_lat, n_in = (mesh.shape[a] for a in ("dp", "lat", "inner"))

    def step(*args):
        return local(n_dp, n_lat, n_in, *args)

    return jax.shard_map(step, mesh=mesh, in_specs=in_specs, out_specs=out_specs, check_vma=False)
```

time: 165 us -> 133 us (0.81)
  waiting for transfers between devices: 50.2 us -> 18.3 us
  starting transfers between devices: 65.4 us -> 83.9 us
  blocking collectives: 17.1 us -> 0 us
  Pallas kernels: 12.9 us -> 6.13 us
  local copies, waits for them, and re-layouts: 5.7 us -> 9.18 us
    all_to_all x3 -> x4, waiting for transfers between devices: 18.7 us -> 1.1 us  [exchange(): lax.all_to_all(v, ('dp', 'lat', 'inner'), 0, 0, axis_index_groups=groups,...]
    all_to_all x1 -> x0, blocking collectives: 17.1 us -> none  [spread(): lax.all_to_all(jnp.broadcast_to(v[None], (side,) + v.shape), ('dp', 'lat'...]
    ppermute x6 -> x7, waiting for transfers between devices: 30.4 us -> 16 us  [send(): return lax.ppermute(v, 'dp', [(i, i ^ step) for i in range(n_dp)])]
    ppermute x6 -> x7, starting transfers between devices: 22 us -> 34.5 us  [send(): return lax.ppermute(v, 'dp', [(i, i ^ step) for i in range(n_dp)])]
    ppermute x1, starting transfers between devices: 6.86 us -> 16.1 us  [local(): small_other = lax.ppermute(small, 'inner', swap)]
    pallas_call x1, Pallas kernels: 12.9 us -> 6.13 us  [make_sel(): pl.pallas_call(sel_kernel, in_specs=[pl.BlockSpec(memory_space=pltpu.SMEM...]
    ppermute x1, starting transfers between devices: 5.71 us -> 1.92 us  [local(): dec_other = lax.ppermute(dec_rows, 'inner', swap)]
    ppermute x1, starting transfers between devices: 3.43 us -> 5.59 us  [local(): got = lax.ppermute(sent, 'inner', swap).astype(jnp.float32)]
  transfers between devices with their start and end apart: 12 -> 14, of which waited for: 7 -> 7; matrix products, arithmetic and copies ran while one was open for 6% -> 12% of each run, Pallas kernels for 8% -> 5%
where the time goes in v3:
time: 133 us; the launch traced here: 132 us
  starting transfers between devices  83.9 us (63%)
  waiting for transfers between devices  18.3 us (14%)
  local copies, waits for them, and re-layouts  9.18 us (7%)
  other arithmetic  6.62 us (5%)
  matrix products  6.62 us (5%)
  Pallas kernels  6.13 us (5%)
    ppermute x7, starting transfers between devices, send(): return lax.ppermute(v, 'dp', [(i, i ^ step) for i in range(n_dp)])  34.5 us
    all_to_all x4, starting transfers between devices, exchange(): lax.all_to_all(v, ('dp', 'lat', 'inner'), 0, 0, axis_index_groups=groups,...  25.8 us
    ppermute x1, starting transfers between devices, local(): small_other = lax.ppermute(small, 'inner', swap)  16.1 us
    ppermute x7, waiting for transfers between devices, send(): return lax.ppermute(v, 'dp', [(i, i ^ step) for i in range(n_dp)])  16 us
    pallas_call x1, Pallas kernels, make_sel(): pl.pallas_call(sel_kernel, in_specs=[pl.BlockSpec(memory_space=pltpu.SMEM...  6.13 us
    ppermute x1, starting transfers between devices, local(): got = lax.ppermute(sent, 'inner', swap).astype(jnp.float32)  5.59 us
    dot_general x6, matrix products, cols_dot(): lax.dot_general(left, right, (((0,), (0,)), ((), ())), preferred_element_...  3.36 us
    unnamed x15, local copies, waits for them, and re-layouts  3.3 us
  transfers between devices with their start and end apart: 14, of which 7 were waited for; matrix products, arithmetic and copies ran while one was open for 12% of the time, Pallas kernels for 5%

profile of v3, /device:TPU:1, one launch (start us, length us, event | category | flops | bytes accessed | tf_op | source)
XLA Modules:
  0.0 131.8 jit_solution(11720947431204025842)
XLA Ops:
  0.6 0.8 pad_add_fusion
  1.4 16.1 %collective-permute-start = (s32[384]{0:T(512)S(1)}, s32[384]{0:T(512)S(1)}, u32[]{:S(2)}, u32[]{:S(2)}) collective-permute-start(s32[384]{0:T(512)S(1)} %pad_add_fusion), channel_id=1, source_target_pairs={{0,1},{1,0},{2,3},{3,2},{4,5},{5,4},{6,7},{7,6},{8,9},{9,8},{10,11... | collective-permute-start | bytes 4616 | tf_op jit(solution)/shard_map/ppermute | solution.py:135
  17.5 0.8 pad_maximum_fusion.6
  18.3 0.7 broadcast_in_dim.44
  19.0 3.4 %all-to-all-start = ((bf16[8,2,4096]{2,1,0:T(2,128)(2,1)}), bf16[8,2,4096]{2,1,0:T(2,128)(2,1)S(1)}, u32[]{:S(2)}, u32[]{:S(2)}) async-start(bf16[8,2,4096]{2,1,0:T(2,128)(2,1)} %broadcast_in_dim.44), calls=%async_computation | async-start | bytes 262144 | tf_op jit(solution)/shard_map/all_to_all | solution.py:128
  22.4 1.5 %copy.27.top_idx = s32[128,64]{1,0:T(8,128)} copy(s32[128,64]{0,1:T(8,128)} %param.13) | data formatting | bytes 65536 | tf_op args[3]
  23.8 1.4 %copy.28.top_val = bf16[128,64]{1,0:T(8,128)(2,1)} copy(bf16[128,64]{0,1:T(8,128)(2,1)} %param.14) | data formatting | bytes 32768 | tf_op args[4]
  25.3 0.0 collective-permute-done
  25.3 1.3 pad_add_fusion.1
  26.5 0.7 compare_select_fusion.2
  27.3 0.7 pad_add_fusion.2.place
  27.9 6.1 %sel.1 = bf16[64,1024]{1,0:T(8,128)(2,1)} custom-call(s32[6]{0:T(128)} %pad_add_fusion.2.place, s32[128,64]{1,0:T(8,128)} %copy.27.top_idx, bf16[128,64]{1,0:T(8,128)(2,1)} %copy.28.top_val, s32[128,512]{1,0:T(8,128)} %aux_idx.1, bf16[128,512]{1,0:T(8,128)(2,1)} %aux_val.1, s32[1,512]{1,0:T(1,128)} %bitcast.91), custom_call_target="tpu_custom_call" | custom-call | flops 1342177280 | bytes 1048576 | tf_op jit(solution)/shard_map/sel/pallas_call | solution.py:66
  34.1 0.0 all-to-all-done
  34.1 0.1 copy.31
  34.2 0.0 copy-start
  34.2 0.0 copy-start.2
  34.2 0.0 copy-start.3
  34.2 0.0 copy-start.4
  34.2 0.0 copy-start.5
  34.2 1.1 broadcast_in_dim.49
  35.3 3.6 %all-to-all-start.2 = ((bf16[8,8,2,4096]{3,1,2,0:T(8,128)(2,1)}), bf16[8,8,2,4096]{3,1,2,0:T(8,128)(2,1)S(1)}, u32[]{:S(2)}, u32[]{:S(2)}) async-start(bf16[8,8,2,4096]{3,1,2,0:T(8,128)(2,1)} %broadcast_in_dim.49), calls=%async_computation.2 | async-start | bytes 2097152 | tf_op jit(solution)/shard_map/all_to_all | solution.py:128
  38.9 1.9 %collective-permute-start.3 = (bf16[256,4096]{1,0:T(8,128)(2,1)S(1)}, bf16[256,4096]{1,0:T(8,128)(2,1)}, u32[]{:S(2)}, u32[]{:S(2)}) collective-permute-start(bf16[256,4096]{1,0:T(8,128)(2,1)S(1)} %copy-done), channel_id=1, source_target_pairs={{0,1},{1,0},{2,3},{3,2},{4,5},{5,4},{6,7},{7,6},{8,9},{9,8},{10,11... | collective-permute-start | bytes 6291464 | tf_op jit(solution)/shard_map/ppermute | solution.py:133
  40.8 9.0 %collective-permute-start.1 = (bf16[1,64,1024]{2,1,0:T(8,128)(2,1)S(1)}, bf16[1,64,1024]{2,1,0:T(8,128)(2,1)S(1)}, u32[]{:S(2)}, u32[]{:S(2)}) collective-permute-start(bf16[1,64,1024]{2,1,0:T(8,128)(2,1)S(1)} %bitcast.87), channel_id=1, source_target_pairs={{0,512},{128,640},{256,768},{384,896},{512,0},{640,128},{768,256},... | collective-permute-start | bytes 393224 | tf_op jit(solution)/shard_map/ppermute | solution.py:122
  49.8 0.1 pad_maximum_fusion.5
  50.0 3.7 %collective-permute-done.1 = bf16[1,64,1024]{2,1,0:T(8,128)(2,1)S(1)} collective-permute-done((bf16[1,64,1024]{2,1,0:T(8,128)(2,1)S(1)}, bf16[1,64,1024]{2,1,0:T(8,128)(2,1)S(1)}, u32[]{:S(2)}, u32[]{:S(2)}) %collective-permute-start.1) | collective-permute-done | bytes 131104 | tf_op jit(solution)/shard_map/ppermute | solution.py:122
  53.6 0.7 pad_maximum_fusion.2
  54.4 7.0 %collective-permute-start.2 = (bf16[2,64,1024]{2,1,0:T(8,128)(2,1)}, bf16[2,64,1024]{2,1,0:T(8,128)(2,1)}, u32[]{:S(2)}, u32[]{:S(2)}) collective-permute-start(bf16[2,64,1024]{2,1,0:T(8,128)(2,1)} %pad_maximum_fusion.2), channel_id=1, source_target_pairs={{0,256},{128,384},{256,0},{384,128},{512,768},{640,896},{768,512},... | collective-permute-start | bytes 786440 | tf_op jit(solution)/shard_map/ppermute | solution.py:122
  61.4 0.8 broadcast_in_dim.48
  62.2 12.8 %all-to-all-start.1 = ((bf16[64,4,512]{2,1,0:T(4,128)(2,1)}), bf16[64,4,512]{2,1,0:T(4,128)(2,1)S(1)}, u32[]{:S(2)}, u32[]{:S(2)}) async-start(bf16[64,4,512]{2,1,0:T(4,128)(2,1)} %bitcast.83), calls=%async_computation.1 | async-start | bytes 524288 | tf_op jit(solution)/shard_map/all_to_all | solution.py:128
  74.9 0.1 copy.32
  75.0 0.8 fusion.28
  75.9 0.0 collective-permute-done.3
  75.9 2.4 %fusion.29 = f32[128,256]{1,0:T(8,128)S(1)} fusion(bf16[128,4096]{1,0:T(8,128)(2,1)S(1)} %bitcast.71, bf16[256,4096]{1,0:T(8,128)(2,1)} %collective-permute-done.3), kind=kOutput, calls=%fused_computation.65 | convolution fusion | flops 268435456 | bytes 3276800 | tf_op jit(solution)/shard_map/dot_general | solution.py:85
  78.3 6.9 %collective-permute-start.4 = (bf16[1,64,512]{2,1,0:T(8,128)(2,1)S(1)}, bf16[1,64,512]{2,1,0:T(8,128)(2,1)S(1)}, u32[]{:S(2)}, u32[]{:S(2)}) collective-permute-start(bf16[1,64,512]{2,1,0:T(8,128)(2,1)S(1)} %fusion.22), channel_id=1, source_target_pairs={{0,512},{128,640},{256,768},{384,896},{512,0},{640,128},{768,256},... | collective-permute-start | bytes 196616 | tf_op jit(solution)/shard_map/ppermute | solution.py:122
  85.3 0.0 collective-permute-done.2
  85.3 1.1 pad_maximum_fusion
  86.4 1.1 all-to-all-done.1
  87.5 1.1 collective-permute-done.4
  88.7 0.1 reverse_select_fusion.1
  88.9 0.1 copy.35
  88.9 1.3 broadcast_in_dim.53
  90.2 6.2 %all-to-all-start.3 = ((bf16[8,8,24,512]{3,2,1,0:T(8,128)(2,1)}), bf16[8,8,24,512]{3,2,1,0:T(8,128)(2,1)S(1)}, u32[]{:S(2)}, u32[]{:S(2)}) async-start(bf16[8,8,24,512]{3,2,1,0:T(8,128)(2,1)} %broadcast_in_dim.53), calls=%async_computation.3 | async-start | bytes 3145728 | tf_op jit(solution)/shard_map/all_to_all | solution.py:128
  96.4 2.4 %collective-permute-start.5 = (bf16[4,64,1024]{2,1,0:T(8,128)(2,1)S(1)}, bf16[4,64,1024]{2,1,0:T(8,128)(2,1)S(1)}, u32[]{:S(2)}, u32[]{:S(2)}) collective-permute-start(bf16[4,64,1024]{2,1,0:T(8,128)(2,1)S(1)} %pad_maximum_fusion), channel_id=1, source_target_pairs={{0,128},{128,0},{256,384},{384,256},{512,640},{640,512},{768,896},... | collective-permute-start | bytes 1572872 | tf_op jit(solution)/shard_map/ppermute | solution.py:122
  98.8 4.0 %collective-permute-start.6 = (bf16[2,64,512]{2,1,0:T(8,128)(2,1)S(1)}, bf16[2,64,512]{2,1,0:T(8,128)(2,1)S(1)}, u32[]{:S(2)}, u32[]{:S(2)}) collective-permute-start(bf16[2,64,512]{2,1,0:T(8,128)(2,1)S(1)} %pad_maximum_fusion.4), channel_id=1, source_target_pairs={{0,256},{128,384},{256,0},{384,128},{512,768},{640,896},{768,512},... | collective-permute-start | bytes 393224 | tf_op jit(solution)/shard_map/ppermute | solution.py:122
  102.8 2.9 %collective-permute-start.7 = (bf16[2,64,512]{2,1,0:T(8,128)(2,1)S(1)}, bf16[2,64,512]{2,1,0:T(8,128)(2,1)S(1)}, u32[]{:S(2)}, u32[]{:S(2)}) collective-permute-start(bf16[2,64,512]{2,1,0:T(8,128)(2,1)S(1)} %pad_maximum_fusion.4), channel_id=1, source_target_pairs={{0,128},{128,0},{256,384},{384,256},{512,640},{640,512},{768,896},... | collective-permute-start | bytes 393224 | tf_op jit(solution)/shard_map/ppermute | solution.py:122
  105.8 2.3 %collective-permute-start.8 = (bf16[2,64,512]{2,1,0:T(8,128)(2,1)S(1)}, bf16[2,64,512]{2,1,0:T(8,128)(2,1)S(1)}, u32[]{:S(2)}, u32[]{:S(2)}) collective-permute-start(bf16[2,64,512]{2,1,0:T(8,128)(2,1)S(1)} %pad_maximum_fusion.4), channel_id=1, source_target_pairs={{0,384},{128,256},{256,128},{384,0},{512,896},{640,768},{768,640},... | collective-permute-start | bytes 393224 | tf_op jit(solution)/shard_map/ppermute | solution.py:122
  108.1 1.5 %collective-permute-done.6 = bf16[2,64,512]{2,1,0:T(8,128)(2,1)S(1)} collective-permute-done((bf16[2,64,512]{2,1,0:T(8,128)(2,1)S(1)}, bf16[2,64,512]{2,1,0:T(8,128)(2,1)S(1)}, u32[]{:S(2)}, u32[]{:S(2)}) %collective-permute-start.6) | collective-permute-done | bytes 131104 | tf_op jit(solution)/shard_map/ppermute | solution.py:122
  109.6 5.4 %collective-permute-done.7 = bf16[2,64,512]{2,1,0:T(8,128)(2,1)S(1)} collective-permute-done((bf16[2,64,512]{2,1,0:T(8,128)(2,1)S(1)}, bf16[2,64,512]{2,1,0:T(8,128)(2,1)S(1)}, u32[]{:S(2)}, u32[]{:S(2)}) %collective-permute-start.7) | collective-permute-done | bytes 131104 | tf_op jit(solution)/shard_map/ppermute | solution.py:122
  115.0 4.2 %collective-permute-done.8 = bf16[2,64,512]{2,1,0:T(8,128)(2,1)S(1)} collective-permute-done((bf16[2,64,512]{2,1,0:T(8,128)(2,1)S(1)}, bf16[2,64,512]{2,1,0:T(8,128)(2,1)S(1)}, u32[]{:S(2)}, u32[]{:S(2)}) %collective-permute-start.8) | collective-permute-done | bytes 131104 | tf_op jit(solution)/shard_map/ppermute | solution.py:122
  119.2 0.1 maximum_bitcast_fusion.1
  119.3 1.1 copy.42
  120.4 0.1 maximum_bitcast_fusion
  120.5 0.6 copy.41
  121.1 0.3 fusion.7
  121.4 0.3 fusion.2
  121.8 0.4 copy-done.1
  122.1 0.3 fusion.1
  122.5 0.1 pad_maximum_fusion.1
  122.5 5.6 %collective-permute-start.9 = (bf16[2,256,512]{2,1,0:T(8,128)(2,1)S(1)}, bf16[2,256,512]{2,1,0:T(8,128)(2,1)S(1)}, u32[]{:S(2)}, u32[]{:S(2)}) collective-permute-start(bf16[2,256,512]{2,1,0:T(8,128)(2,1)S(1)} %pad_maximum_fusion.1), channel_id=1, source_target_pairs={{0,1},{1,0},{2,3},{3,2},{4,5},{5,4},{6,7},{7,6},{8,9},{9,8},{10,11... | collective-permute-start | bytes 1572872 | tf_op jit(solution)/shard_map/ppermute | solution.py:179
  128.1 0.3 fusion.8
  128.4 1.2 collective-permute-done.9
  129.6 0.1 convert_element_type.14
  129.8 1.0 fusion.4
  130.8 1.0 fusion.6
  (21 shorter events, 0.3 us)
Async XLA Ops:
  1.4 23.9 %collective-permute-start = (s32[384]{0:T(512)S(1)}, s32[384]{0:T(512)S(1)}, u32[]{:S(2)}, u32[]{:S(2)}) collective-permute-start(s32[384]{0:T(512)S(1)} %pad_add_fusion), channel_id=1, source_target_pairs={{0,1},{1,0},{2,3},{3,2},{4,5},{5,4},{6,7},{7,6},{8,9},{9,8},{10,11... | collective-permute-start | bytes 4616 | tf_op jit(solution)/shard_map/ppermute | solution.py:135
  19.0 15.1 %all-to-all-start = ((bf16[8,2,4096]{2,1,0:T(2,128)(2,1)}), bf16[8,2,4096]{2,1,0:T(2,128)(2,1)S(1)}, u32[]{:S(2)}, u32[]{:S(2)}) async-start(bf16[8,2,4096]{2,1,0:T(2,128)(2,1)} %broadcast_in_dim.44), calls=%async_computation | async-start | bytes 262144 | tf_op jit(solution)/shard_map/all_to_all | solution.py:128
  34.2 4.7 %copy-start = (bf16[256,4096]{1,0:T(8,128)(2,1)S(1)}, bf16[256,4096]{1,0:T(8,128)(2,1)}, u32[]{:S(2)}) copy-start(bf16[256,4096]{1,0:T(8,128)(2,1)} %param.19) | copy-start | bytes 6291460
  34.2 6.6 %copy-start.2 = (bf16[64,1024]{1,0:T(8,128)(2,1)S(1)}, bf16[64,1024]{1,0:T(8,128)(2,1)}, u32[]{:S(2)}) copy-start(bf16[64,1024]{1,0:T(8,128)(2,1)} %sel.1) | copy-start | bytes 393220
  34.2 15.6 %copy-start.3 = (bf16[1,4096]{1,0:T(2,128)(2,1)S(1)}, bf16[1,4096]{1,0:T(2,128)(2,1)}, u32[]{:S(2)}) copy-start(bf16[1,4096]{1,0:T(2,128)(2,1)} %param.11) | copy-start | bytes 24580
  34.2 15.6 %copy-start.4 = (bf16[1,4096]{1,0:T(2,128)(2,1)S(1)}, bf16[1,4096]{1,0:T(2,128)(2,1)}, u32[]{:S(2)}) copy-start(bf16[1,4096]{1,0:T(2,128)(2,1)} %param.10) | copy-start | bytes 24580
  34.2 15.6 %copy-start.5 = (bf16[1,4096]{1,0:T(2,128)(2,1)S(1)}, bf16[1,4096]{1,0:T(2,128)(2,1)}, u32[]{:S(2)}) copy-start(bf16[1,4096]{1,0:T(2,128)(2,1)} %param.12) | copy-start | bytes 24580
  35.3 26.1 %all-to-all-start.2 = ((bf16[8,8,2,4096]{3,1,2,0:T(8,128)(2,1)}), bf16[8,8,2,4096]{3,1,2,0:T(8,128)(2,1)S(1)}, u32[]{:S(2)}, u32[]{:S(2)}) async-start(bf16[8,8,2,4096]{3,1,2,0:T(8,128)(2,1)} %broadcast_in_dim.49), calls=%async_computation.2 | async-start | bytes 2097152 | tf_op jit(solution)/shard_map/all_to_all | solution.py:128
  38.9 37.0 %collective-permute-start.3 = (bf16[256,4096]{1,0:T(8,128)(2,1)S(1)}, bf16[256,4096]{1,0:T(8,128)(2,1)}, u32[]{:S(2)}, u32[]{:S(2)}) collective-permute-start(bf16[256,4096]{1,0:T(8,128)(2,1)S(1)} %copy-done), channel_id=1, source_target_pairs={{0,1},{1,0},{2,3},{3,2},{4,5},{5,4},{6,7},{7,6},{8,9},{9,8},{10,11... | collective-permute-start | bytes 6291464 | tf_op jit(solution)/shard_map/ppermute | solution.py:133
  40.8 12.8 %collective-permute-start.1 = (bf16[1,64,1024]{2,1,0:T(8,128)(2,1)S(1)}, bf16[1,64,1024]{2,1,0:T(8,128)(2,1)S(1)}, u32[]{:S(2)}, u32[]{:S(2)}) collective-permute-start(bf16[1,64,1024]{2,1,0:T(8,128)(2,1)S(1)} %bitcast.87), channel_id=1, source_target_pairs={{0,512},{128,640},{256,768},{384,896},{512,0},{640,128},{768,256},... | collective-permute-start | bytes 393224 | tf_op jit(solution)/shard_map/ppermute | solution.py:122
  54.4 30.9 %collective-permute-start.2 = (bf16[2,64,1024]{2,1,0:T(8,128)(2,1)}, bf16[2,64,1024]{2,1,0:T(8,128)(2,1)}, u32[]{:S(2)}, u32[]{:S(2)}) collective-permute-start(bf16[2,64,1024]{2,1,0:T(8,128)(2,1)} %pad_maximum_fusion.2), channel_id=1, source_target_pairs={{0,256},{128,384},{256,0},{384,128},{512,768},{640,896},{768,512},... | collective-permute-start | bytes 786440 | tf_op jit(solution)/shard_map/ppermute | solution.py:122
  62.2 25.3 %all-to-all-start.1 = ((bf16[64,4,512]{2,1,0:T(4,128)(2,1)}), bf16[64,4,512]{2,1,0:T(4,128)(2,1)S(1)}, u32[]{:S(2)}, u32[]{:S(2)}) async-start(bf16[64,4,512]{2,1,0:T(4,128)(2,1)} %bitcast.83), calls=%async_computation.1 | async-start | bytes 524288 | tf_op jit(solution)/shard_map/all_to_all | solution.py:128
  78.3 10.3 %collective-permute-start.4 = (bf16[1,64,512]{2,1,0:T(8,128)(2,1)S(1)}, bf16[1,64,512]{2,1,0:T(8,128)(2,1)S(1)}, u32[]{:S(2)}, u32[]{:S(2)}) collective-permute-start(bf16[1,64,512]{2,1,0:T(8,128)(2,1)S(1)} %fusion.22), channel_id=1, source_target_pairs={{0,512},{128,640},{256,768},{384,896},{512,0},{640,128},{768,256},... | collective-permute-start | bytes 196616 | tf_op jit(solution)/shard_map/ppermute | solution.py:122
  90.2 30.9 %all-to-all-start.3 = ((bf16[8,8,24,512]{3,2,1,0:T(8,128)(2,1)}), bf16[8,8,24,512]{3,2,1,0:T(8,128)(2,1)S(1)}, u32[]{:S(2)}, u32[]{:S(2)}) async-start(bf16[8,8,24,512]{3,2,1,0:T(8,128)(2,1)} %broadcast_in_dim.53), calls=%async_computation.3 | async-start | bytes 3145728 | tf_op jit(solution)/shard_map/all_to_all | solution.py:128
  96.4 24.0 %collective-permute-start.5 = (bf16[4,64,1024]{2,1,0:T(8,128)(2,1)S(1)}, bf16[4,64,1024]{2,1,0:T(8,128)(2,1)S(1)}, u32[]{:S(2)}, u32[]{:S(2)}) collective-permute-start(bf16[4,64,1024]{2,1,0:T(8,128)(2,1)S(1)} %pad_maximum_fusion), channel_id=1, source_target_pairs={{0,128},{128,0},{256,384},{384,256},{512,640},{640,512},{768,896},... | collective-permute-start | bytes 1572872 | tf_op jit(solution)/shard_map/ppermute | solution.py:122
  98.8 10.8 %collective-permute-start.6 = (bf16[2,64,512]{2,1,0:T(8,128)(2,1)S(1)}, bf16[2,64,512]{2,1,0:T(8,128)(2,1)S(1)}, u32[]{:S(2)}, u32[]{:S(2)}) collective-permute-start(bf16[2,64,512]{2,1,0:T(8,128)(2,1)S(1)} %pad_maximum_fusion.4), channel_id=1, source_target_pairs={{0,256},{128,384},{256,0},{384,128},{512,768},{640,896},{768,512},... | collective-permute-start | bytes 393224 | tf_op jit(solution)/shard_map/ppermute | solution.py:122
  102.8 12.2 %collective-permute-start.7 = (bf16[2,64,512]{2,1,0:T(8,128)(2,1)S(1)}, bf16[2,64,512]{2,1,0:T(8,128)(2,1)S(1)}, u32[]{:S(2)}, u32[]{:S(2)}) collective-permute-start(bf16[2,64,512]{2,1,0:T(8,128)(2,1)S(1)} %pad_maximum_fusion.4), channel_id=1, source_target_pairs={{0,128},{128,0},{256,384},{384,256},{512,640},{640,512},{768,896},... | collective-permute-start | bytes 393224 | tf_op jit(solution)/shard_map/ppermute | solution.py:122
  105.8 13.5 %collective-permute-start.8 = (bf16[2,64,512]{2,1,0:T(8,128)(2,1)S(1)}, bf16[2,64,512]{2,1,0:T(8,128)(2,1)S(1)}, u32[]{:S(2)}, u32[]{:S(2)}) collective-permute-start(bf16[2,64,512]{2,1,0:T(8,128)(2,1)S(1)} %pad_maximum_fusion.4), channel_id=1, source_target_pairs={{0,384},{128,256},{256,128},{384,0},{512,896},{640,768},{768,640},... | collective-permute-start | bytes 393224 | tf_op jit(solution)/shard_map/ppermute | solution.py:122
  121.1 1.0 copy-start.1
  122.5 7.1 %collective-permute-start.9 = (bf16[2,256,512]{2,1,0:T(8,128)(2,1)S(1)}, bf16[2,256,512]{2,1,0:T(8,128)(2,1)S(1)}, u32[]{:S(2)}, u32[]{:S(2)}) collective-permute-start(bf16[2,256,512]{2,1,0:T(8,128)(2,1)S(1)} %pad_maximum_fusion.1), channel_id=1, source_target_pairs={{0,1},{1,0},{2,3},{3,2},{4,5},{5,4},{6,7},{7,6},{8,9},{9,8},{10,11... | collective-permute-start | bytes 1572872 | tf_op jit(solution)/shard_map/ppermute | solution.py:179

commit v4 on v3

--- a/solution.py
+++ b/solution.py
@@ -11,10 +11,11 @@
 BLOCK = 128
 
 
-def sel_kernel(place, top_idx, top_val, aux_idx, aux_val, dead, out, high, low, val, found):
-    rows, n_top = top_idx.shape
+def sel_kernel(place, top_idx, top_val, aux_idx, aux_val, cores, out, high, low, val, found):
+    n_top, rows = top_idx.shape
     n_aux = aux_idx.shape[1]
-    slots = dead.shape[1]
+    slots = out.shape[1] // 2
+    width = slots // 2
     side = math.isqrt(rows // 2)
     tables = 2 * slots // 128
     core = place[0]
@@ -23,16 +24,20 @@
         to = pl.ds(at, col.shape[1])
         high[:, to] = col >> 7
         low[:, to] = col & 127
-        val[:, to] = v[...].astype(jnp.float32)
+        val[:, to] = v
 
     col = aux_idx[...] - place[1] * slots
     inside = (col >= 0) & (col < slots)
-    put(0, jnp.where(inside, slots + ((col + core * (slots // 2)) & (slots - 1)), -1), aux_val)
+    put(0, jnp.where(inside, slots + ((col + core * width) & (slots - 1)), -1), aux_val[...].astype(jnp.float32))
     block, inside = top_idx[...] >> 7, top_idx[...] & (BLOCK - 1)
     col = jnp.full(top_idx.shape, -1, jnp.int32)
     for m in range(slots // BLOCK):
-        col = jnp.where(block == place[2 + m], m * BLOCK + inside, col)
-    put(n_aux, col, top_val)
+        other, at = divmod(m, width // BLOCK)
+        shard = 2 * place[1] + (core if other == 0 else 1 - core)
+        number = cores[other : other + 1, width + at : width + at + 1]
+        here = (block == number + shard * (LAT_DEV // BLOCK)) & (number >= 0)
+        col = jnp.where(here, m * BLOCK + inside, col)
+    put(n_aux, col.T, top_val[...].astype(jnp.float32).T)
 
     n = n_aux + n_top
     row_high = lax.broadcasted_iota(jnp.int32, (tables, n), 0)
@@ -54,14 +59,14 @@
     for k in range(tables):
         table = found[side * side * k : side * side * (k + 1), :]
         if 128 * k >= slots:
-            table = table * dead[:, 128 * k - slots : 128 * (k + 1) - slots].astype(jnp.float32)
+            other, at = divmod(128 * k - slots, width)
+            table = table * cores[other : other + 1, at : at + 128].astype(jnp.float32)
         out[:, 128 * k : 128 * (k + 1)] = table.astype(out.dtype)
 
 
-def make_sel(place, top_idx, top_val, aux_idx, aux_val, dead):
-    rows, n_top = top_idx.shape
+def make_sel(place, top_idx, top_val, aux_idx, aux_val, cores, slots):
+    rows = aux_idx.shape[0]
     entries = aux_idx.shape[1] + 128
-    slots = dead.shape[1]
     whole = pl.BlockSpec(memory_space=pltpu.VMEM)
     return pl.pallas_call(
         sel_kernel,
@@ -78,7 +83,7 @@
             flops=rows * entries * slots * 32, bytes_accessed=1 << 20, transcendentals=0
         ),
         name="sel",
-    )(place, top_idx, top_val, aux_idx, aux_val, dead)
+    )(place, top_idx.T, top_val.T, aux_idx, aux_val, cores)
 
 
 def rows_dot(left, right):
@@ -99,10 +104,10 @@
         return ((z * side + y) * side + x) * n_in + c
 
     ranks, dps, cores = range(side), range(n_dp), range(n_in)
-    first = [[device(z, a, b, c) for b in ranks] for z in dps for a in ranks for c in cores]
+    plane = [[device(z, a, b, c) for a in ranks for b in ranks] for z in dps for c in cores]
     wide = [[device(z, a, b, c) for z in dps for b in ranks] for a in ranks for c in cores]
     second = [[device(z, a, b, c) for a in ranks] for z in dps for b in ranks for c in cores]
-    return first, wide, second
+    return plane, wide, second
 
 
 def local(
@@ -116,7 +121,7 @@
     lat = lax.axis_index("lat")
     core = lax.axis_index("inner")
     swap = [(i, (i + 1) % n_in) for i in range(n_in)]
-    first, wide, second = plane_groups(n_dp, side, n_in)
+    plane, wide, second = plane_groups(n_dp, side, n_in)
 
     def send(v, step):
         return lax.ppermute(v, "dp", [(i, i ^ step) for i in range(n_dp)])
@@ -133,16 +138,12 @@
     dec_other = lax.ppermute(dec_rows, "inner", swap)
     small = jnp.concatenate([dead, blocks, jnp.zeros((128 - blocks.shape[0],), jnp.int32)])
     small_other = lax.ppermute(small, "inner", swap)
-    dead_all = jnp.concatenate([dead, small_other[:width]])[None]
-    table = jnp.concatenate([blocks, small_other[width : width + blocks.shape[0]]])
-    owner = lat * n_in + (core + jnp.arange(table.shape[0], dtype=jnp.int32) // blocks.shape[0]) % n_in
-    keys = jnp.where(table >= 0, owner * (LAT_DEV // BLOCK) + table, -1)
-    place = jnp.concatenate([jnp.stack([core, lat]), keys])
-    sel = make_sel(place, top_idx, top_val, aux_idx, aux_val, dead_all)
+    cores = jnp.stack([small, small_other])
+    place = jnp.stack([core, lat])
+    sel = make_sel(place, top_idx, top_val, aux_idx, aux_val, cores, slots)
 
-    near = spread(jnp.concatenate([err_main, err_aux], axis=0), first)
-    near, sel = lax.optimization_barrier((near, sel))
-    full = spread(near, second)
+    full = jnp.concatenate([err_main, err_aux], axis=0)
+    full = exchange(jnp.broadcast_to(full[None], (n_lat,) + full.shape), plane)
     sel_all = grow(sel[None], 4)
 
     both = full.reshape(n_lat, 2, d).transpose(1, 0, 2).reshape(2 * n_lat, d)
@@ -176,9 +177,9 @@
         return dec_term, cols_dot(pick(dpre_all, 0), res)
 
     sent = jnp.stack(half(1)).astype(jnp.bfloat16)
-    got = lax.ppermute(sent, "inner", swap).astype(jnp.float32)
-    dec_term, enc_term = half(0)
-    return ((dec_term + got[0]).astype(jnp.bfloat16), (enc_term + got[1]).astype(jnp.bfloat16))
+    got = lax.ppermute(sent, "inner", swap)
+    kept = lax.optimization_barrier(half(0))
+    return tuple((kept[i] + got[i].astype(jnp.float32)).astype(jnp.bfloat16) for i in range(2))
 
 
 def solution(mesh):

time: 133 us -> 127 us (0.955)
  local copies, waits for them, and re-layouts: 9.18 us -> 5.74 us
  matrix products: 6.62 us -> 5.22 us
    ppermute x1, starting transfers between devices: 16.1 us -> 1.91 us  [local(): small_other = lax.ppermute(small, 'inner', swap)]
    all_to_all x4 -> x3, starting transfers between devices: 25.8 us -> 32.2 us  [exchange(): lax.all_to_all(v, ('dp', 'lat', 'inner'), 0, 0, axis_index_groups=groups,...]
    ppermute x1, starting transfers between devices: 1.92 us -> 6.68 us  [local(): dec_other = lax.ppermute(dec_rows, 'inner', swap)]
    unnamed x15, local copies, waits for them, and re-layouts: 3.3 us -> 0.05 us
    ppermute x7, starting transfers between devices: 34.5 us -> 36.7 us  [send(): return lax.ppermute(v, 'dp', [(i, i ^ step) for i in range(n_dp)])]
    broadcast_in_dim x0 -> x1, local copies, waits for them, and re-layouts: none -> 1.99 us  [local(): full = exchange(jnp.broadcast_to(full[None], (n_lat,) + full.shape), plane)]
    concatenate x3 -> x1, other arithmetic: 2.71 us -> 0.78 us  [local(): full = jnp.concatenate([err_main, err_aux], axis=0)]
    broadcast_in_dim x4 -> x2, local copies, waits for them, and re-layouts: 3.17 us -> 1.36 us  [spread(): return exchange(jnp.broadcast_to(v[None], (side,) + v.shape), groups)]
  transfers between devices with their start and end apart: 14 -> 13, of which waited for: 7 -> 8; matrix products, arithmetic and copies ran while one was open for 12% -> 8% of each run, Pallas kernels for 5% -> 5%
where the time goes in v4:
time: 127 us; the launch traced here: 126 us
  starting transfers between devices  83.1 us (65%)
  waiting for transfers between devices  18.4 us (14%)
  Pallas kernels  6.32 us (5%)
  other arithmetic  6.16 us (5%)
  local copies, waits for them, and re-layouts  5.74 us (5%)
  matrix products  5.22 us (4%)
    ppermute x7, starting transfers between devices, send(): return lax.ppermute(v, 'dp', [(i, i ^ step) for i in range(n_dp)])  36.7 us
    all_to_all x3, starting transfers between devices, exchange(): lax.all_to_all(v, ('dp', 'lat', 'inner'), 0, 0, axis_index_groups=groups,...  32.2 us
    ppermute x7, waiting for transfers between devices, send(): return lax.ppermute(v, 'dp', [(i, i ^ step) for i in range(n_dp)])  15.8 us
    ppermute x1, starting transfers between devices, local(): dec_other = lax.ppermute(dec_rows, 'inner', swap)  6.68 us
    pallas_call x1, Pallas kernels, make_sel(): pl.pallas_call(sel_kernel, in_specs=[pl.BlockSpec(memory_space=pltpu.SMEM...  6.32 us
    ppermute x1, starting transfers between devices, local(): got = lax.ppermute(sent, 'inner', swap)  5.64 us
    dot_general x2, matrix products, rows_dot(): lax.dot_general(left, right, (((1,), (1,)), ((), ())), preferred_element_...  3.29 us
    concatenate x3, other arithmetic, grow(): return jnp.concatenate([v, send(v, step)], axis=0)  2.72 us
  transfers between devices with their start and end apart: 13, of which 8 were waited for; matrix products, arithmetic and copies ran while one was open for 8% of the time, Pallas kernels for 5%

profile of v4, /device:TPU:1, one launch (start us, length us, event | category | flops | bytes accessed | tf_op | source)
XLA Modules:
  0.0 126.0 jit_solution(8109573871004320373)
XLA Ops:
  0.6 0.8 pad_maximum_fusion.6
  1.4 0.0 copy-start
  1.4 0.0 copy-start.5
  1.4 0.0 copy-start.6
  1.4 2.0 %broadcast_in_dim.36 = bf16[64,2,4096]{2,1,0:T(2,128)(2,1)} broadcast(bf16[2,4096]{1,0:T(2,128)(2,1)S(1)} %pad_maximum_fusion.6), dimensions={1,2} | broadcast | bytes 1064960 | tf_op jit(solution)/shard_map/broadcast_in_dim | solution.py:146
  3.4 14.0 %all-to-all-start.1 = ((bf16[64,2,4096]{2,1,0:T(2,128)(2,1)}), bf16[64,2,4096]{2,1,0:T(2,128)(2,1)S(1)}, u32[]{:S(2)}, u32[]{:S(2)}) async-start(bf16[64,2,4096]{2,1,0:T(2,128)(2,1)} %broadcast_in_dim.36), calls=%async_computation.1 | async-start | bytes 2097152 | tf_op jit(solution)/shard_map/all_to_all | solution.py:133
  17.5 6.7 %collective-permute-start.3 = (bf16[256,4096]{1,0:T(8,128)(2,1)S(1)}, bf16[256,4096]{1,0:T(8,128)(2,1)}, u32[]{:S(2)}, u32[]{:S(2)}) collective-permute-start(bf16[256,4096]{1,0:T(8,128)(2,1)S(1)} %copy-done), channel_id=1, source_target_pairs={{0,1},{1,0},{2,3},{3,2},{4,5},{5,4},{6,7},{7,6},{8,9},{9,8},{10,11... | collective-permute-start | bytes 6291464 | tf_op jit(solution)/shard_map/ppermute | solution.py:138
  24.2 0.0 copy-done.5
  24.2 0.0 copy-done.6
  24.2 0.1 pad_add_fusion.1
  24.3 1.9 %collective-permute-start = (s32[384]{0:T(512)S(1)}, s32[384]{0:T(512)S(1)}, u32[]{:S(2)}, u32[]{:S(2)}) collective-permute-start(s32[384]{0:T(512)S(1)} %pad_add_fusion.1), channel_id=1, source_target_pairs={{0,1},{1,0},{2,3},{3,2},{4,5},{5,4},{6,7},{7,6},{8,9},{9,8},{10,11... | collective-permute-start | bytes 4616 | tf_op jit(solution)/shard_map/ppermute | solution.py:140
  26.2 0.6 pad_add_fusion.2.place
  26.8 1.2 collective-permute-done
  28.0 0.6 pad_add_fusion.cores
  28.5 6.3 %sel.1 = bf16[64,1024]{1,0:T(8,128)(2,1)} custom-call(s32[2]{0:T(128)} %pad_add_fusion.2.place, s32[64,128]{1,0:T(8,128)} %bitcast.84, bf16[64,128]{1,0:T(8,128)(2,1)} %bitcast.85, s32[128,512]{1,0:T(8,128)} %aux_idx.1, bf16[128,512]{1,0:T(8,128)(2,1)} %aux_val.1, s32[2,384]{1,0:T(2,128)} %pad_add_fusion.cores), custom_call_target="tpu_custom_call" | custom-call | flops 1342177280 | bytes 1048576 | tf_op jit(solution)/shard_map/sel/pallas_call | solution.py:71
  34.9 10.4 %collective-permute-start.1 = (bf16[1,64,1024]{2,1,0:T(8,128)(2,1)}, bf16[1,64,1024]{2,1,0:T(8,128)(2,1)S(1)}, u32[]{:S(2)}, u32[]{:S(2)}) collective-permute-start(bf16[1,64,1024]{2,1,0:T(8,128)(2,1)} %bitcast.80), channel_id=1, source_target_pairs={{0,512},{128,640},{256,768},{384,896},{512,0},{640,128},{768,256},... | collective-permute-start | bytes 393224 | tf_op jit(solution)/shard_map/ppermute | solution.py:127
  45.3 0.0 copy-done.2
  45.3 0.0 copy-done.3
  45.3 0.0 copy-done.4
  45.4 0.1 pad_maximum_fusion.5
  45.5 3.6 %collective-permute-done.1 = bf16[1,64,1024]{2,1,0:T(8,128)(2,1)S(1)} collective-permute-done((bf16[1,64,1024]{2,1,0:T(8,128)(2,1)}, bf16[1,64,1024]{2,1,0:T(8,128)(2,1)S(1)}, u32[]{:S(2)}, u32[]{:S(2)}) %collective-permute-start.1) | collective-permute-done | bytes 131104 | tf_op jit(solution)/shard_map/ppermute | solution.py:127
  49.1 1.6 %pad_maximum_fusion.2 = bf16[2,64,1024]{2,1,0:T(8,128)(2,1)} fusion(bf16[1,64,1024]{2,1,0:T(8,128)(2,1)S(1)} %collective-permute-done.1, bf16[1,64,1024]{2,1,0:T(8,128)(2,1)} %bitcast.81), kind=kLoop, calls=%fused_computation.32 | loop fusion | flops 131072 | bytes 524288 | tf_op jit(solution)/shard_map/concatenate | solution.py:130
  50.7 7.2 %collective-permute-start.2 = (bf16[2,64,1024]{2,1,0:T(8,128)(2,1)}, bf16[2,64,1024]{2,1,0:T(8,128)(2,1)}, u32[]{:S(2)}, u32[]{:S(2)}) collective-permute-start(bf16[2,64,1024]{2,1,0:T(8,128)(2,1)} %pad_maximum_fusion.2), channel_id=1, source_target_pairs={{0,256},{128,384},{256,0},{384,128},{512,768},{640,896},{768,512},... | collective-permute-start | bytes 786440 | tf_op jit(solution)/shard_map/ppermute | solution.py:127
  58.0 0.0 all-to-all-done.1
  58.0 0.8 broadcast_in_dim.35
  58.8 12.5 %all-to-all-start = ((bf16[64,4,512]{2,1,0:T(4,128)(2,1)}), bf16[64,4,512]{2,1,0:T(4,128)(2,1)S(1)}, u32[]{:S(2)}, u32[]{:S(2)}) async-start(bf16[64,4,512]{2,1,0:T(4,128)(2,1)} %bitcast.78), calls=%async_computation | async-start | bytes 524288 | tf_op jit(solution)/shard_map/all_to_all | solution.py:133
  71.2 0.6 copy.23
  71.8 0.8 fusion.21
  72.7 0.0 copy-start.1
  72.7 0.0 collective-permute-done.3
  72.7 2.5 %fusion.22 = f32[128,256]{1,0:T(8,128)S(1)} fusion(bf16[128,4096]{1,0:T(8,128)(2,1)S(1)} %bitcast.70, bf16[256,4096]{1,0:T(8,128)(2,1)} %collective-permute-done.3), kind=kOutput, calls=%fused_computation.52 | convolution fusion | flops 268435456 | bytes 3276800 | tf_op jit(solution)/shard_map/dot_general | solution.py:90
  75.2 0.0 copy-done.1
  75.2 6.9 %collective-permute-start.4 = (bf16[1,64,512]{2,1,0:T(8,128)(2,1)S(1)}, bf16[1,64,512]{2,1,0:T(8,128)(2,1)S(1)}, u32[]{:S(2)}, u32[]{:S(2)}) collective-permute-start(bf16[1,64,512]{2,1,0:T(8,128)(2,1)S(1)} %fusion.20), channel_id=1, source_target_pairs={{0,512},{128,640},{256,768},{384,896},{512,0},{640,128},{768,256},... | collective-permute-start | bytes 196616 | tf_op jit(solution)/shard_map/ppermute | solution.py:127
  82.1 0.0 collective-permute-done.2
  82.1 1.1 pad_maximum_fusion
  83.2 0.6 all-to-all-done
  83.9 1.1 collective-permute-done.4
  85.0 0.1 reverse_select_fusion.1
  85.2 0.1 copy.26
  85.3 1.3 %broadcast_in_dim.40 = bf16[8,8,24,512]{3,2,1,0:T(8,128)(2,1)} broadcast(bf16[8,24,512]{2,1,0:T(8,128)(2,1)S(1)} %copy.26), dimensions={1,2,3} | broadcast | bytes 1769472 | tf_op jit(solution)/shard_map/broadcast_in_dim | solution.py:136
  86.6 5.7 %all-to-all-start.2 = ((bf16[8,8,24,512]{3,2,1,0:T(8,128)(2,1)}), bf16[8,8,24,512]{3,2,1,0:T(8,128)(2,1)S(1)}, u32[]{:S(2)}, u32[]{:S(2)}) async-start(bf16[8,8,24,512]{3,2,1,0:T(8,128)(2,1)} %broadcast_in_dim.40), calls=%async_computation.2 | async-start | bytes 3145728 | tf_op jit(solution)/shard_map/all_to_all | solution.py:133
  92.3 2.8 %collective-permute-start.5 = (bf16[4,64,1024]{2,1,0:T(8,128)(2,1)S(1)}, bf16[4,64,1024]{2,1,0:T(8,128)(2,1)S(1)}, u32[]{:S(2)}, u32[]{:S(2)}) collective-permute-start(bf16[4,64,1024]{2,1,0:T(8,128)(2,1)S(1)} %pad_maximum_fusion), channel_id=1, source_target_pairs={{0,128},{128,0},{256,384},{384,256},{512,640},{640,512},{768,896},... | collective-permute-start | bytes 1572872 | tf_op jit(solution)/shard_map/ppermute | solution.py:127
  95.1 4.0 %collective-permute-start.6 = (bf16[2,64,512]{2,1,0:T(8,128)(2,1)S(1)}, bf16[2,64,512]{2,1,0:T(8,128)(2,1)S(1)}, u32[]{:S(2)}, u32[]{:S(2)}) collective-permute-start(bf16[2,64,512]{2,1,0:T(8,128)(2,1)S(1)} %pad_maximum_fusion.4), channel_id=1, source_target_pairs={{0,256},{128,384},{256,0},{384,128},{512,768},{640,896},{768,512},... | collective-permute-start | bytes 393224 | tf_op jit(solution)/shard_map/ppermute | solution.py:127
  99.2 2.8 %collective-permute-start.7 = (bf16[2,64,512]{2,1,0:T(8,128)(2,1)S(1)}, bf16[2,64,512]{2,1,0:T(8,128)(2,1)S(1)}, u32[]{:S(2)}, u32[]{:S(2)}) collective-permute-start(bf16[2,64,512]{2,1,0:T(8,128)(2,1)S(1)} %pad_maximum_fusion.4), channel_id=1, source_target_pairs={{0,128},{128,0},{256,384},{384,256},{512,640},{640,512},{768,896},... | collective-permute-start | bytes 393224 | tf_op jit(solution)/shard_map/ppermute | solution.py:127
  102.0 2.4 %collective-permute-start.8 = (bf16[2,64,512]{2,1,0:T(8,128)(2,1)S(1)}, bf16[2,64,512]{2,1,0:T(8,128)(2,1)S(1)}, u32[]{:S(2)}, u32[]{:S(2)}) collective-permute-start(bf16[2,64,512]{2,1,0:T(8,128)(2,1)S(1)} %pad_maximum_fusion.4), channel_id=1, source_target_pairs={{0,384},{128,256},{256,128},{384,0},{512,896},{640,768},{768,640},... | collective-permute-start | bytes 393224 | tf_op jit(solution)/shard_map/ppermute | solution.py:127
  104.4 1.2 collective-permute-done.6
  105.6 4.9 %collective-permute-done.7 = bf16[2,64,512]{2,1,0:T(8,128)(2,1)S(1)} collective-permute-done((bf16[2,64,512]{2,1,0:T(8,128)(2,1)S(1)}, bf16[2,64,512]{2,1,0:T(8,128)(2,1)S(1)}, u32[]{:S(2)}, u32[]{:S(2)}) %collective-permute-start.7) | collective-permute-done | bytes 131104 | tf_op jit(solution)/shard_map/ppermute | solution.py:127
  110.5 5.0 %collective-permute-done.8 = bf16[2,64,512]{2,1,0:T(8,128)(2,1)S(1)} collective-permute-done((bf16[2,64,512]{2,1,0:T(8,128)(2,1)S(1)}, bf16[2,64,512]{2,1,0:T(8,128)(2,1)S(1)}, u32[]{:S(2)}, u32[]{:S(2)}) %collective-permute-start.8) | collective-permute-done | bytes 131104 | tf_op jit(solution)/shard_map/ppermute | solution.py:127
  115.4 0.1 maximum_bitcast_fusion.1
  115.5 0.3 copy.33
  115.8 0.0 collective-permute-done.5
  115.8 0.1 maximum_bitcast_fusion
  115.9 0.6 copy.32
  116.5 0.0 all-to-all-done.2
  116.5 0.3 fusion.1
  116.8 0.3 fusion.7
  117.2 0.3 fusion.5
  117.5 0.3 fusion.2
  117.8 0.1 pad_maximum_fusion.1
  117.9 5.6 %collective-permute-start.9 = (bf16[2,256,512]{2,1,0:T(8,128)(2,1)S(1)}, bf16[2,256,512]{2,1,0:T(8,128)(2,1)S(1)}, u32[]{:S(2)}, u32[]{:S(2)}) collective-permute-start(bf16[2,256,512]{2,1,0:T(8,128)(2,1)S(1)} %pad_maximum_fusion.1), channel_id=1, source_target_pairs={{0,1},{1,0},{2,3},{3,2},{4,5},{5,4},{6,7},{7,6},{8,9},{9,8},{10,11... | collective-permute-start | bytes 1572872 | tf_op jit(solution)/shard_map/ppermute | solution.py:180
  123.5 0.3 fusion.6
  123.9 0.3 convolution_add_fusion.1
  124.2 0.9 collective-permute-done.9
  125.1 0.9 fusion.3
  (16 shorter events, 0.2 us)
Async XLA Ops:
  1.4 16.1 %copy-start = (bf16[256,4096]{1,0:T(8,128)(2,1)S(1)}, bf16[256,4096]{1,0:T(8,128)(2,1)}, u32[]{:S(2)}) copy-start(bf16[256,4096]{1,0:T(8,128)(2,1)} %param.19) | copy-start | bytes 6291460
  1.4 22.8 %copy-start.5 = (s32[256]{0:T(256)S(1)}, s32[256]{0:T(256)}, u32[]{:S(2)}) copy-start(s32[256]{0:T(256)} %param.18) | copy-start | bytes 3076
  1.4 22.8 %copy-start.6 = (s32[2]{0:T(128)S(1)}, s32[2]{0:T(128)}, u32[]{:S(2)}) copy-start(s32[2]{0:T(128)} %param.17) | copy-start | bytes 28
  3.4 54.5 %all-to-all-start.1 = ((bf16[64,2,4096]{2,1,0:T(2,128)(2,1)}), bf16[64,2,4096]{2,1,0:T(2,128)(2,1)S(1)}, u32[]{:S(2)}, u32[]{:S(2)}) async-start(bf16[64,2,4096]{2,1,0:T(2,128)(2,1)} %broadcast_in_dim.36), calls=%async_computation.1 | async-start | bytes 2097152 | tf_op jit(solution)/shard_map/all_to_all | solution.py:133
  17.5 55.2 %collective-permute-start.3 = (bf16[256,4096]{1,0:T(8,128)(2,1)S(1)}, bf16[256,4096]{1,0:T(8,128)(2,1)}, u32[]{:S(2)}, u32[]{:S(2)}) collective-permute-start(bf16[256,4096]{1,0:T(8,128)(2,1)S(1)} %copy-done), channel_id=1, source_target_pairs={{0,1},{1,0},{2,3},{3,2},{4,5},{5,4},{6,7},{7,6},{8,9},{9,8},{10,11... | collective-permute-start | bytes 6291464 | tf_op jit(solution)/shard_map/ppermute | solution.py:138
  24.3 3.7 %collective-permute-start = (s32[384]{0:T(512)S(1)}, s32[384]{0:T(512)S(1)}, u32[]{:S(2)}, u32[]{:S(2)}) collective-permute-start(s32[384]{0:T(512)S(1)} %pad_add_fusion.1), channel_id=1, source_target_pairs={{0,1},{1,0},{2,3},{3,2},{4,5},{5,4},{6,7},{7,6},{8,9},{9,8},{10,11... | collective-permute-start | bytes 4616 | tf_op jit(solution)/shard_map/ppermute | solution.py:140
  28.5 16.8 %copy-start.2 = (bf16[1,4096]{1,0:T(2,128)(2,1)S(1)}, bf16[1,4096]{1,0:T(2,128)(2,1)}, u32[]{:S(2)}) copy-start(bf16[1,4096]{1,0:T(2,128)(2,1)} %param.11) | copy-start | bytes 24580
  28.5 16.8 %copy-start.3 = (bf16[1,4096]{1,0:T(2,128)(2,1)S(1)}, bf16[1,4096]{1,0:T(2,128)(2,1)}, u32[]{:S(2)}) copy-start(bf16[1,4096]{1,0:T(2,128)(2,1)} %param.10) | copy-start | bytes 24580
  28.5 16.8 %copy-start.4 = (bf16[1,4096]{1,0:T(2,128)(2,1)S(1)}, bf16[1,4096]{1,0:T(2,128)(2,1)}, u32[]{:S(2)}) copy-start(bf16[1,4096]{1,0:T(2,128)(2,1)} %param.12) | copy-start | bytes 24580
  34.9 14.2 %collective-permute-start.1 = (bf16[1,64,1024]{2,1,0:T(8,128)(2,1)}, bf16[1,64,1024]{2,1,0:T(8,128)(2,1)S(1)}, u32[]{:S(2)}, u32[]{:S(2)}) collective-permute-start(bf16[1,64,1024]{2,1,0:T(8,128)(2,1)} %bitcast.80), channel_id=1, source_target_pairs={{0,512},{128,640},{256,768},{384,896},{512,0},{640,128},{768,256},... | collective-permute-start | bytes 393224 | tf_op jit(solution)/shard_map/ppermute | solution.py:127
  50.7 31.4 %collective-permute-start.2 = (bf16[2,64,1024]{2,1,0:T(8,128)(2,1)}, bf16[2,64,1024]{2,1,0:T(8,128)(2,1)}, u32[]{:S(2)}, u32[]{:S(2)}) collective-permute-start(bf16[2,64,1024]{2,1,0:T(8,128)(2,1)} %pad_maximum_fusion.2), channel_id=1, source_target_pairs={{0,256},{128,384},{256,0},{384,128},{512,768},{640,896},{768,512},... | collective-permute-start | bytes 786440 | tf_op jit(solution)/shard_map/ppermute | solution.py:127
  58.8 25.1 %all-to-all-start = ((bf16[64,4,512]{2,1,0:T(4,128)(2,1)}), bf16[64,4,512]{2,1,0:T(4,128)(2,1)S(1)}, u32[]{:S(2)}, u32[]{:S(2)}) async-start(bf16[64,4,512]{2,1,0:T(4,128)(2,1)} %bitcast.78), calls=%async_computation | async-start | bytes 524288 | tf_op jit(solution)/shard_map/all_to_all | solution.py:133
  72.7 2.5 %copy-start.1 = (bf16[64,1024]{1,0:T(8,128)(2,1)S(1)}, bf16[64,1024]{1,0:T(8,128)(2,1)}, u32[]{:S(2)}) copy-start(bf16[64,1024]{1,0:T(8,128)(2,1)} %sel.1) | copy-start | bytes 393220
  75.2 9.8 %collective-permute-start.4 = (bf16[1,64,512]{2,1,0:T(8,128)(2,1)S(1)}, bf16[1,64,512]{2,1,0:T(8,128)(2,1)S(1)}, u32[]{:S(2)}, u32[]{:S(2)}) collective-permute-start(bf16[1,64,512]{2,1,0:T(8,128)(2,1)S(1)} %fusion.20), channel_id=1, source_target_pairs={{0,512},{128,640},{256,768},{384,896},{512,0},{640,128},{768,256},... | collective-permute-start | bytes 196616 | tf_op jit(solution)/shard_map/ppermute | solution.py:127
  86.6 29.9 %all-to-all-start.2 = ((bf16[8,8,24,512]{3,2,1,0:T(8,128)(2,1)}), bf16[8,8,24,512]{3,2,1,0:T(8,128)(2,1)S(1)}, u32[]{:S(2)}, u32[]{:S(2)}) async-start(bf16[8,8,24,512]{3,2,1,0:T(8,128)(2,1)} %broadcast_in_dim.40), calls=%async_computation.2 | async-start | bytes 3145728 | tf_op jit(solution)/shard_map/all_to_all | solution.py:133
  92.3 23.5 %collective-permute-start.5 = (bf16[4,64,1024]{2,1,0:T(8,128)(2,1)S(1)}, bf16[4,64,1024]{2,1,0:T(8,128)(2,1)S(1)}, u32[]{:S(2)}, u32[]{:S(2)}) collective-permute-start(bf16[4,64,1024]{2,1,0:T(8,128)(2,1)S(1)} %pad_maximum_fusion), channel_id=1, source_target_pairs={{0,128},{128,0},{256,384},{384,256},{512,640},{640,512},{768,896},... | collective-permute-start | bytes 1572872 | tf_op jit(solution)/shard_map/ppermute | solution.py:127
  95.1 10.5 %collective-permute-start.6 = (bf16[2,64,512]{2,1,0:T(8,128)(2,1)S(1)}, bf16[2,64,512]{2,1,0:T(8,128)(2,1)S(1)}, u32[]{:S(2)}, u32[]{:S(2)}) collective-permute-start(bf16[2,64,512]{2,1,0:T(8,128)(2,1)S(1)} %pad_maximum_fusion.4), channel_id=1, source_target_pairs={{0,256},{128,384},{256,0},{384,128},{512,768},{640,896},{768,512},... | collective-permute-start | bytes 393224 | tf_op jit(solution)/shard_map/ppermute | solution.py:127
  99.2 11.3 %collective-permute-start.7 = (bf16[2,64,512]{2,1,0:T(8,128)(2,1)S(1)}, bf16[2,64,512]{2,1,0:T(8,128)(2,1)S(1)}, u32[]{:S(2)}, u32[]{:S(2)}) collective-permute-start(bf16[2,64,512]{2,1,0:T(8,128)(2,1)S(1)} %pad_maximum_fusion.4), channel_id=1, source_target_pairs={{0,128},{128,0},{256,384},{384,256},{512,640},{640,512},{768,896},... | collective-permute-start | bytes 393224 | tf_op jit(solution)/shard_map/ppermute | solution.py:127
  102.0 13.4 %collective-permute-start.8 = (bf16[2,64,512]{2,1,0:T(8,128)(2,1)S(1)}, bf16[2,64,512]{2,1,0:T(8,128)(2,1)S(1)}, u32[]{:S(2)}, u32[]{:S(2)}) collective-permute-start(bf16[2,64,512]{2,1,0:T(8,128)(2,1)S(1)} %pad_maximum_fusion.4), channel_id=1, source_target_pairs={{0,384},{128,256},{256,128},{384,0},{512,896},{640,768},{768,640},... | collective-permute-start | bytes 393224 | tf_op jit(solution)/shard_map/ppermute | solution.py:127
  117.9 7.2 %collective-permute-start.9 = (bf16[2,256,512]{2,1,0:T(8,128)(2,1)S(1)}, bf16[2,256,512]{2,1,0:T(8,128)(2,1)S(1)}, u32[]{:S(2)}, u32[]{:S(2)}) collective-permute-start(bf16[2,256,512]{2,1,0:T(8,128)(2,1)S(1)} %pad_maximum_fusion.1), channel_id=1, source_target_pairs={{0,1},{1,0},{2,3},{3,2},{4,5},{5,4},{6,7},{7,6},{8,9},{9,8},{10,11... | collective-permute-start | bytes 1572872 | tf_op jit(solution)/shard_map/ppermute | solution.py:180

commit v5 on v4

--- a/solution.py
+++ b/solution.py
@@ -9,6 +9,7 @@
 
 LAT_DEV = 32768
 BLOCK = 128
+LOW = 64
 
 
 def sel_kernel(place, top_idx, top_val, aux_idx, aux_val, cores, out, high, low, val, found):
@@ -17,13 +18,13 @@
     slots = out.shape[1] // 2
     width = slots // 2
     side = math.isqrt(rows // 2)
-    tables = 2 * slots // 128
+    tables = 2 * slots // LOW
     core = place[0]
 
     def put(at, col, v):
         to = pl.ds(at, col.shape[1])
-        high[:, to] = col >> 7
-        low[:, to] = col & 127
+        high[:, to] = col >> 6
+        low[:, to] = col & (LOW - 1)
         val[:, to] = v
 
     col = aux_idx[...] - place[1] * slots
@@ -41,7 +42,7 @@
 
     n = n_aux + n_top
     row_high = lax.broadcasted_iota(jnp.int32, (tables, n), 0)
-    row_low = lax.broadcasted_iota(jnp.int32, (128, n), 0)
+    row_low = lax.broadcasted_iota(jnp.int32, (LOW, n), 0)
 
     def step(a, carry):
         for b in range(side):
@@ -52,12 +53,15 @@
             table = lax.dot_general(
                 spread, hot, (((1,), (1,)), ((), ())), preferred_element_type=jnp.float32
             )
-            found[pl.ds(side * a + b, tables, stride=side * side), :] = table
+            found[pl.ds(side * a + b, tables, stride=side * side), :] = jnp.concatenate([table, table], axis=1)
         return carry
 
     lax.fori_loop(0, side, step, 0)
-    for k in range(tables):
-        table = found[side * side * k : side * side * (k + 1), :]
+    first = lax.broadcasted_iota(jnp.int32, (1, 128), 1) < LOW
+    for k in range(2 * slots // 128):
+        even = found[2 * k * side * side : (2 * k + 1) * side * side, :]
+        odd = found[(2 * k + 1) * side * side : (2 * k + 2) * side * side, :]
+        table = jnp.where(first, even, odd)
         if 128 * k >= slots:
             other, at = divmod(128 * k - slots, width)
             table = table * cores[other : other + 1, at : at + 128].astype(jnp.float32)
@@ -77,7 +81,7 @@
             pltpu.VMEM((rows, entries), jnp.int32),
             pltpu.VMEM((rows, entries), jnp.int32),
             pltpu.VMEM((rows, entries), jnp.float32),
-            pltpu.VMEM((rows * slots // 128, 128), jnp.float32),
+            pltpu.VMEM((rows * slots // LOW, 128), jnp.float32),
         ],
         cost_estimate=pl.CostEstimate(
             flops=rows * entries * slots * 32, bytes_accessed=1 << 20, transcendentals=0

time: 127 us -> 126 us (level)
  transfers between devices with their start and end apart: 13 -> 13, of which waited for: 8 -> 8; matrix products, arithmetic and copies ran while one was open for 8% -> 8% of each run, Pallas kernels for 5% -> 4%
where the time goes in v5:
time: 126 us; the launch traced here: 125 us
  starting transfers between devices  83.1 us (66%)
  waiting for transfers between devices  18.4 us (15%)
  other arithmetic  6.16 us (5%)
  local copies, waits for them, and re-layouts  5.74 us (5%)
  Pallas kernels  5.31 us (4%)
  matrix products  5.22 us (4%)
    ppermute x7, starting transfers between devices, send(): return lax.ppermute(v, 'dp', [(i, i ^ step) for i in range(n_dp)])  36.7 us
    all_to_all x3, starting transfers between devices, exchange(): lax.all_to_all(v, ('dp', 'lat', 'inner'), 0, 0, axis_index_groups=groups,...  32.2 us
    ppermute x7, waiting for transfers between devices, send(): return lax.ppermute(v, 'dp', [(i, i ^ step) for i in range(n_dp)])  15.8 us
    ppermute x1, starting transfers between devices, local(): dec_other = lax.ppermute(dec_rows, 'inner', swap)  6.68 us
    ppermute x1, starting transfers between devices, local(): got = lax.ppermute(sent, 'inner', swap)  5.65 us
    pallas_call x1, Pallas kernels, make_sel(): pl.pallas_call(sel_kernel, in_specs=[pl.BlockSpec(memory_space=pltpu.SMEM...  5.31 us
    dot_general x2, matrix products, rows_dot(): lax.dot_general(left, right, (((1,), (1,)), ((), ())), preferred_element_...  3.29 us
    concatenate x3, other arithmetic, grow(): return jnp.concatenate([v, send(v, step)], axis=0)  2.72 us
  transfers between devices with their start and end apart: 13, of which 8 were waited for; matrix products, arithmetic and copies ran while one was open for 8% of the time, Pallas kernels for 4%

profile of v5, /device:TPU:1, one launch (start us, length us, event | category | flops | bytes accessed | tf_op | source)
XLA Modules:
  0.0 125.0 jit_solution(12280867724016284796)
XLA Ops:
  0.6 0.8 pad_maximum_fusion.6
  1.4 0.0 copy-start
  1.4 0.0 copy-start.5
  1.4 0.0 copy-start.6
  1.4 2.0 %broadcast_in_dim.36 = bf16[64,2,4096]{2,1,0:T(2,128)(2,1)} broadcast(bf16[2,4096]{1,0:T(2,128)(2,1)S(1)} %pad_maximum_fusion.6), dimensions={1,2} | broadcast | bytes 1064960 | tf_op jit(solution)/shard_map/broadcast_in_dim | solution.py:150
  3.4 14.0 %all-to-all-start.1 = ((bf16[64,2,4096]{2,1,0:T(2,128)(2,1)}), bf16[64,2,4096]{2,1,0:T(2,128)(2,1)S(1)}, u32[]{:S(2)}, u32[]{:S(2)}) async-start(bf16[64,2,4096]{2,1,0:T(2,128)(2,1)} %broadcast_in_dim.36), calls=%async_computation.1 | async-start | bytes 2097152 | tf_op jit(solution)/shard_map/all_to_all | solution.py:137
  17.5 0.0 copy-done
  17.5 6.7 %collective-permute-start.3 = (bf16[256,4096]{1,0:T(8,128)(2,1)S(1)}, bf16[256,4096]{1,0:T(8,128)(2,1)}, u32[]{:S(2)}, u32[]{:S(2)}) collective-permute-start(bf16[256,4096]{1,0:T(8,128)(2,1)S(1)} %copy-done), channel_id=1, source_target_pairs={{0,1},{1,0},{2,3},{3,2},{4,5},{5,4},{6,7},{7,6},{8,9},{9,8},{10,11... | collective-permute-start | bytes 6291464 | tf_op jit(solution)/shard_map/ppermute | solution.py:142
  24.2 0.0 copy-done.5
  24.2 0.0 copy-done.6
  24.2 0.1 pad_add_fusion.1
  24.3 1.9 %collective-permute-start = (s32[384]{0:T(512)S(1)}, s32[384]{0:T(512)S(1)}, u32[]{:S(2)}, u32[]{:S(2)}) collective-permute-start(s32[384]{0:T(512)S(1)} %pad_add_fusion.1), channel_id=1, source_target_pairs={{0,1},{1,0},{2,3},{3,2},{4,5},{5,4},{6,7},{7,6},{8,9},{9,8},{10,11... | collective-permute-start | bytes 4616 | tf_op jit(solution)/shard_map/ppermute | solution.py:144
  26.2 0.6 pad_add_fusion.2.place
  26.8 1.2 collective-permute-done
  28.0 0.6 pad_add_fusion.cores
  28.5 5.3 %sel.1 = bf16[64,1024]{1,0:T(8,128)(2,1)} custom-call(s32[2]{0:T(128)} %pad_add_fusion.2.place, s32[64,128]{1,0:T(8,128)} %bitcast.84, bf16[64,128]{1,0:T(8,128)(2,1)} %bitcast.85, s32[128,512]{1,0:T(8,128)} %aux_idx.1, bf16[128,512]{1,0:T(8,128)(2,1)} %aux_val.1, s32[2,384]{1,0:T(2,128)} %pad_add_fusion.cores), custom_call_target="tpu_custom_call" | custom-call | flops 1342177280 | bytes 1048576 | tf_op jit(solution)/shard_map/sel/pallas_call | solution.py:75
  33.9 10.4 %collective-permute-start.1 = (bf16[1,64,1024]{2,1,0:T(8,128)(2,1)}, bf16[1,64,1024]{2,1,0:T(8,128)(2,1)S(1)}, u32[]{:S(2)}, u32[]{:S(2)}) collective-permute-start(bf16[1,64,1024]{2,1,0:T(8,128)(2,1)} %bitcast.80), channel_id=1, source_target_pairs={{0,512},{128,640},{256,768},{384,896},{512,0},{640,128},{768,256},... | collective-permute-start | bytes 393224 | tf_op jit(solution)/shard_map/ppermute | solution.py:131
  44.3 0.0 copy-done.2
  44.3 0.0 copy-done.3
  44.3 0.0 copy-done.4
  44.3 0.1 pad_maximum_fusion.5
  44.5 3.6 %collective-permute-done.1 = bf16[1,64,1024]{2,1,0:T(8,128)(2,1)S(1)} collective-permute-done((bf16[1,64,1024]{2,1,0:T(8,128)(2,1)}, bf16[1,64,1024]{2,1,0:T(8,128)(2,1)S(1)}, u32[]{:S(2)}, u32[]{:S(2)}) %collective-permute-start.1) | collective-permute-done | bytes 131104 | tf_op jit(solution)/shard_map/ppermute | solution.py:131
  48.1 1.6 %pad_maximum_fusion.2 = bf16[2,64,1024]{2,1,0:T(8,128)(2,1)} fusion(bf16[1,64,1024]{2,1,0:T(8,128)(2,1)S(1)} %collective-permute-done.1, bf16[1,64,1024]{2,1,0:T(8,128)(2,1)} %bitcast.81), kind=kLoop, calls=%fused_computation.32 | loop fusion | flops 131072 | bytes 524288 | tf_op jit(solution)/shard_map/concatenate | solution.py:134
  49.7 7.2 %collective-permute-start.2 = (bf16[2,64,1024]{2,1,0:T(8,128)(2,1)}, bf16[2,64,1024]{2,1,0:T(8,128)(2,1)}, u32[]{:S(2)}, u32[]{:S(2)}) collective-permute-start(bf16[2,64,1024]{2,1,0:T(8,128)(2,1)} %pad_maximum_fusion.2), channel_id=1, source_target_pairs={{0,256},{128,384},{256,0},{384,128},{512,768},{640,896},{768,512},... | collective-permute-start | bytes 786440 | tf_op jit(solution)/shard_map/ppermute | solution.py:131
  57.0 0.0 all-to-all-done.1
  57.0 0.8 broadcast_in_dim.35
  57.8 12.5 %all-to-all-start = ((bf16[64,4,512]{2,1,0:T(4,128)(2,1)}), bf16[64,4,512]{2,1,0:T(4,128)(2,1)S(1)}, u32[]{:S(2)}, u32[]{:S(2)}) async-start(bf16[64,4,512]{2,1,0:T(4,128)(2,1)} %bitcast.78), calls=%async_computation | async-start | bytes 524288 | tf_op jit(solution)/shard_map/all_to_all | solution.py:137
  70.2 0.6 copy.23
  70.8 0.8 fusion.21
  71.7 0.0 collective-permute-done.3
  71.7 2.5 %fusion.22 = f32[128,256]{1,0:T(8,128)S(1)} fusion(bf16[128,4096]{1,0:T(8,128)(2,1)S(1)} %bitcast.70, bf16[256,4096]{1,0:T(8,128)(2,1)} %collective-permute-done.3), kind=kOutput, calls=%fused_computation.52 | convolution fusion | flops 268435456 | bytes 3276800 | tf_op jit(solution)/shard_map/dot_general | solution.py:94
  74.1 0.0 copy-done.1
  74.2 6.9 %collective-permute-start.4 = (bf16[1,64,512]{2,1,0:T(8,128)(2,1)S(1)}, bf16[1,64,512]{2,1,0:T(8,128)(2,1)S(1)}, u32[]{:S(2)}, u32[]{:S(2)}) collective-permute-start(bf16[1,64,512]{2,1,0:T(8,128)(2,1)S(1)} %fusion.20), channel_id=1, source_target_pairs={{0,512},{128,640},{256,768},{384,896},{512,0},{640,128},{768,256},... | collective-permute-start | bytes 196616 | tf_op jit(solution)/shard_map/ppermute | solution.py:131
  81.1 0.0 collective-permute-done.2
  81.1 1.1 pad_maximum_fusion
  82.2 0.6 all-to-all-done
  82.9 1.1 collective-permute-done.4
  84.0 0.1 reverse_select_fusion.1
  84.2 0.1 copy.26
  84.3 1.3 %broadcast_in_dim.40 = bf16[8,8,24,512]{3,2,1,0:T(8,128)(2,1)} broadcast(bf16[8,24,512]{2,1,0:T(8,128)(2,1)S(1)} %copy.26), dimensions={1,2,3} | broadcast | bytes 1769472 | tf_op jit(solution)/shard_map/broadcast_in_dim | solution.py:140
  85.6 5.7 %all-to-all-start.2 = ((bf16[8,8,24,512]{3,2,1,0:T(8,128)(2,1)}), bf16[8,8,24,512]{3,2,1,0:T(8,128)(2,1)S(1)}, u32[]{:S(2)}, u32[]{:S(2)}) async-start(bf16[8,8,24,512]{3,2,1,0:T(8,128)(2,1)} %broadcast_in_dim.40), calls=%async_computation.2 | async-start | bytes 3145728 | tf_op jit(solution)/shard_map/all_to_all | solution.py:137
  91.3 2.8 %collective-permute-start.5 = (bf16[4,64,1024]{2,1,0:T(8,128)(2,1)S(1)}, bf16[4,64,1024]{2,1,0:T(8,128)(2,1)S(1)}, u32[]{:S(2)}, u32[]{:S(2)}) collective-permute-start(bf16[4,64,1024]{2,1,0:T(8,128)(2,1)S(1)} %pad_maximum_fusion), channel_id=1, source_target_pairs={{0,128},{128,0},{256,384},{384,256},{512,640},{640,512},{768,896},... | collective-permute-start | bytes 1572872 | tf_op jit(solution)/shard_map/ppermute | solution.py:131
  94.1 4.0 %collective-permute-start.6 = (bf16[2,64,512]{2,1,0:T(8,128)(2,1)S(1)}, bf16[2,64,512]{2,1,0:T(8,128)(2,1)S(1)}, u32[]{:S(2)}, u32[]{:S(2)}) collective-permute-start(bf16[2,64,512]{2,1,0:T(8,128)(2,1)S(1)} %pad_maximum_fusion.4), channel_id=1, source_target_pairs={{0,256},{128,384},{256,0},{384,128},{512,768},{640,896},{768,512},... | collective-permute-start | bytes 393224 | tf_op jit(solution)/shard_map/ppermute | solution.py:131
  98.2 2.8 %collective-permute-start.7 = (bf16[2,64,512]{2,1,0:T(8,128)(2,1)S(1)}, bf16[2,64,512]{2,1,0:T(8,128)(2,1)S(1)}, u32[]{:S(2)}, u32[]{:S(2)}) collective-permute-start(bf16[2,64,512]{2,1,0:T(8,128)(2,1)S(1)} %pad_maximum_fusion.4), channel_id=1, source_target_pairs={{0,128},{128,0},{256,384},{384,256},{512,640},{640,512},{768,896},... | collective-permute-start | bytes 393224 | tf_op jit(solution)/shard_map/ppermute | solution.py:131
  101.0 2.4 %collective-permute-start.8 = (bf16[2,64,512]{2,1,0:T(8,128)(2,1)S(1)}, bf16[2,64,512]{2,1,0:T(8,128)(2,1)S(1)}, u32[]{:S(2)}, u32[]{:S(2)}) collective-permute-start(bf16[2,64,512]{2,1,0:T(8,128)(2,1)S(1)} %pad_maximum_fusion.4), channel_id=1, source_target_pairs={{0,384},{128,256},{256,128},{384,0},{512,896},{640,768},{768,640},... | collective-permute-start | bytes 393224 | tf_op jit(solution)/shard_map/ppermute | solution.py:131
  103.4 1.2 collective-permute-done.6
  104.6 4.9 %collective-permute-done.7 = bf16[2,64,512]{2,1,0:T(8,128)(2,1)S(1)} collective-permute-done((bf16[2,64,512]{2,1,0:T(8,128)(2,1)S(1)}, bf16[2,64,512]{2,1,0:T(8,128)(2,1)S(1)}, u32[]{:S(2)}, u32[]{:S(2)}) %collective-permute-start.7) | collective-permute-done | bytes 131104 | tf_op jit(solution)/shard_map/ppermute | solution.py:131
  109.5 4.9 %collective-permute-done.8 = bf16[2,64,512]{2,1,0:T(8,128)(2,1)S(1)} collective-permute-done((bf16[2,64,512]{2,1,0:T(8,128)(2,1)S(1)}, bf16[2,64,512]{2,1,0:T(8,128)(2,1)S(1)}, u32[]{:S(2)}, u32[]{:S(2)}) %collective-permute-start.8) | collective-permute-done | bytes 131104 | tf_op jit(solution)/shard_map/ppermute | solution.py:131
  114.4 0.1 maximum_bitcast_fusion.1
  114.5 0.3 copy.33
  114.8 0.0 collective-permute-done.5
  114.8 0.1 maximum_bitcast_fusion
  114.9 0.6 copy.32
  115.5 0.0 all-to-all-done.2
  115.5 0.3 fusion.1
  115.8 0.3 fusion.7
  116.2 0.3 fusion.5
  116.5 0.3 fusion.2
  116.8 0.1 pad_maximum_fusion.1
  116.9 5.6 %collective-permute-start.9 = (bf16[2,256,512]{2,1,0:T(8,128)(2,1)S(1)}, bf16[2,256,512]{2,1,0:T(8,128)(2,1)S(1)}, u32[]{:S(2)}, u32[]{:S(2)}) collective-permute-start(bf16[2,256,512]{2,1,0:T(8,128)(2,1)S(1)} %pad_maximum_fusion.1), channel_id=1, source_target_pairs={{0,1},{1,0},{2,3},{3,2},{4,5},{5,4},{6,7},{7,6},{8,9},{9,8},{10,11... | collective-permute-start | bytes 1572872 | tf_op jit(solution)/shard_map/ppermute | solution.py:184
  122.5 0.3 fusion.6
  122.9 0.3 convolution_add_fusion.1
  123.2 0.9 collective-permute-done.9
  124.1 0.9 fusion.3
  (16 shorter events, 0.2 us)
Async XLA Ops:
  1.4 16.1 %copy-start = (bf16[256,4096]{1,0:T(8,128)(2,1)S(1)}, bf16[256,4096]{1,0:T(8,128)(2,1)}, u32[]{:S(2)}) copy-start(bf16[256,4096]{1,0:T(8,128)(2,1)} %param.19) | copy-start | bytes 6291460
  1.4 22.8 %copy-start.5 = (s32[256]{0:T(256)S(1)}, s32[256]{0:T(256)}, u32[]{:S(2)}) copy-start(s32[256]{0:T(256)} %param.18) | copy-start | bytes 3076
  1.4 22.8 %copy-start.6 = (s32[2]{0:T(128)S(1)}, s32[2]{0:T(128)}, u32[]{:S(2)}) copy-start(s32[2]{0:T(128)} %param.17) | copy-start | bytes 28
  3.4 53.5 %all-to-all-start.1 = ((bf16[64,2,4096]{2,1,0:T(2,128)(2,1)}), bf16[64,2,4096]{2,1,0:T(2,128)(2,1)S(1)}, u32[]{:S(2)}, u32[]{:S(2)}) async-start(bf16[64,2,4096]{2,1,0:T(2,128)(2,1)} %broadcast_in_dim.36), calls=%async_computation.1 | async-start | bytes 2097152 | tf_op jit(solution)/shard_map/all_to_all | solution.py:137
  17.5 54.2 %collective-permute-start.3 = (bf16[256,4096]{1,0:T(8,128)(2,1)S(1)}, bf16[256,4096]{1,0:T(8,128)(2,1)}, u32[]{:S(2)}, u32[]{:S(2)}) collective-permute-start(bf16[256,4096]{1,0:T(8,128)(2,1)S(1)} %copy-done), channel_id=1, source_target_pairs={{0,1},{1,0},{2,3},{3,2},{4,5},{5,4},{6,7},{7,6},{8,9},{9,8},{10,11... | collective-permute-start | bytes 6291464 | tf_op jit(solution)/shard_map/ppermute | solution.py:142
  24.3 3.7 %collective-permute-start = (s32[384]{0:T(512)S(1)}, s32[384]{0:T(512)S(1)}, u32[]{:S(2)}, u32[]{:S(2)}) collective-permute-start(s32[384]{0:T(512)S(1)} %pad_add_fusion.1), channel_id=1, source_target_pairs={{0,1},{1,0},{2,3},{3,2},{4,5},{5,4},{6,7},{7,6},{8,9},{9,8},{10,11... | collective-permute-start | bytes 4616 | tf_op jit(solution)/shard_map/ppermute | solution.py:144
  28.5 15.8 %copy-start.2 = (bf16[1,4096]{1,0:T(2,128)(2,1)S(1)}, bf16[1,4096]{1,0:T(2,128)(2,1)}, u32[]{:S(2)}) copy-start(bf16[1,4096]{1,0:T(2,128)(2,1)} %param.11) | copy-start | bytes 24580
  28.5 15.8 %copy-start.3 = (bf16[1,4096]{1,0:T(2,128)(2,1)S(1)}, bf16[1,4096]{1,0:T(2,128)(2,1)}, u32[]{:S(2)}) copy-start(bf16[1,4096]{1,0:T(2,128)(2,1)} %param.10) | copy-start | bytes 24580
  28.5 15.8 %copy-start.4 = (bf16[1,4096]{1,0:T(2,128)(2,1)S(1)}, bf16[1,4096]{1,0:T(2,128)(2,1)}, u32[]{:S(2)}) copy-start(bf16[1,4096]{1,0:T(2,128)(2,1)} %param.12) | copy-start | bytes 24580
  33.9 14.2 %collective-permute-start.1 = (bf16[1,64,1024]{2,1,0:T(8,128)(2,1)}, bf16[1,64,1024]{2,1,0:T(8,128)(2,1)S(1)}, u32[]{:S(2)}, u32[]{:S(2)}) collective-permute-start(bf16[1,64,1024]{2,1,0:T(8,128)(2,1)} %bitcast.80), channel_id=1, source_target_pairs={{0,512},{128,640},{256,768},{384,896},{512,0},{640,128},{768,256},... | collective-permute-start | bytes 393224 | tf_op jit(solution)/shard_map/ppermute | solution.py:131
  49.7 31.4 %collective-permute-start.2 = (bf16[2,64,1024]{2,1,0:T(8,128)(2,1)}, bf16[2,64,1024]{2,1,0:T(8,128)(2,1)}, u32[]{:S(2)}, u32[]{:S(2)}) collective-permute-start(bf16[2,64,1024]{2,1,0:T(8,128)(2,1)} %pad_maximum_fusion.2), channel_id=1, source_target_pairs={{0,256},{128,384},{256,0},{384,128},{512,768},{640,896},{768,512},... | collective-permute-start | bytes 786440 | tf_op jit(solution)/shard_map/ppermute | solution.py:131
  57.8 25.1 %all-to-all-start = ((bf16[64,4,512]{2,1,0:T(4,128)(2,1)}), bf16[64,4,512]{2,1,0:T(4,128)(2,1)S(1)}, u32[]{:S(2)}, u32[]{:S(2)}) async-start(bf16[64,4,512]{2,1,0:T(4,128)(2,1)} %bitcast.78), calls=%async_computation | async-start | bytes 524288 | tf_op jit(solution)/shard_map/all_to_all | solution.py:137
  71.7 2.5 %copy-start.1 = (bf16[64,1024]{1,0:T(8,128)(2,1)S(1)}, bf16[64,1024]{1,0:T(8,128)(2,1)}, u32[]{:S(2)}) copy-start(bf16[64,1024]{1,0:T(8,128)(2,1)} %sel.1) | copy-start | bytes 393220
  74.2 9.8 %collective-permute-start.4 = (bf16[1,64,512]{2,1,0:T(8,128)(2,1)S(1)}, bf16[1,64,512]{2,1,0:T(8,128)(2,1)S(1)}, u32[]{:S(2)}, u32[]{:S(2)}) collective-permute-start(bf16[1,64,512]{2,1,0:T(8,128)(2,1)S(1)} %fusion.20), channel_id=1, source_target_pairs={{0,512},{128,640},{256,768},{384,896},{512,0},{640,128},{768,256},... | collective-permute-start | bytes 196616 | tf_op jit(solution)/shard_map/ppermute | solution.py:131
  85.6 29.9 %all-to-all-start.2 = ((bf16[8,8,24,512]{3,2,1,0:T(8,128)(2,1)}), bf16[8,8,24,512]{3,2,1,0:T(8,128)(2,1)S(1)}, u32[]{:S(2)}, u32[]{:S(2)}) async-start(bf16[8,8,24,512]{3,2,1,0:T(8,128)(2,1)} %broadcast_in_dim.40), calls=%async_computation.2 | async-start | bytes 3145728 | tf_op jit(solution)/shard_map/all_to_all | solution.py:137
  91.3 23.5 %collective-permute-start.5 = (bf16[4,64,1024]{2,1,0:T(8,128)(2,1)S(1)}, bf16[4,64,1024]{2,1,0:T(8,128)(2,1)S(1)}, u32[]{:S(2)}, u32[]{:S(2)}) collective-permute-start(bf16[4,64,1024]{2,1,0:T(8,128)(2,1)S(1)} %pad_maximum_fusion), channel_id=1, source_target_pairs={{0,128},{128,0},{256,384},{384,256},{512,640},{640,512},{768,896},... | collective-permute-start | bytes 1572872 | tf_op jit(solution)/shard_map/ppermute | solution.py:131
  94.1 10.5 %collective-permute-start.6 = (bf16[2,64,512]{2,1,0:T(8,128)(2,1)S(1)}, bf16[2,64,512]{2,1,0:T(8,128)(2,1)S(1)}, u32[]{:S(2)}, u32[]{:S(2)}) collective-permute-start(bf16[2,64,512]{2,1,0:T(8,128)(2,1)S(1)} %pad_maximum_fusion.4), channel_id=1, source_target_pairs={{0,256},{128,384},{256,0},{384,128},{512,768},{640,896},{768,512},... | collective-permute-start | bytes 393224 | tf_op jit(solution)/shard_map/ppermute | solution.py:131
  98.2 11.3 %collective-permute-start.7 = (bf16[2,64,512]{2,1,0:T(8,128)(2,1)S(1)}, bf16[2,64,512]{2,1,0:T(8,128)(2,1)S(1)}, u32[]{:S(2)}, u32[]{:S(2)}) collective-permute-start(bf16[2,64,512]{2,1,0:T(8,128)(2,1)S(1)} %pad_maximum_fusion.4), channel_id=1, source_target_pairs={{0,128},{128,0},{256,384},{384,256},{512,640},{640,512},{768,896},... | collective-permute-start | bytes 393224 | tf_op jit(solution)/shard_map/ppermute | solution.py:131
  101.0 13.4 %collective-permute-start.8 = (bf16[2,64,512]{2,1,0:T(8,128)(2,1)S(1)}, bf16[2,64,512]{2,1,0:T(8,128)(2,1)S(1)}, u32[]{:S(2)}, u32[]{:S(2)}) collective-permute-start(bf16[2,64,512]{2,1,0:T(8,128)(2,1)S(1)} %pad_maximum_fusion.4), channel_id=1, source_target_pairs={{0,384},{128,256},{256,128},{384,0},{512,896},{640,768},{768,640},... | collective-permute-start | bytes 393224 | tf_op jit(solution)/shard_map/ppermute | solution.py:131
  116.9 7.2 %collective-permute-start.9 = (bf16[2,256,512]{2,1,0:T(8,128)(2,1)S(1)}, bf16[2,256,512]{2,1,0:T(8,128)(2,1)S(1)}, u32[]{:S(2)}, u32[]{:S(2)}) collective-permute-start(bf16[2,256,512]{2,1,0:T(8,128)(2,1)S(1)} %pad_maximum_fusion.1), channel_id=1, source_target_pairs={{0,1},{1,0},{2,3},{3,2},{4,5},{5,4},{6,7},{7,6},{8,9},{9,8},{10,11... | collective-permute-start | bytes 1572872 | tf_op jit(solution)/shard_map/ppermute | solution.py:184

commit v6 on v5

--- a/solution.py
+++ b/solution.py
@@ -108,10 +108,10 @@
         return ((z * side + y) * side + x) * n_in + c
 
     ranks, dps, cores = range(side), range(n_dp), range(n_in)
-    plane = [[device(z, a, b, c) for a in ranks for b in ranks] for z in dps for c in cores]
+    first = [[device(z, a, b, c) for b in ranks] for z in dps for a in ranks for c in cores]
     wide = [[device(z, a, b, c) for z in dps for b in ranks] for a in ranks for c in cores]
     second = [[device(z, a, b, c) for a in ranks] for z in dps for b in ranks for c in cores]
-    return plane, wide, second
+    return first, wide, second
 
 
 def local(
@@ -125,7 +125,7 @@
     lat = lax.axis_index("lat")
     core = lax.axis_index("inner")
     swap = [(i, (i + 1) % n_in) for i in range(n_in)]
-    plane, wide, second = plane_groups(n_dp, side, n_in)
+    first, wide, second = plane_groups(n_dp, side, n_in)
 
     def send(v, step):
         return lax.ppermute(v, "dp", [(i, i ^ step) for i in range(n_dp)])
@@ -146,8 +146,9 @@
     place = jnp.stack([core, lat])
     sel = make_sel(place, top_idx, top_val, aux_idx, aux_val, cores, slots)
 
-    full = jnp.concatenate([err_main, err_aux], axis=0)
-    full = exchange(jnp.broadcast_to(full[None], (n_lat,) + full.shape), plane)
+    near = spread(jnp.concatenate([err_main, err_aux], axis=0), first)
+    near, sel = lax.optimization_barrier((near, sel))
+    full = spread(near, second)
     sel_all = grow(sel[None], 4)
 
     both = full.reshape(n_lat, 2, d).transpose(1, 0, 2).reshape(2 * n_lat, d)

time: 126 us -> 126 us (level)
    ppermute x1, starting transfers between devices: 1.91 us -> 16.1 us  [local(): small_other = lax.ppermute(small, 'inner', swap)]
    all_to_all x3 -> x4, starting transfers between devices: 32.2 us -> 23.6 us  [exchange(): lax.all_to_all(v, ('dp', 'lat', 'inner'), 0, 0, axis_index_groups=groups,...]
    ppermute x1, starting transfers between devices: 6.68 us -> 3.08 us  [local(): dec_other = lax.ppermute(dec_rows, 'inner', swap)]
    ppermute x7, starting transfers between devices: 36.7 us -> 34.7 us  [send(): return lax.ppermute(v, 'dp', [(i, i ^ step) for i in range(n_dp)])]
    broadcast_in_dim x1 -> x0, local copies, waits for them, and re-layouts: 1.99 us -> none  [local(): full = exchange(jnp.broadcast_to(full[None], (n_lat,) + full.shape), plane)]
    broadcast_in_dim x2 -> x4, local copies, waits for them, and re-layouts: 1.36 us -> 3.17 us  [spread(): return exchange(jnp.broadcast_to(v[None], (side,) + v.shape), groups)]
    all_to_all x3 -> x4, waiting for transfers between devices: 0.6 us -> 2.36 us  [exchange(): lax.all_to_all(v, ('dp', 'lat', 'inner'), 0, 0, axis_index_groups=groups,...]
  transfers between devices with their start and end apart: 13 -> 14, of which waited for: 8 -> 8; matrix products, arithmetic and copies ran while one was open for 8% -> 8% of each run, Pallas kernels for 4% -> 4%
where the time goes in v6:
time: 126 us; the launch traced here: 125 us
  starting transfers between devices  83.6 us (66%)
  waiting for transfers between devices  19 us (15%)
  other arithmetic  5.98 us (5%)
  Pallas kernels  5.29 us (4%)
  matrix products  5.19 us (4%)
  local copies, waits for them, and re-layouts  5.11 us (4%)
    ppermute x7, starting transfers between devices, send(): return lax.ppermute(v, 'dp', [(i, i ^ step) for i in range(n_dp)])  34.7 us
    all_to_all x4, starting transfers between devices, exchange(): lax.all_to_all(v, ('dp', 'lat', 'inner'), 0, 0, axis_index_groups=groups,...  23.6 us
    ppermute x1, starting transfers between devices, local(): small_other = lax.ppermute(small, 'inner', swap)  16.1 us
    ppermute x7, waiting for transfers between devices, send(): return lax.ppermute(v, 'dp', [(i, i ^ step) for i in range(n_dp)])  15.8 us
    ppermute x1, starting transfers between devices, local(): got = lax.ppermute(sent, 'inner', swap)  6.22 us
    pallas_call x1, Pallas kernels, make_sel(): pl.pallas_call(sel_kernel, in_specs=[pl.BlockSpec(memory_space=pltpu.SMEM...  5.29 us
    dot_general x2, matrix products, rows_dot(): lax.dot_general(left, right, (((1,), (1,)), ((), ())), preferred_element_...  3.26 us
    broadcast_in_dim x4, local copies, waits for them, and re-layouts, spread(): return exchange(jnp.broadcast_to(v[None], (side,) + v.shape), groups)  3.17 us
  transfers between devices with their start and end apart: 14, of which 8 were waited for; matrix products, arithmetic and copies ran while one was open for 8% of the time, Pallas kernels for 4%

profile of v6, /device:TPU:1, one launch (start us, length us, event | category | flops | bytes accessed | tf_op | source)
XLA Modules:
  0.0 125.3 jit_solution(4218221385591554841)
XLA Ops:
  0.6 0.8 pad_add_fusion.1
  1.4 16.1 %collective-permute-start = (s32[384]{0:T(512)S(1)}, s32[384]{0:T(512)S(1)}, u32[]{:S(2)}, u32[]{:S(2)}) collective-permute-start(s32[384]{0:T(512)S(1)} %pad_add_fusion.1), channel_id=1, source_target_pairs={{0,1},{1,0},{2,3},{3,2},{4,5},{5,4},{6,7},{7,6},{8,9},{9,8},{10,11... | collective-permute-start | bytes 4616 | tf_op jit(solution)/shard_map/ppermute | solution.py:144
  17.5 0.8 pad_maximum_fusion.6
  18.3 0.7 broadcast_in_dim.39
  19.0 3.4 %all-to-all-start = ((bf16[8,2,4096]{2,1,0:T(2,128)(2,1)}), bf16[8,2,4096]{2,1,0:T(2,128)(2,1)S(1)}, u32[]{:S(2)}, u32[]{:S(2)}) async-start(bf16[8,2,4096]{2,1,0:T(2,128)(2,1)} %broadcast_in_dim.39), calls=%async_computation | async-start | bytes 262144 | tf_op jit(solution)/shard_map/all_to_all | solution.py:137
  22.4 0.6 pad_add_fusion.2.place
  23.0 0.0 collective-permute-done
  23.0 0.6 pad_add_fusion.cores
  23.6 5.3 %sel.1 = bf16[64,1024]{1,0:T(8,128)(2,1)} custom-call(s32[2]{0:T(128)} %pad_add_fusion.2.place, s32[64,128]{1,0:T(8,128)} %bitcast.86, bf16[64,128]{1,0:T(8,128)(2,1)} %bitcast.87, s32[128,512]{1,0:T(8,128)} %aux_idx.1, bf16[128,512]{1,0:T(8,128)(2,1)} %aux_val.1, s32[2,384]{1,0:T(2,128)} %pad_add_fusion.cores), custom_call_target="tpu_custom_call" | custom-call | flops 1342177280 | bytes 1048576 | tf_op jit(solution)/shard_map/sel/pallas_call | solution.py:75
  28.9 1.3 %all-to-all-done = bf16[8,2,4096]{2,1,0:T(2,128)(2,1)S(1)} async-done(((bf16[8,2,4096]{2,1,0:T(2,128)(2,1)}), bf16[8,2,4096]{2,1,0:T(2,128)(2,1)S(1)}, u32[]{:S(2)}, u32[]{:S(2)}) %all-to-all-start) | async-done | bytes 131104 | tf_op jit(solution)/shard_map/all_to_all | solution.py:137
  30.2 0.1 copy.23
  30.3 0.0 copy-start
  30.3 0.0 copy-start.1
  30.3 0.0 copy-start.2
  30.3 0.0 copy-start.3
  30.3 0.0 copy-start.4
  30.3 1.1 broadcast_in_dim.43
  31.4 3.6 %all-to-all-start.2 = ((bf16[8,8,2,4096]{3,1,2,0:T(8,128)(2,1)}), bf16[8,8,2,4096]{3,1,2,0:T(8,128)(2,1)S(1)}, u32[]{:S(2)}, u32[]{:S(2)}) async-start(bf16[8,8,2,4096]{3,1,2,0:T(8,128)(2,1)} %broadcast_in_dim.43), calls=%async_computation.2 | async-start | bytes 2097152 | tf_op jit(solution)/shard_map/all_to_all | solution.py:137
  35.0 0.0 copy-done
  35.0 3.1 %collective-permute-start.3 = (bf16[256,4096]{1,0:T(8,128)(2,1)S(1)}, bf16[256,4096]{1,0:T(8,128)(2,1)}, u32[]{:S(2)}, u32[]{:S(2)}) collective-permute-start(bf16[256,4096]{1,0:T(8,128)(2,1)S(1)} %copy-done), channel_id=1, source_target_pairs={{0,1},{1,0},{2,3},{3,2},{4,5},{5,4},{6,7},{7,6},{8,9},{9,8},{10,11... | collective-permute-start | bytes 6291464 | tf_op jit(solution)/shard_map/ppermute | solution.py:142
  38.1 9.1 %collective-permute-start.1 = (bf16[1,64,1024]{2,1,0:T(8,128)(2,1)S(1)}, bf16[1,64,1024]{2,1,0:T(8,128)(2,1)S(1)}, u32[]{:S(2)}, u32[]{:S(2)}) collective-permute-start(bf16[1,64,1024]{2,1,0:T(8,128)(2,1)S(1)} %bitcast.82), channel_id=1, source_target_pairs={{0,512},{128,640},{256,768},{384,896},{512,0},{640,128},{768,256},... | collective-permute-start | bytes 393224 | tf_op jit(solution)/shard_map/ppermute | solution.py:131
  47.2 0.1 pad_maximum_fusion.5
  47.3 3.7 %collective-permute-done.1 = bf16[1,64,1024]{2,1,0:T(8,128)(2,1)S(1)} collective-permute-done((bf16[1,64,1024]{2,1,0:T(8,128)(2,1)S(1)}, bf16[1,64,1024]{2,1,0:T(8,128)(2,1)S(1)}, u32[]{:S(2)}, u32[]{:S(2)}) %collective-permute-start.1) | collective-permute-done | bytes 131104 | tf_op jit(solution)/shard_map/ppermute | solution.py:131
  51.0 0.7 pad_maximum_fusion.2
  51.7 7.0 %collective-permute-start.2 = (bf16[2,64,1024]{2,1,0:T(8,128)(2,1)}, bf16[2,64,1024]{2,1,0:T(8,128)(2,1)}, u32[]{:S(2)}, u32[]{:S(2)}) collective-permute-start(bf16[2,64,1024]{2,1,0:T(8,128)(2,1)} %pad_maximum_fusion.2), channel_id=1, source_target_pairs={{0,256},{128,384},{256,0},{384,128},{512,768},{640,896},{768,512},... | collective-permute-start | bytes 786440 | tf_op jit(solution)/shard_map/ppermute | solution.py:131
  58.8 0.0 all-to-all-done.2
  58.8 0.8 broadcast_in_dim.42
  59.5 12.8 %all-to-all-start.1 = ((bf16[64,4,512]{2,1,0:T(4,128)(2,1)}), bf16[64,4,512]{2,1,0:T(4,128)(2,1)S(1)}, u32[]{:S(2)}, u32[]{:S(2)}) async-start(bf16[64,4,512]{2,1,0:T(4,128)(2,1)} %bitcast.80), calls=%async_computation.1 | async-start | bytes 524288 | tf_op jit(solution)/shard_map/all_to_all | solution.py:137
  72.3 0.1 copy.24
  72.4 0.8 fusion.21
  73.2 0.0 collective-permute-done.3
  73.2 2.4 %fusion.22 = f32[128,256]{1,0:T(8,128)S(1)} fusion(bf16[128,4096]{1,0:T(8,128)(2,1)S(1)} %bitcast.72, bf16[256,4096]{1,0:T(8,128)(2,1)} %collective-permute-done.3), kind=kOutput, calls=%fused_computation.52 | convolution fusion | flops 268435456 | bytes 3276800 | tf_op jit(solution)/shard_map/dot_general | solution.py:94
  75.7 6.9 %collective-permute-start.4 = (bf16[1,64,512]{2,1,0:T(8,128)(2,1)S(1)}, bf16[1,64,512]{2,1,0:T(8,128)(2,1)S(1)}, u32[]{:S(2)}, u32[]{:S(2)}) collective-permute-start(bf16[1,64,512]{2,1,0:T(8,128)(2,1)S(1)} %fusion.20), channel_id=1, source_target_pairs={{0,512},{128,640},{256,768},{384,896},{512,0},{640,128},{768,256},... | collective-permute-start | bytes 196616 | tf_op jit(solution)/shard_map/ppermute | solution.py:131
  82.7 0.0 collective-permute-done.2
  82.7 1.1 pad_maximum_fusion
  83.7 1.0 all-to-all-done.1
  84.8 1.2 collective-permute-done.4
  86.0 0.1 reverse_select_fusion.1
  86.2 0.1 copy.27
  86.3 1.3 %broadcast_in_dim.47 = bf16[8,8,24,512]{3,2,1,0:T(8,128)(2,1)} broadcast(bf16[8,24,512]{2,1,0:T(8,128)(2,1)S(1)} %copy.27), dimensions={1,2,3} | broadcast | bytes 1769472 | tf_op jit(solution)/shard_map/broadcast_in_dim | solution.py:140
  87.6 3.9 %all-to-all-start.3 = ((bf16[8,8,24,512]{3,2,1,0:T(8,128)(2,1)}), bf16[8,8,24,512]{3,2,1,0:T(8,128)(2,1)S(1)}, u32[]{:S(2)}, u32[]{:S(2)}) async-start(bf16[8,8,24,512]{3,2,1,0:T(8,128)(2,1)} %broadcast_in_dim.47), calls=%async_computation.3 | async-start | bytes 3145728 | tf_op jit(solution)/shard_map/all_to_all | solution.py:137
  91.5 2.4 %collective-permute-start.5 = (bf16[4,64,1024]{2,1,0:T(8,128)(2,1)S(1)}, bf16[4,64,1024]{2,1,0:T(8,128)(2,1)S(1)}, u32[]{:S(2)}, u32[]{:S(2)}) collective-permute-start(bf16[4,64,1024]{2,1,0:T(8,128)(2,1)S(1)} %pad_maximum_fusion), channel_id=1, source_target_pairs={{0,128},{128,0},{256,384},{384,256},{512,640},{640,512},{768,896},... | collective-permute-start | bytes 1572872 | tf_op jit(solution)/shard_map/ppermute | solution.py:131
  93.8 4.1 %collective-permute-start.6 = (bf16[2,64,512]{2,1,0:T(8,128)(2,1)S(1)}, bf16[2,64,512]{2,1,0:T(8,128)(2,1)S(1)}, u32[]{:S(2)}, u32[]{:S(2)}) collective-permute-start(bf16[2,64,512]{2,1,0:T(8,128)(2,1)S(1)} %pad_maximum_fusion.4), channel_id=1, source_target_pairs={{0,256},{128,384},{256,0},{384,128},{512,768},{640,896},{768,512},... | collective-permute-start | bytes 393224 | tf_op jit(solution)/shard_map/ppermute | solution.py:131
  97.9 3.4 %collective-permute-start.7 = (bf16[2,64,512]{2,1,0:T(8,128)(2,1)S(1)}, bf16[2,64,512]{2,1,0:T(8,128)(2,1)S(1)}, u32[]{:S(2)}, u32[]{:S(2)}) collective-permute-start(bf16[2,64,512]{2,1,0:T(8,128)(2,1)S(1)} %pad_maximum_fusion.4), channel_id=1, source_target_pairs={{0,128},{128,0},{256,384},{384,256},{512,640},{640,512},{768,896},... | collective-permute-start | bytes 393224 | tf_op jit(solution)/shard_map/ppermute | solution.py:131
  101.3 1.9 %collective-permute-start.8 = (bf16[2,64,512]{2,1,0:T(8,128)(2,1)S(1)}, bf16[2,64,512]{2,1,0:T(8,128)(2,1)S(1)}, u32[]{:S(2)}, u32[]{:S(2)}) collective-permute-start(bf16[2,64,512]{2,1,0:T(8,128)(2,1)S(1)} %pad_maximum_fusion.4), channel_id=1, source_target_pairs={{0,384},{128,256},{256,128},{384,0},{512,896},{640,768},{768,640},... | collective-permute-start | bytes 393224 | tf_op jit(solution)/shard_map/ppermute | solution.py:131
  103.2 1.5 %collective-permute-done.6 = bf16[2,64,512]{2,1,0:T(8,128)(2,1)S(1)} collective-permute-done((bf16[2,64,512]{2,1,0:T(8,128)(2,1)S(1)}, bf16[2,64,512]{2,1,0:T(8,128)(2,1)S(1)}, u32[]{:S(2)}, u32[]{:S(2)}) %collective-permute-start.6) | collective-permute-done | bytes 131104 | tf_op jit(solution)/shard_map/ppermute | solution.py:131
  104.7 5.3 %collective-permute-done.7 = bf16[2,64,512]{2,1,0:T(8,128)(2,1)S(1)} collective-permute-done((bf16[2,64,512]{2,1,0:T(8,128)(2,1)S(1)}, bf16[2,64,512]{2,1,0:T(8,128)(2,1)S(1)}, u32[]{:S(2)}, u32[]{:S(2)}) %collective-permute-start.7) | collective-permute-done | bytes 131104 | tf_op jit(solution)/shard_map/ppermute | solution.py:131
  110.0 4.2 %collective-permute-done.8 = bf16[2,64,512]{2,1,0:T(8,128)(2,1)S(1)} collective-permute-done((bf16[2,64,512]{2,1,0:T(8,128)(2,1)S(1)}, bf16[2,64,512]{2,1,0:T(8,128)(2,1)S(1)}, u32[]{:S(2)}, u32[]{:S(2)}) %collective-permute-start.8) | collective-permute-done | bytes 131104 | tf_op jit(solution)/shard_map/ppermute | solution.py:131
  114.1 0.1 maximum_bitcast_fusion.1
  114.2 0.3 copy.34
  114.5 0.0 collective-permute-done.5
  114.5 0.1 maximum_bitcast_fusion
  114.6 0.6 copy.33
  115.2 0.0 all-to-all-done.3
  115.2 0.3 fusion.1
  115.5 0.3 fusion.7
  115.9 0.3 fusion.5
  116.2 0.3 fusion.2
  116.5 0.1 pad_maximum_fusion.1
  116.6 6.2 %collective-permute-start.9 = (bf16[2,256,512]{2,1,0:T(8,128)(2,1)S(1)}, bf16[2,256,512]{2,1,0:T(8,128)(2,1)S(1)}, u32[]{:S(2)}, u32[]{:S(2)}) collective-permute-start(bf16[2,256,512]{2,1,0:T(8,128)(2,1)S(1)} %pad_maximum_fusion.1), channel_id=1, source_target_pairs={{0,1},{1,0},{2,3},{3,2},{4,5},{5,4},{6,7},{7,6},{8,9},{9,8},{10,11... | collective-permute-start | bytes 1572872 | tf_op jit(solution)/shard_map/ppermute | solution.py:185
  122.8 0.3 fusion.6
  123.1 0.3 convolution_add_fusion.1
  123.5 0.9 collective-permute-done.9
  124.3 0.9 fusion.3
  (16 shorter events, 0.3 us)
Async XLA Ops:
  1.4 21.6 %collective-permute-start = (s32[384]{0:T(512)S(1)}, s32[384]{0:T(512)S(1)}, u32[]{:S(2)}, u32[]{:S(2)}) collective-permute-start(s32[384]{0:T(512)S(1)} %pad_add_fusion.1), channel_id=1, source_target_pairs={{0,1},{1,0},{2,3},{3,2},{4,5},{5,4},{6,7},{7,6},{8,9},{9,8},{10,11... | collective-permute-start | bytes 4616 | tf_op jit(solution)/shard_map/ppermute | solution.py:144
  19.0 11.2 %all-to-all-start = ((bf16[8,2,4096]{2,1,0:T(2,128)(2,1)}), bf16[8,2,4096]{2,1,0:T(2,128)(2,1)S(1)}, u32[]{:S(2)}, u32[]{:S(2)}) async-start(bf16[8,2,4096]{2,1,0:T(2,128)(2,1)} %broadcast_in_dim.39), calls=%async_computation | async-start | bytes 262144 | tf_op jit(solution)/shard_map/all_to_all | solution.py:137
  30.3 4.7 %copy-start = (bf16[256,4096]{1,0:T(8,128)(2,1)S(1)}, bf16[256,4096]{1,0:T(8,128)(2,1)}, u32[]{:S(2)}) copy-start(bf16[256,4096]{1,0:T(8,128)(2,1)} %param.19) | copy-start | bytes 6291460
  30.3 7.8 %copy-start.1 = (bf16[64,1024]{1,0:T(8,128)(2,1)S(1)}, bf16[64,1024]{1,0:T(8,128)(2,1)}, u32[]{:S(2)}) copy-start(bf16[64,1024]{1,0:T(8,128)(2,1)} %sel.1) | copy-start | bytes 393220
  30.3 16.9 %copy-start.2 = (bf16[1,4096]{1,0:T(2,128)(2,1)S(1)}, bf16[1,4096]{1,0:T(2,128)(2,1)}, u32[]{:S(2)}) copy-start(bf16[1,4096]{1,0:T(2,128)(2,1)} %param.11) | copy-start | bytes 24580
  30.3 16.9 %copy-start.3 = (bf16[1,4096]{1,0:T(2,128)(2,1)S(1)}, bf16[1,4096]{1,0:T(2,128)(2,1)}, u32[]{:S(2)}) copy-start(bf16[1,4096]{1,0:T(2,128)(2,1)} %param.10) | copy-start | bytes 24580
  30.3 16.9 %copy-start.4 = (bf16[1,4096]{1,0:T(2,128)(2,1)S(1)}, bf16[1,4096]{1,0:T(2,128)(2,1)}, u32[]{:S(2)}) copy-start(bf16[1,4096]{1,0:T(2,128)(2,1)} %param.12) | copy-start | bytes 24580
  31.4 27.3 %all-to-all-start.2 = ((bf16[8,8,2,4096]{3,1,2,0:T(8,128)(2,1)}), bf16[8,8,2,4096]{3,1,2,0:T(8,128)(2,1)S(1)}, u32[]{:S(2)}, u32[]{:S(2)}) async-start(bf16[8,8,2,4096]{3,1,2,0:T(8,128)(2,1)} %broadcast_in_dim.43), calls=%async_computation.2 | async-start | bytes 2097152 | tf_op jit(solution)/shard_map/all_to_all | solution.py:137
  35.0 38.2 %collective-permute-start.3 = (bf16[256,4096]{1,0:T(8,128)(2,1)S(1)}, bf16[256,4096]{1,0:T(8,128)(2,1)}, u32[]{:S(2)}, u32[]{:S(2)}) collective-permute-start(bf16[256,4096]{1,0:T(8,128)(2,1)S(1)} %copy-done), channel_id=1, source_target_pairs={{0,1},{1,0},{2,3},{3,2},{4,5},{5,4},{6,7},{7,6},{8,9},{9,8},{10,11... | collective-permute-start | bytes 6291464 | tf_op jit(solution)/shard_map/ppermute | solution.py:142
  38.1 12.9 %collective-permute-start.1 = (bf16[1,64,1024]{2,1,0:T(8,128)(2,1)S(1)}, bf16[1,64,1024]{2,1,0:T(8,128)(2,1)S(1)}, u32[]{:S(2)}, u32[]{:S(2)}) collective-permute-start(bf16[1,64,1024]{2,1,0:T(8,128)(2,1)S(1)} %bitcast.82), channel_id=1, source_target_pairs={{0,512},{128,640},{256,768},{384,896},{512,0},{640,128},{768,256},... | collective-permute-start | bytes 393224 | tf_op jit(solution)/shard_map/ppermute | solution.py:131
  51.7 30.9 %collective-permute-start.2 = (bf16[2,64,1024]{2,1,0:T(8,128)(2,1)}, bf16[2,64,1024]{2,1,0:T(8,128)(2,1)}, u32[]{:S(2)}, u32[]{:S(2)}) collective-permute-start(bf16[2,64,1024]{2,1,0:T(8,128)(2,1)} %pad_maximum_fusion.2), channel_id=1, source_target_pairs={{0,256},{128,384},{256,0},{384,128},{512,768},{640,896},{768,512},... | collective-permute-start | bytes 786440 | tf_op jit(solution)/shard_map/ppermute | solution.py:131
  59.5 25.2 %all-to-all-start.1 = ((bf16[64,4,512]{2,1,0:T(4,128)(2,1)}), bf16[64,4,512]{2,1,0:T(4,128)(2,1)S(1)}, u32[]{:S(2)}, u32[]{:S(2)}) async-start(bf16[64,4,512]{2,1,0:T(4,128)(2,1)} %bitcast.80), calls=%async_computation.1 | async-start | bytes 524288 | tf_op jit(solution)/shard_map/all_to_all | solution.py:137
  75.7 10.3 %collective-permute-start.4 = (bf16[1,64,512]{2,1,0:T(8,128)(2,1)S(1)}, bf16[1,64,512]{2,1,0:T(8,128)(2,1)S(1)}, u32[]{:S(2)}, u32[]{:S(2)}) collective-permute-start(bf16[1,64,512]{2,1,0:T(8,128)(2,1)S(1)} %fusion.20), channel_id=1, source_target_pairs={{0,512},{128,640},{256,768},{384,896},{512,0},{640,128},{768,256},... | collective-permute-start | bytes 196616 | tf_op jit(solution)/shard_map/ppermute | solution.py:131
  87.6 27.6 %all-to-all-start.3 = ((bf16[8,8,24,512]{3,2,1,0:T(8,128)(2,1)}), bf16[8,8,24,512]{3,2,1,0:T(8,128)(2,1)S(1)}, u32[]{:S(2)}, u32[]{:S(2)}) async-start(bf16[8,8,24,512]{3,2,1,0:T(8,128)(2,1)} %broadcast_in_dim.47), calls=%async_computation.3 | async-start | bytes 3145728 | tf_op jit(solution)/shard_map/all_to_all | solution.py:137
  91.5 23.0 %collective-permute-start.5 = (bf16[4,64,1024]{2,1,0:T(8,128)(2,1)S(1)}, bf16[4,64,1024]{2,1,0:T(8,128)(2,1)S(1)}, u32[]{:S(2)}, u32[]{:S(2)}) collective-permute-start(bf16[4,64,1024]{2,1,0:T(8,128)(2,1)S(1)} %pad_maximum_fusion), channel_id=1, source_target_pairs={{0,128},{128,0},{256,384},{384,256},{512,640},{640,512},{768,896},... | collective-permute-start | bytes 1572872 | tf_op jit(solution)/shard_map/ppermute | solution.py:131
  93.8 10.8 %collective-permute-start.6 = (bf16[2,64,512]{2,1,0:T(8,128)(2,1)S(1)}, bf16[2,64,512]{2,1,0:T(8,128)(2,1)S(1)}, u32[]{:S(2)}, u32[]{:S(2)}) collective-permute-start(bf16[2,64,512]{2,1,0:T(8,128)(2,1)S(1)} %pad_maximum_fusion.4), channel_id=1, source_target_pairs={{0,256},{128,384},{256,0},{384,128},{512,768},{640,896},{768,512},... | collective-permute-start | bytes 393224 | tf_op jit(solution)/shard_map/ppermute | solution.py:131
  97.9 12.0 %collective-permute-start.7 = (bf16[2,64,512]{2,1,0:T(8,128)(2,1)S(1)}, bf16[2,64,512]{2,1,0:T(8,128)(2,1)S(1)}, u32[]{:S(2)}, u32[]{:S(2)}) collective-permute-start(bf16[2,64,512]{2,1,0:T(8,128)(2,1)S(1)} %pad_maximum_fusion.4), channel_id=1, source_target_pairs={{0,128},{128,0},{256,384},{384,256},{512,640},{640,512},{768,896},... | collective-permute-start | bytes 393224 | tf_op jit(solution)/shard_map/ppermute | solution.py:131
  101.3 12.9 %collective-permute-start.8 = (bf16[2,64,512]{2,1,0:T(8,128)(2,1)S(1)}, bf16[2,64,512]{2,1,0:T(8,128)(2,1)S(1)}, u32[]{:S(2)}, u32[]{:S(2)}) collective-permute-start(bf16[2,64,512]{2,1,0:T(8,128)(2,1)S(1)} %pad_maximum_fusion.4), channel_id=1, source_target_pairs={{0,384},{128,256},{256,128},{384,0},{512,896},{640,768},{768,640},... | collective-permute-start | bytes 393224 | tf_op jit(solution)/shard_map/ppermute | solution.py:131
  116.6 7.7 %collective-permute-start.9 = (bf16[2,256,512]{2,1,0:T(8,128)(2,1)S(1)}, bf16[2,256,512]{2,1,0:T(8,128)(2,1)S(1)}, u32[]{:S(2)}, u32[]{:S(2)}) collective-permute-start(bf16[2,256,512]{2,1,0:T(8,128)(2,1)S(1)} %pad_maximum_fusion.1), channel_id=1, source_target_pairs={{0,1},{1,0},{2,3},{3,2},{4,5},{5,4},{6,7},{7,6},{8,9},{9,8},{10,11... | collective-permute-start | bytes 1572872 | tf_op jit(solution)/shard_map/ppermute | solution.py:185
